TPU v7x, 32 devices: a whole 2x2x4 slice. The times are simulated.
32 devices in a mesh: kv: 4 (over y, x), blk: 8 (over z, core).
Axes of the slice: x: 2, y: 2, z: 4, core: 2. Of those that a mesh axis runs over, the one named last changes fastest.
Arguments:
- prefix_pool: bfloat16 [4, 192, 64, 512], P('kv', 'blk'), may hold values from -6 to 6
- slot_page: int32 [192], P('blk'), may hold values from 0 to 191, as said below
- prompt_len: int32 [3], replicated, may hold values from 1 to 6048, 12096 in all
- request_ids: int32 [48], replicated, may hold values from 0 to 47, each once
- tail_len: int32 [48], P('blk'), may hold values from 1 to 128, 3072 in all
- tail_cache: bfloat16 [4, 48, 128, 512], P('kv', 'blk'), may hold values from -6 to 6
- queries: bfloat16 [48, 2, 2048], P('blk', None, 'kv'), may hold values from -120 to 120
- new_kv: bfloat16 [4, 48, 2, 512], P('kv', 'blk'), may hold values from -5.1 to 5.1
- hidden: bfloat16 [48, 2, 2048], P('blk'), may hold values from -4 to 4
- out_weight: bfloat16 [2048, 2048], P('kv'), may hold values from -0.125 to 0.125
- norm_gain: float32 [2048], replicated, may hold values from 0.1 to 1.9
- score_weight: float32 [2048], replicated, may hold values from -0.125 to 0.125
Outputs:
- hidden_out: bfloat16 [48, 2, 2048], P('blk')
- scores_out: float32 [48], P('blk')
Inputs may be any that keep to these rules, and one draw needn't show every extreme that they name: `slot_page`: the pages of all prompts fit the pool; every logical page number appears once. Request slot r serves sample request_ids[r] % 16 of prompt request_ids[r] // 16; every pair once.
All inputs are finite; a program needn't handle non-finite values. No bound on the sum of `tail_len` on one device may be relied on, other than what follows from the above.
Results may differ from a plain program's by a relative error of at most 0.02.
Values may be sent and summed in bfloat16 or wider, within the bound.
No kernel may reach another device: no remote copies, remote signals or barrier semaphores. Data moves between devices by JAX's collectives and lax.ppermute only.
A program may use at most 64 MiB of HBM per device.

v0:
```python
import jax
import jax.numpy as jnp
from jax import lax
from jax.sharding import PartitionSpec as P

SAMPLES = 16


NEG_FLOOR = -1e30


def page_layout(slot_page, prompt_len, page_tokens):
    needed = (prompt_len + page_tokens - 1) // page_tokens
    page_ends = jnp.cumsum(needed)
    page_starts = page_ends - needed
    page_owner = jnp.sum((slot_page[:, None] >= page_ends[None, :]).astype(jnp.int32), axis=1)
    in_use = page_owner < prompt_len.shape[0]
    page_owner = jnp.minimum(page_owner, prompt_len.shape[0] - 1)
    offset = slot_page - page_starts[page_owner]
    position = offset[:, None] * page_tokens + jnp.arange(page_tokens, dtype=jnp.int32)[None, :]
    live_keys = in_use[:, None] & (position < prompt_len[page_owner][:, None])
    return (page_owner, live_keys)


def home_slots(request_ids):
    total_count = request_ids.shape[0]
    return (
        jnp.zeros((total_count,), jnp.int32)
        .at[request_ids]
        .set(jnp.arange(total_count, dtype=jnp.int32))
    )


def own_attention(
    own_queries, tail_block, fresh_block, tail_len, prefix_peak, prefix_num, prefix_den
):
    req_count, drafts, head_width = own_queries.shape
    head_size = tail_block.shape[2] // 2
    group_size = head_width // head_size
    row_count = drafts * group_size
    score_scale = head_size ** (-0.5)
    flat_queries = own_queries.reshape(req_count, row_count, head_size)
    tail_logits = (
        jnp.einsum(
            "rqh,rkh->rqk",
            flat_queries,
            tail_block[:, :, :head_size],
            preferred_element_type=jnp.float32,
        )
        * score_scale
    )
    tail_live = (jnp.arange(tail_block.shape[1], dtype=jnp.int32)[None, :] < tail_len[:, None])[
        :, None, :
    ]
    tail_logits = jnp.where(tail_live, tail_logits, NEG_FLOOR)
    fresh_logits = (
        jnp.einsum(
            "rqh,rkh->rqk",
            flat_queries,
            fresh_block[:, :, :head_size],
            preferred_element_type=jnp.float32,
        )
        * score_scale
    )
    fresh_live = (
        jnp.arange(drafts, dtype=jnp.int32)[None, :]
        <= (jnp.arange(row_count, dtype=jnp.int32) // group_size)[:, None]
    )[None]
    fresh_logits = jnp.where(fresh_live, fresh_logits, NEG_FLOOR)
    own_peak = jnp.maximum(jnp.max(tail_logits, axis=2), jnp.max(fresh_logits, axis=2))
    top_peak = jnp.maximum(prefix_peak, own_peak)
    tail_weights = jnp.where(tail_live, jnp.exp(tail_logits - top_peak[:, :, None]), 0.0)
    fresh_weights = jnp.where(fresh_live, jnp.exp(fresh_logits - top_peak[:, :, None]), 0.0)
    carried = jnp.exp(prefix_peak - top_peak)
    numer = prefix_num * carried[:, :, None]
    numer = numer + jnp.einsum(
        "rqk,rkh->rqh",
        tail_weights.astype(jnp.bfloat16),
        tail_block[:, :, head_size:],
        preferred_element_type=jnp.float32,
    )
    numer = numer + jnp.einsum(
        "rqk,rkh->rqh",
        fresh_weights.astype(jnp.bfloat16),
        fresh_block[:, :, head_size:],
        preferred_element_type=jnp.float32,
    )
    denom = prefix_den * carried + jnp.sum(tail_weights, axis=2) + jnp.sum(fresh_weights, axis=2)
    return (numer / denom[:, :, None]).astype(jnp.bfloat16).reshape(req_count, drafts, head_width)


def page_sums(
    logits, live_keys, slot_rows, peak_table, page_pool, total_count, row_count, head_size
):
    page_count = page_pool.shape[0]
    flat_rows = slot_rows.reshape(-1)
    ref_peak = peak_table[slot_rows].reshape(page_count, -1)
    weights = jnp.where(live_keys[:, None, :], jnp.exp(logits - ref_peak[:, :, None]), 0.0)
    slot_den = jnp.sum(weights, axis=2).reshape(-1, row_count)
    slot_num = jnp.einsum(
        "prk,pkh->prh",
        weights.astype(jnp.bfloat16),
        page_pool[:, :, head_size:],
        preferred_element_type=jnp.float32,
    ).reshape(-1, row_count, head_size)
    prefix_num = (
        jnp.zeros((total_count, row_count, head_size), jnp.float32).at[flat_rows].add(slot_num)
    )
    prefix_den = jnp.zeros((total_count, row_count), jnp.float32).at[flat_rows].add(slot_den)
    return (prefix_num, prefix_den)


def body(
    prefix_pool,
    slot_page,
    prompt_len,
    request_ids,
    tail_len,
    tail_cache,
    queries,
    new_kv,
    hidden,
    out_weight,
    norm_gain,
    score_weight,
):
    page_pool = prefix_pool[0]
    page_count = page_pool.shape[0]
    page_tokens = page_pool.shape[1]
    head_size = page_pool.shape[2] // 2
    local_count, drafts, head_width = queries.shape
    group_size = head_width // head_size
    row_count = drafts * group_size
    total_count = request_ids.shape[0]
    score_scale = head_size ** (-0.5)
    page_owner, live_keys = page_layout(slot_page, prompt_len, page_tokens)
    home_rows = home_slots(request_ids)
    slot_rows = home_rows[
        page_owner[:, None] * SAMPLES + jnp.arange(SAMPLES, dtype=jnp.int32)[None, :]
    ]
    all_queries = lax.all_gather(queries, "blk", axis=0, tiled=True)
    picked = all_queries[slot_rows].reshape(page_count, -1, head_size)
    logits = (
        jnp.einsum(
            "prh,pkh->prk", picked, page_pool[:, :, :head_size], preferred_element_type=jnp.float32
        )
        * score_scale
    )
    logits = jnp.where(live_keys[:, None, :], logits, NEG_FLOOR)
    flat_rows = slot_rows.reshape(-1)
    slot_peak = jnp.max(logits, axis=2).reshape(-1, row_count)
    local_peak = (
        jnp.full((total_count, row_count), NEG_FLOOR, jnp.float32).at[flat_rows].max(slot_peak)
    )
    row_start = lax.axis_index("blk") * local_count
    global_peak = lax.pmax(local_peak, "blk")
    prefix_num, prefix_den = page_sums(
        logits, live_keys, slot_rows, global_peak, page_pool, total_count, row_count, head_size
    )
    total_num, total_den = lax.psum((prefix_num, prefix_den), "blk")
    own_num = lax.dynamic_slice_in_dim(total_num, row_start, local_count, 0)
    own_den = lax.dynamic_slice_in_dim(total_den, row_start, local_count, 0)
    own_peak = lax.dynamic_slice_in_dim(global_peak, row_start, local_count, 0)
    attention = own_attention(
        queries, tail_cache[0], new_kv[0], tail_len, own_peak, own_num, own_den
    )
    partial_value = jnp.dot(
        attention.reshape(-1, head_width), out_weight, preferred_element_type=jnp.float32
    )
    summed = lax.psum(partial_value.astype(jnp.bfloat16), "kv").astype(jnp.float32)
    hidden_out = (hidden.astype(jnp.float32) + summed.reshape(hidden.shape)).astype(jnp.bfloat16)
    last_hidden = hidden_out[:, -1, :].astype(jnp.float32)
    normed = (
        last_hidden
        * lax.rsqrt(jnp.mean(last_hidden * last_hidden, axis=-1, keepdims=True) + 1e-06)
        * norm_gain
    )
    scores_out = jnp.sum(normed * score_weight, axis=-1)
    return (hidden_out, scores_out)


def solution(mesh):
    in_specs = (
        P("kv", "blk", None, None),
        P("blk"),
        P(),
        P(),
        P("blk"),
        P("kv", "blk", None, None),
        P("blk", None, "kv"),
        P("kv", "blk", None, None),
        P("blk", None, None),
        P("kv", None),
        P(),
        P(),
    )
    out_specs = (P("blk", None, None), P("blk"))
    return jax.shard_map(body, mesh=mesh, in_specs=in_specs, out_specs=out_specs, check_vma=False)
```

profile of v0, /device:TPU:0, one launch (start us, length us, event | category | flops | bytes accessed | tf_op | source)
XLA Modules:
  0.0 191.1 jit_solution(2587523549059877191)
XLA Ops:
  7.2 0.0 copy-start
  7.2 0.0 all-reduce.2.cloned.1.call-start
  7.2 0.8 fusion.54
  8.0 1.4 fusion.45
  9.4 0.2 reduce-window.8
  9.6 0.7 bitcast_subtract_fusion
  10.3 0.7 fusion.44
  11.0 0.7 convert_reduce_fusion
  11.7 2.6 %fusion.38 = (s32[24]{0:T(128)S(1)}, s32[24]{0:T(128)S(1)}) fusion(s32[24]{0:T(128)} %param.13, s32[]{:T(128)} %bitcast.3, s32[]{:T(128)} %bitcast.5, s32[]{:T(128)} %bitcast.4, s32[24]{0:T(128)S(1)} %convert_reduce_fusion), kind=kLoop, calls=%fused_computation.83 | loop fusion | flops 264 | bytes 396 | tf_op jit(solution)/shard_map/mul | solution.py:20
  14.3 0.1 compare_select_fusion.1
  14.4 0.1 reshape.278
  14.5 0.7 compare_select_fusion.4
  15.2 0.7 scatter_custom_fusion
  15.9 0.0 copy-start.2
  15.9 2.7 %gather_fusion = s32[384]{0:T(512)S(1)} fusion(s32[48]{0:T(128)S(1)} %scatter_custom_fusion, s32[1024]{0:T(1024)S(1)} %pad_clamp_fusion.1), kind=kCustom, calls=%fused_computation | custom fusion | bytes 4608 | tf_op jit(solution)/shard_map/gather | solution.py:138
  18.6 0.1 gather.20
  18.7 0.1 reshape.306
  18.8 0.0 copy-done.2
  18.8 15.6 %all_gather.3 = bf16[48,2,512]{2,1,0:T(2,128)(2,1)S(1)} all-gather(bf16[6,2,512]{2,1,0:T(2,128)(2,1)S(1)} %copy-done.2), channel_id=1, replica_groups=mesh['kv'=4,'blk'=8] {'blk'}, dimensions={0}, use_global_device_ids=true | all-gather | bytes 110592 | tf_op jit(solution)/shard_map/all_gather | solution.py:141
  34.4 3.5 %gather_fusion.1 = bf16[384,2,512]{2,1,0:T(2,128)(2,1)S(1)} fusion(bf16[48,2,512]{2,1,0:T(2,128)(2,1)S(1)} %all_gather.3, s32[1024]{0:T(1024)S(1)} %pad_clamp_fusion), kind=kCustom, calls=%fused_computation.1 | custom fusion | bytes 1574400 | tf_op jit(solution)/shard_map/gather | solution.py:142
  37.9 1.4 reshape.268
  39.3 1.8 fusion.35
  41.1 0.1 fusion.24
  41.2 1.8 fusion.46
  43.0 0.1 reshape.332
  43.1 1.8 scatter_custom_fusion.1
  45.0 29.1 %pmax.7 = f32[48,4]{1,0:T(8,128)S(1)} all-reduce(f32[48,4]{1,0:T(8,128)S(1)} %scatter_custom_fusion.1), channel_id=1, replica_groups=mesh['kv'=4,'blk'=8] {'blk'}, use_global_device_ids=true, to_apply=%region_5.6 | all-reduce | flops 192 | bytes 1536 | tf_op jit(solution)/shard_map/pmax | solution.py:156
  74.1 1.1 gather_fusion.2
  75.2 0.1 sub.55
  75.3 3.0 %fusion.5 = f32[24,64,256]{2,1,0:T(8,128)} fusion(bf16[24,64,512]{2,1,0:T(8,128)(2,1)} %bitcast.44, f32[24,64,64]{1,2,0:T(8,128)S(1)} %get-tuple-element.19, f32[24,64]{1,0:T(8,128)S(1)} %sub.55, pred[24,64]{1,0:T(8,128)(4,1)S(1)} %fusion.24), kind=kOutput, calls=%fused_computation.18 | convolution fusion | flops 50626560 | bytes 2760192 | tf_op jit(solution)/shard_map/prk,pkh->prh/dot_general | solution.py:100
  78.3 2.7 %reshape.340 = f32[384,4,256]{2,1,0:T(4,128)} reshape(f32[24,64,256]{2,1,0:T(8,128)} %fusion.5) | data formatting | bytes 3145728 | tf_op jit(solution)/shard_map/reshape | solution.py:105
  81.1 0.0 copy-start.7
  81.1 29.1 %scatter_fusion = f32[48,4,256]{2,1,0:T(4,128)S(1)} fusion(f32[48,4,256]{2,1,0:T(4,128)S(1)} %broadcast_in_dim.99, s32[384]{0:T(512)S(1)} %fusion.34, f32[384,4,256]{2,1,0:T(4,128)} %reshape.340), kind=kCustom, calls=%fused_computation.5 | custom fusion | flops 393216 | bytes 4720128 | tf_op jit(solution)/shard_map/scatter-add | solution.py:107
  110.1 0.0 copy-start.1
  110.1 0.0 copy-start.6
  110.2 0.7 copy-done.1
  110.8 0.0 all-reduce.2.cloned.1.call-update
  110.8 0.3 fusion.8
  111.2 0.1 reshape.348
  111.3 1.8 scatter_custom_fusion.3
  113.2 26.0 %psum.22 = f32[48,4]{1,0:T(8,128)S(1)} all-reduce(f32[48,4]{1,0:T(8,128)S(1)} %scatter_custom_fusion.3), channel_id=1, replica_groups=mesh['kv'=4,'blk'=8] {'blk'}, use_global_device_ids=true, to_apply=%region_12.13 | all-reduce | flops 192 | bytes 1536 | tf_op jit(solution)/shard_map/psum | solution.py:160
  139.2 0.0 copy-done.7
  139.2 0.1 iota_compare_fusion
  139.3 1.3 fusion.47
  140.6 0.0 copy-done.6
  140.6 0.2 fusion.48
  140.8 0.2 fusion.25
  141.0 22.9 %all-reduce.2.cloned.1.call-done = f32[48,4,256]{2,1,0:T(4,128)} async-done(((f32[48,4,256]{2,1,0:T(4,128)}), f32[48,4,256]{2,1,0:T(4,128)}) %all-reduce.2.cloned.1.call-update) | async-done | bytes 196624 | tf_op jit(solution)/shard_map/psum | solution.py:160
  163.9 0.0 copy-start.3
  163.9 1.2 convolution_add_fusion.1
  165.1 0.0 copy-start.4
  165.1 0.0 copy-start.5
  165.1 0.2 fusion.2
  165.4 0.0 copy-done
  165.4 0.4 convolution_convert_fusion
  165.8 0.1 reshape.273
  165.8 16.9 %psum.23 = bf16[6,2,2048]{2,0,1:T(8,128)(2,1)S(1)} all-reduce(bf16[6,2,2048]{2,0,1:T(8,128)(2,1)S(1)} %copy.25), channel_id=1, replica_groups=mesh['kv'=4,'blk'=8] {'kv'}, use_global_device_ids=true, to_apply=%region_15.16 | all-reduce | flops 24576 | bytes 98304 | tf_op jit(solution)/shard_map/psum | solution.py:170
  182.7 0.0 copy-done.3
  182.8 0.1 fusion.16
  182.9 0.7 copy.26
  183.6 0.0 copy-done.4
  183.6 0.0 copy-done.5
  183.6 0.7 fusion.19
  (17 shorter events, 0.2 us)
Async XLA Ops:
  7.2 158.2 %copy-start = (bf16[512,2048]{1,0:T(8,128)(2,1)S(1)}, bf16[512,2048]{1,0:T(8,128)(2,1)}, u32[]{:S(2)}) copy-start(bf16[512,2048]{1,0:T(8,128)(2,1)} %param.21) | copy-start | bytes 6291460
  7.2 156.7 %all-reduce.2.cloned.1.call-start = ((), (), s32[]{:S(2)}) async-start(), calls=%async_computation | async-start | bytes 393216 | tf_op jit(solution)/shard_map/psum | solution.py:160
  15.9 2.9 %copy-start.2 = (bf16[6,2,512]{2,1,0:T(2,128)(2,1)S(1)}, bf16[6,2,512]{2,1,0:T(2,128)(2,1)}, u32[]{:S(2)}) copy-start(bf16[6,2,512]{2,1,0:T(2,128)(2,1)} %param.18) | copy-start | bytes 36868
  81.1 58.2 %copy-start.7 = (s32[6]{0:T(128)S(1)}, s32[6]{0:T(128)}, u32[]{:S(2)}) copy-start(s32[6]{0:T(128)} %param.16) | copy-start | bytes 76
  110.1 0.7 copy-start.1
  110.1 30.4 %copy-start.6 = (bf16[1,6,2,512]{3,2,1,0:T(2,128)(2,1)S(1)}, bf16[1,6,2,512]{3,2,1,0:T(2,128)(2,1)}, u32[]{:S(2)}) copy-start(bf16[1,6,2,512]{3,2,1,0:T(2,128)(2,1)} %param.19) | copy-start | bytes 36868
  163.9 18.8 %copy-start.3 = (bf16[6,2,2048]{2,1,0:T(2,128)(2,1)S(1)}, bf16[6,2,2048]{2,1,0:T(2,128)(2,1)}, u32[]{:S(2)}) copy-start(bf16[6,2,2048]{2,1,0:T(2,128)(2,1)} %param.20) | copy-start | bytes 147460
  165.1 18.5 %copy-start.4 = (f32[2048]{0:T(1024)S(1)}, f32[2048]{0:T(1024)}, u32[]{:S(2)}) copy-start(f32[2048]{0:T(1024)} %param.23) | copy-start | bytes 24580
  165.1 18.5 %copy-start.5 = (f32[2048]{0:T(1024)S(1)}, f32[2048]{0:T(1024)}, u32[]{:S(2)}) copy-start(f32[2048]{0:T(1024)} %param.22) | copy-start | bytes 24580
Sparse Core Ops, SparseCore 0:
  111.0 52.8 all-reduce.1
where the time goes:
time: 193 us; the launch traced here: 191 us
  blocking collectives  87.6 us (45%)
  other arithmetic  41.9 us (22%)
  waiting for transfers between devices  22.9 us (12%)
  local copies, waits for them, and re-layouts  16.3 us (8%)
  between operations  14.3 us (7%)
  matrix products  8 us (4%)
    pmax x1, blocking collectives, body(): global_peak = lax.pmax(local_peak, 'blk')  29.1 us
    scatter-add x1, other arithmetic, page_sums(): jnp.zeros((total_count, row_count, head_size), jnp.float32).at[flat_rows]  29.1 us
    psum x1, blocking collectives, body(): total_num, total_den = lax.psum((prefix_num, prefix_den), 'blk')  26 us
    psum x1, waiting for transfers between devices, body(): total_num, total_den = lax.psum((prefix_num, prefix_den), 'blk')  22.9 us
    psum x1, blocking collectives, body(): lax.psum(partial_value.astype(jnp.bfloat16), 'kv').astype(jnp.float32)  16.9 us
    all_gather x1, blocking collectives, body(): all_queries = lax.all_gather(queries, 'blk', axis=0, tiled=True)  15.6 us
  transfers between devices with their start and end apart: 1, of which 1 were waited for; matrix products, arithmetic and copies ran while one was open for 2% of the time, Pallas kernels for 0%

commit v1 on v0

v1 whole, which is shorter than its diff:
```python
import functools

import jax
import jax.numpy as jnp
from jax import lax
from jax.experimental import pallas as pl
from jax.experimental.pallas import tpu as pltpu
from jax.sharding import PartitionSpec as P

SAMPLES = 16
LANES = 128
FLOOR = -(2.0**100)
LOG2E = 1.4426950408889634
VMEM = pl.BlockSpec(memory_space=pltpu.VMEM)
SMEM = pl.BlockSpec(memory_space=pltpu.SMEM)


def round_up(value, unit):
    return (value + unit - 1) // unit * unit


def iota(shape, dim):
    return lax.broadcasted_iota(jnp.int32, shape, dim)


def rounded_peak(peak):
    return peak.astype(jnp.bfloat16).astype(jnp.float32)


def softmax_parts(logits):
    peak = rounded_peak(jnp.max(logits, axis=1, keepdims=True))
    weights = jnp.exp2(logits - peak)
    return peak, weights, jnp.sum(weights, axis=1, keepdims=True)


def pack_stats(peak, den):
    high = den.astype(jnp.bfloat16).astype(jnp.float32)
    lane = iota((peak.shape[0], LANES), 1)
    stats = jnp.where(lane == 0, peak, jnp.where(lane == 1, high, den - high))
    return jnp.where(lane < 3, stats, 0.0)


def unpack_stats(stats):
    stats = stats.astype(jnp.float32)
    return stats[:, 0:1], stats[:, 1:2] + stats[:, 2:3]


def spread_rows(dest, base, block, heads, head_size, rows):
    reqs, drafts, _ = block.shape
    pad = rows - reqs * drafts
    for c in range(heads):
        cols = pl.ds(c * head_size, head_size)
        for r in range(reqs):
            dest[pl.ds(base + c * rows + r * drafts, drafts), :] = block[r, :, cols]
        if pad:
            dest[pl.ds(base + c * rows + reqs * drafts, pad), :] = jnp.zeros((pad, head_size), dest.dtype)


def layout_kernel(device_of, slots, local, rows, heads, drafts, page_tokens,
                  ids_ref, len_ref, page_ref, low_ref, high_ref, key_ref, start_ref):
    me = lax.axis_index("blk")
    prompts = len_ref.shape[0]

    def place(p, start):
        start_ref[p] = start
        return start + (len_ref[p] + page_tokens - 1) // page_tokens * page_tokens

    lax.fori_loop(0, prompts, place, jnp.int32(0))
    request = iota((rows, LANES), 0) // drafts

    def one(j, _):
        device = device_of(j, me)
        low = jnp.zeros((rows, LANES), jnp.int32)
        high = low
        for r in range(local):
            prompt = ids_ref[device * local + r] // SAMPLES
            start = start_ref[prompt]
            low = jnp.where(request == r, start, low)
            high = jnp.where(request == r, start + len_ref[prompt], high)
        for c in range(heads):
            place_at = pl.ds(pl.multiple_of((j * heads + c) * rows, rows), rows)
            low_ref[place_at, :] = low
            high_ref[place_at, :] = high
        return 0

    lax.fori_loop(0, slots, one, 0, unroll=slots <= 8)
    lane = iota((8, page_tokens), 1)
    for s in range(page_ref.shape[0]):
        key_ref[:, pl.ds(s * page_tokens, page_tokens)] = lane + page_ref[s] * page_tokens


def prefix_kernel(heads, rows, scale, q_ref, low_ref, high_ref, key_ref, pool_ref, *rest):
    out_ref, q_rows = rest
    slots = q_ref.shape[0]
    head_size = pool_ref.shape[2] // 2
    keys = pool_ref.shape[0] * pool_ref.shape[1]
    for j in range(slots):
        spread_rows(q_rows, j * heads * rows, q_ref.at[j], heads, head_size, rows)
    logits = lax.dot_general(
        q_rows[...], pool_ref[:, :, :head_size].reshape(keys, head_size),
        (((1,), (1,)), ((), ())), preferred_element_type=jnp.float32,
    )
    low, high = low_ref[...], high_ref[...]
    parts = []
    for k in range(0, keys, LANES):
        key = key_ref[0:1, k:k + LANES]
        live = (key >= low) & (key < high)
        parts.append(jnp.where(live, logits[:, k:k + LANES] * scale, FLOOR))
    peak, weights, den = softmax_parts(jnp.concatenate(parts, axis=1))
    num = jnp.dot(
        weights.astype(jnp.bfloat16), pool_ref[:, :, head_size:].reshape(keys, head_size),
        preferred_element_type=jnp.float32,
    )
    per = heads * rows
    out_ref[:, :, :head_size] = num.reshape(slots, per, head_size).astype(out_ref.dtype)
    out_ref[:, :, head_size:] = pack_stats(peak, den).reshape(slots, per, LANES).astype(out_ref.dtype)


def own_kernel(heads, rows, scale, len_ref, q_ref, tail_ref, fresh_ref, out_ref, q_rows, f_rows):
    reqs, drafts, _ = q_ref.shape
    tail = tail_ref.shape[1]
    head_size = tail_ref.shape[2] // 2
    spread_rows(q_rows, 0, q_ref, heads, head_size, rows)
    spread_rows(f_rows, 0, fresh_ref, 2, head_size, rows)
    queries = q_rows[...]
    contract = (((1,), (1,)), ((), ()))
    logits = lax.dot_general(
        queries, tail_ref[:, :, :head_size].reshape(reqs * tail, head_size),
        contract, preferred_element_type=jnp.float32,
    )
    total = heads * rows
    row = iota((total, tail), 0) % rows
    lane = iota((total, tail), 1)
    parts = []
    for r in range(reqs):
        live = (row // drafts == r) & (lane < len_ref[r])
        parts.append(jnp.where(live, logits[:, r * tail:(r + 1) * tail] * scale, FLOOR))
    fresh = lax.dot_general(
        queries, f_rows[0:rows, :], contract, preferred_element_type=jnp.float32
    )
    row = iota((total, rows), 0) % rows
    key = iota((total, rows), 1)
    live = (row // drafts == key // drafts) & (key % drafts <= row % drafts)
    fresh = jnp.where(live, fresh * scale, FLOOR)
    logits = jnp.concatenate(parts, axis=1)
    peak = jnp.maximum(
        jnp.max(logits, axis=1, keepdims=True), jnp.max(fresh, axis=1, keepdims=True)
    )
    peak = rounded_peak(peak)
    weights = jnp.exp2(logits - peak)
    fresh = jnp.exp2(fresh - peak)
    den = jnp.sum(weights, axis=1, keepdims=True) + jnp.sum(fresh, axis=1, keepdims=True)
    num = jnp.dot(
        weights.astype(jnp.bfloat16), tail_ref[:, :, head_size:].reshape(reqs * tail, head_size),
        preferred_element_type=jnp.float32,
    )
    num = num + jnp.dot(
        fresh.astype(jnp.bfloat16), f_rows[rows:2 * rows, :], preferred_element_type=jnp.float32
    )
    out_ref[:, :head_size] = num
    out_ref[:, head_size:] = pack_stats(peak, den)


def summed_parts(blocks, head_size):
    nums = [b[:, :head_size].astype(jnp.float32) for b in blocks]
    stats = [unpack_stats(b[:, head_size:]) for b in blocks]
    peak = functools.reduce(jnp.maximum, [s[0] for s in stats])
    factors = [jnp.exp2(s[0] - peak) for s in stats]
    num = sum(n * f for n, f in zip(nums, factors))
    den = sum(s[1] * f for s, f in zip(stats, factors))
    return num, peak, den


def merge_kernel(head_size, a_ref, b_ref, *out_refs):
    for j, out_ref in enumerate(out_refs):
        num, peak, den = summed_parts([a_ref[j], b_ref[j]], head_size)
        out_ref[:, :head_size] = num.astype(out_ref.dtype)
        out_ref[:, head_size:] = pack_stats(peak, den).astype(out_ref.dtype)


def project(num, den, weight_ref, out_ref, heads, rows):
    reqs, drafts, _ = out_ref.shape
    attention = (num / den).astype(jnp.bfloat16)
    head_size = attention.shape[1]
    value = sum(
        jnp.dot(
            attention[c * rows:(c + 1) * rows, :], weight_ref[c * head_size:(c + 1) * head_size, :],
            preferred_element_type=jnp.float32,
        )
        for c in range(heads)
    ).astype(out_ref.dtype)
    for r in range(reqs):
        out_ref[r] = value[r * drafts:(r + 1) * drafts, :]


def combine_kernel(heads, rows, head_size, *refs):
    *block_refs, weight_ref, out_ref = refs
    num, _, den = summed_parts([b[...] for b in block_refs], head_size)
    project(num, den, weight_ref, out_ref, heads, rows)


def combine_many_kernel(heads, rows, head_size, own_ref, many_ref, weight_ref, out_ref):
    def one(j, carry):
        num, peak, den = carry
        block = many_ref[j]
        next_peak, next_den = unpack_stats(block[:, head_size:])
        top = jnp.maximum(peak, next_peak)
        old, new = jnp.exp2(peak - top), jnp.exp2(next_peak - top)
        return num * old + block[:, :head_size].astype(jnp.float32) * new, top, den * old + next_den * new

    own = own_ref[...]
    carry = (own[:, :head_size], *unpack_stats(own[:, head_size:]))
    num, _, den = lax.fori_loop(0, many_ref.shape[0], one, carry)
    project(num, den, weight_ref, out_ref, heads, rows)


def final_kernel(*refs):
    *part_refs, hidden_ref, gain_ref, score_ref, out_ref, scores_ref = refs
    reqs, drafts, width = hidden_ref.shape
    mix = gain_ref[...] * score_ref[...]
    lane = iota((1, LANES), 1)
    scores = jnp.zeros((1, LANES), jnp.float32)
    for r in range(reqs):
        total = sum(p[r].astype(jnp.float32) for p in part_refs)
        value = (hidden_ref[r].astype(jnp.float32) + total).astype(out_ref.dtype)
        out_ref[r] = value
        last = value.astype(jnp.float32)[drafts - 1:drafts, :]
        square = jnp.sum(last * last, axis=1, keepdims=True) / width
        score = jnp.sum(last * mix, axis=1, keepdims=True) * lax.rsqrt(square + 1e-06)
        scores = jnp.where(lane == r, score, scores)
    scores_ref[...] = scores


def body(sizes, prefix_pool, slot_page, prompt_len, request_ids, tail_len, tail_cache, queries, new_kv, hidden,
         out_weight, norm_gain, score_weight):
    blk, kv = sizes
    pool = prefix_pool[0]
    page_count, page_tokens, head_pair = pool.shape
    head_size = head_pair // 2
    local, drafts, head_width = queries.shape
    heads = head_width // head_size
    rows = round_up(local * drafts, 16)
    per = heads * rows
    keys = page_count * page_tokens
    width = hidden.shape[2]
    scale = head_size ** (-0.5) * LOG2E
    paired = blk in (2, 4, 8)
    half = blk // 2

    def swap(x, axis, size, mask):
        return lax.ppermute(x, axis, [(i, i ^ mask) for i in range(size)])

    def device_of(j, me):
        if not paired:
            return j
        return me ^ (j * 2) if isinstance(j, int) and j < half else me ^ (j % half * 2 + j // half)

    low, high, key = pl.pallas_call(
        functools.partial(layout_kernel, device_of, blk, local, rows, heads, drafts, page_tokens),
        out_shape=(
            jax.ShapeDtypeStruct((blk * per, LANES), jnp.int32),
            jax.ShapeDtypeStruct((blk * per, LANES), jnp.int32),
            jax.ShapeDtypeStruct((8, keys), jnp.int32),
        ),
        in_specs=[SMEM] * 3,
        out_specs=(VMEM,) * 3,
        scratch_shapes=[pltpu.SMEM(prompt_len.shape, jnp.int32)],
        name="key_ranges",
    )(request_ids, prompt_len, slot_page)

    own = pl.pallas_call(
        functools.partial(own_kernel, heads, rows, scale),
        out_shape=jax.ShapeDtypeStruct((per, head_size + LANES), jnp.float32),
        in_specs=[SMEM] + [VMEM] * 3,
        out_specs=VMEM,
        scratch_shapes=[
            pltpu.VMEM((per, head_size), jnp.bfloat16),
            pltpu.VMEM((2 * rows, head_size), jnp.bfloat16),
        ],
        name="own_keys",
    )(tail_len, queries, tail_cache[0], new_kv[0])

    def prefix(block, first):
        slots = block.shape[0]
        step = min(slots, 4)
        grid = slots // step
        offset = first // step
        return pl.pallas_call(
            functools.partial(prefix_kernel, heads, rows, scale),
            out_shape=jax.ShapeDtypeStruct((slots, per, head_size + LANES), jnp.bfloat16),
            grid=(grid,),
            in_specs=[
                pl.BlockSpec((step, local, drafts, head_width), lambda i: (i, 0, 0, 0)),
                pl.BlockSpec((step * per, LANES), lambda i: (i + offset, 0)),
                pl.BlockSpec((step * per, LANES), lambda i: (i + offset, 0)),
                pl.BlockSpec((8, keys), lambda i: (0, 0)),
                pl.BlockSpec((page_count, page_tokens, head_pair), lambda i: (0, 0, 0)),
            ],
            out_specs=pl.BlockSpec((step, per, head_size + LANES), lambda i: (i, 0, 0)),
            scratch_shapes=[pltpu.VMEM((step * per, head_size), jnp.bfloat16)],
            compiler_params=pltpu.CompilerParams(vmem_limit_bytes=32 * 1024 * 1024),
            name="prefix_keys",
        )(block, low, high, key, pool)

    partial_shape = jax.ShapeDtypeStruct((local, drafts, width), jnp.bfloat16)
    limit = pltpu.CompilerParams(vmem_limit_bytes=32 * 1024 * 1024)
    if paired:
        column = [queries] + [swap(queries, "blk", blk, 2 * j) for j in range(1, half)]
        mine = jnp.stack(column)
        theirs = swap(mine, "blk", blk, 1)
        sums_mine = prefix(mine, 0)
        sums_theirs = prefix(theirs, half)
        back = swap(sums_theirs, "blk", blk, 1)
        block_shape = jax.ShapeDtypeStruct((per, head_size + LANES), jnp.bfloat16)
        merged = pl.pallas_call(
            functools.partial(merge_kernel, head_size),
            out_shape=(block_shape,) * half,
            in_specs=[VMEM] * 2,
            out_specs=(VMEM,) * half,
            name="merge_cores",
        )(sums_mine, back)
        blocks = [merged[0]] + [swap(merged[j], "blk", blk, 2 * j) for j in range(1, half)]
        share = pl.pallas_call(
            functools.partial(combine_kernel, heads, rows, head_size),
            out_shape=partial_shape,
            in_specs=[VMEM] * (half + 2),
            out_specs=VMEM,
            compiler_params=limit,
            name="combine_project",
        )(own, *blocks, out_weight)
    else:
        gathered = lax.all_gather(queries, "blk", axis=0)
        blocks = lax.all_to_all(prefix(gathered, 0), "blk", 0, 0)
        share = pl.pallas_call(
            functools.partial(combine_many_kernel, heads, rows, head_size),
            out_shape=partial_shape,
            in_specs=[VMEM] * 3,
            out_specs=VMEM,
            compiler_params=limit,
            name="combine_project",
        )(own, blocks, out_weight)
    if kv in (2, 4):
        shares = [share] + [swap(share, "kv", kv, j) for j in range(1, kv)]
    else:
        shares = [lax.psum(share, "kv")]
    hidden_out, scores = pl.pallas_call(
        final_kernel,
        out_shape=(
            jax.ShapeDtypeStruct(hidden.shape, hidden.dtype),
            jax.ShapeDtypeStruct((1, LANES), jnp.float32),
        ),
        in_specs=[VMEM] * (len(shares) + 3),
        out_specs=(VMEM, VMEM),
        name="residual_scores",
    )(*shares, hidden, norm_gain.reshape(1, width), score_weight.reshape(1, width))
    return hidden_out, scores[0, :local]


def solution(mesh):
    in_specs = (
        P("kv", "blk", None, None),
        P("blk"),
        P(),
        P(),
        P("blk"),
        P("kv", "blk", None, None),
        P("blk", None, "kv"),
        P("kv", "blk", None, None),
        P("blk", None, None),
        P("kv", None),
        P(),
        P(),
    )
    out_specs = (P("blk", None, None), P("blk"))
    sizes = (mesh.shape["blk"], mesh.shape["kv"])
    return jax.shard_map(
        functools.partial(body, sizes), mesh=mesh, in_specs=in_specs, out_specs=out_specs, check_vma=False
    )
```

time: 193 us -> 44 us (0.23)
  blocking collectives: 87.6 us -> 0 us
  other arithmetic: 41.9 us -> 0.79 us
  starting transfers between devices: 0.04 us -> 14.2 us
  waiting for transfers between devices: 22.9 us -> 9.29 us
  between operations: 14.3 us -> 0.71 us
  Pallas kernels: 0 us -> 9.92 us
  matrix products: 8 us -> 0 us
  local copies, waits for them, and re-layouts: 16.3 us -> 8.55 us
    psum x2 -> x0, blocking collectives: 42.9 us -> none  [the longest x1 26 us: body(): total_num, total_den = lax.psum((prefix_num, prefix_den), 'blk')]
    scatter-add x2 -> x0, other arithmetic: 30.9 us -> none  [the longest x1 29.1 us: page_sums(): jnp.zeros((total_count, row_count, head_size), jnp.float32).at[flat_rows]]
    pmax x1 -> x0, blocking collectives: 29.1 us -> none  [body(): global_peak = lax.pmax(local_peak, 'blk')]
    psum x1 -> x0, waiting for transfers between devices: 22.9 us -> none  [body(): total_num, total_den = lax.psum((prefix_num, prefix_den), 'blk')]
    all_gather x1 -> x0, blocking collectives: 15.6 us -> none  [body(): all_queries = lax.all_gather(queries, 'blk', axis=0, tiled=True)]
    ppermute x0 -> x11, starting transfers between devices: none -> 14.2 us  [swap(): return lax.ppermute(x, axis, [(i, i ^ mask) for i in range(size)])]
    pallas_call x0 -> x7, Pallas kernels: none -> 9.92 us  [the longest x1 2.31 us: body(): pl.pallas_call(functools.partial(own_kernel, heads, rows, scale), out_sha...]
    gather x6 -> x0, local copies, waits for them, and re-layouts: 9.46 us -> none  [the longest x1 3.5 us: body(): picked = all_queries[slot_rows].reshape(page_count, -1, head_size)]
  transfers between devices with their start and end apart: 1 -> 11, of which waited for: 1 -> 5; matrix products, arithmetic and copies ran while one was open for 2% -> 0% of each run, Pallas kernels for 0% -> 11%
where the time goes in v1:
time: 44 us; the launch traced here: 43.5 us
  starting transfers between devices  14.2 us (32%)
  Pallas kernels  9.92 us (23%)
  waiting for transfers between devices  9.29 us (21%)
  local copies, waits for them, and re-layouts  8.55 us (19%)
  other arithmetic  0.79 us (2%)
  between operations  0.71 us (2%)
    ppermute x11, starting transfers between devices, swap(): return lax.ppermute(x, axis, [(i, i ^ mask) for i in range(size)])  14.2 us
    ppermute x11, waiting for transfers between devices, swap(): return lax.ppermute(x, axis, [(i, i ^ mask) for i in range(size)])  9.29 us
    unnamed x28, local copies, waits for them, and re-layouts  7.43 us
    pallas_call x1, Pallas kernels, body(): pl.pallas_call(functools.partial(own_kernel, heads, rows, scale), out_sha...  2.31 us
    pallas_call x1, Pallas kernels, body(): pl.pallas_call(functools.partial(merge_kernel, head_size), out_shape=(blo...  1.89 us
    pallas_call x2, Pallas kernels, prefix(): pl.pallas_call(functools.partial(prefix_kernel, heads, rows, scale), out_...  1.77 us
    pallas_call x1, Pallas kernels, body(): pl.pallas_call(functools.partial(layout_kernel, device_of, blk, local, ro...  1.74 us
    pallas_call x1, Pallas kernels, body(): pl.pallas_call(final_kernel, out_shape=(jax.ShapeDtypeStruct(hidden.shape...  1.69 us
  transfers between devices with their start and end apart: 11, of which 5 were waited for; matrix products, arithmetic and copies ran while one was open for 0% of the time, Pallas kernels for 11%

profile of v1, /device:TPU:0, one launch (start us, length us, event | category | flops | bytes accessed | tf_op | source)
XLA Modules:
  0.0 43.5 jit_solution(2696161439763835436)
XLA Ops:
  0.6 3.1 %collective-permute-start = (bf16[6,2,512]{2,1,0:T(2,128)(2,1)}, bf16[6,2,512]{2,1,0:T(2,128)(2,1)S(1)}, u32[]{:S(2)}, u32[]{:S(2)}) collective-permute-start(bf16[6,2,512]{2,1,0:T(2,128)(2,1)} %q_ref.1), channel_id=1, source_target_pairs={{0,2},{1,3},{2,0},{3,1},{4,6},{5,7},{6,4},{7,5},{8,10},{9,11},{10,... | collective-permute-start | bytes 36872 | tf_op jit(solution)/shard_map/ppermute | solution.py:251
  3.7 2.6 %collective-permute-start.1 = (bf16[6,2,512]{2,1,0:T(2,128)(2,1)}, bf16[6,2,512]{2,1,0:T(2,128)(2,1)S(1)}, u32[]{:S(2)}, u32[]{:S(2)}) collective-permute-start(bf16[6,2,512]{2,1,0:T(2,128)(2,1)} %q_ref.1), channel_id=1, source_target_pairs={{0,4},{1,5},{2,6},{3,7},{4,0},{5,1},{6,2},{7,3},{8,12},{9,13},{10,... | collective-permute-start | bytes 36872 | tf_op jit(solution)/shard_map/ppermute | solution.py:251
  6.3 0.0 collective-permute-start.2
  6.3 0.0 collective-permute-done
  6.3 2.2 %collective-permute-done.1 = bf16[6,2,512]{2,1,0:T(2,128)(2,1)S(1)} collective-permute-done((bf16[6,2,512]{2,1,0:T(2,128)(2,1)}, bf16[6,2,512]{2,1,0:T(2,128)(2,1)S(1)}, u32[]{:S(2)}, u32[]{:S(2)}) %collective-permute-start.1) | collective-permute-done | bytes 12320 | tf_op jit(solution)/shard_map/ppermute | solution.py:251
  8.5 3.5 %collective-permute-done.2 = bf16[6,2,512]{2,1,0:T(2,128)(2,1)S(1)} collective-permute-done((bf16[6,2,512]{2,1,0:T(2,128)(2,1)}, bf16[6,2,512]{2,1,0:T(2,128)(2,1)S(1)}, u32[]{:S(2)}, u32[]{:S(2)}) %collective-permute-start.2) | collective-permute-done | bytes 12320 | tf_op jit(solution)/shard_map/ppermute | solution.py:251
  12.0 0.8 %pad_maximum_fusion.q_ref = bf16[4,6,2,512]{3,2,1,0:T(2,128)(2,1)S(1)} fusion(bf16[1,6,2,512]{3,2,1,0:T(2,128)(2,1)S(1)} %bitcast.17, bf16[1,6,2,512]{3,2,1,0:T(2,128)(2,1)S(1)} %bitcast.16, bf16[1,6,2,512]{3,2,1,0:T(2,128)(2,1)S(1)} %bitcast.15, bf16[1,6,2,512]{3,2,1,0:T(2,128)(2,1)} %bitcast.14), kind=kLoop, calls=%fused_computation | loop fusion | flops 73728 | bytes 98304 | tf_op jit(solution)/shard_map/stack | solution.py:309
  12.8 0.1 collective-permute-start.3
  12.9 1.7 %key_ranges.1 = (s32[256,128]{1,0:T(8,128)}, s32[256,128]{1,0:T(8,128)}, s32[8,1536]{1,0:T(8,128)}) custom-call(s32[48]{0:T(128)} %ids_ref.1, s32[3]{0:T(128)} %len_ref.3, s32[24]{0:T(128)} %page_ref.1), custom_call_target="tpu_custom_call" | custom-call | tf_op jit(solution)/shard_map/key_ranges/pallas_call | solution.py:258
  14.6 0.0 collective-permute-done.3.q_ref
  14.6 0.0 copy-start
  14.6 1.4 %copy-done = bf16[1,24,64,512]{3,2,1,0:T(8,128)(2,1)S(1)} copy-done((bf16[1,24,64,512]{3,2,1,0:T(8,128)(2,1)S(1)}, bf16[1,24,64,512]{3,2,1,0:T(8,128)(2,1)}, u32[]{:S(2)}) %copy-start) | copy-done | bytes 1572888
  16.0 0.0 copy-start.3
  16.0 0.9 %copy-done.3 = s32[256,128]{1,0:T(8,128)S(1)} copy-done((s32[256,128]{1,0:T(8,128)S(1)}, s32[256,128]{1,0:T(8,128)}, u32[]{:S(2)}) %copy-start.3) | copy-done | bytes 131096
  16.9 0.0 copy-start.4
  16.9 0.9 %copy-done.4 = s32[256,128]{1,0:T(8,128)S(1)} copy-done((s32[256,128]{1,0:T(8,128)S(1)}, s32[256,128]{1,0:T(8,128)}, u32[]{:S(2)}) %copy-start.4) | copy-done | bytes 131096
  17.8 0.0 copy-start.8
  17.9 0.8 %copy-done.8 = s32[8,1536]{1,0:T(8,128)S(1)} copy-done((s32[8,1536]{1,0:T(8,128)S(1)}, s32[8,1536]{1,0:T(8,128)}, u32[]{:S(2)}) %copy-start.8) | copy-done | bytes 49176
  18.6 0.0 copy-start.1
  18.6 0.0 copy-start.2
  18.7 0.9 %prefix_keys.3 = bf16[4,32,384]{2,1,0:T(8,128)(2,1)S(1)} custom-call(bf16[4,6,2,512]{3,2,1,0:T(2,128)(2,1)S(1)} %collective-permute-done.3.q_ref, s32[256,128]{1,0:T(8,128)S(1)} %copy-done.3, s32[256,128]{1,0:T(8,128)S(1)} %copy-done.4, s32[8,1536]{1,0:T(8,128)S(1)} %copy-done.8, bf16[24,64,512]{2,1,0:T(8,128)(2,1)S(1)} %bitcast.11), custom_call_target="tpu_custom_call" | custom-call | tf_op jit(solution)/shard_map/prefix_keys/pallas_call | solution.py:288
  19.5 0.6 %collective-permute-start.4 = (bf16[4,32,384]{2,1,0:T(8,128)(2,1)S(1)}, bf16[4,32,384]{2,1,0:T(8,128)(2,1)S(1)}, u32[]{:S(2)}, u32[]{:S(2)}) collective-permute-start(bf16[4,32,384]{2,1,0:T(8,128)(2,1)S(1)} %prefix_keys.3), channel_id=1, source_target_pairs={{0,1},{1,0},{2,3},{3,2},{4,5},{5,4},{6,7},{7,6},{8,9},{9,8},{10,11... | collective-permute-start | bytes 294920 | tf_op jit(solution)/shard_map/ppermute | solution.py:251
  20.1 0.0 copy-done.1
  20.1 0.9 %prefix_keys.2.a_ref = bf16[4,32,384]{2,1,0:T(8,128)(2,1)S(1)} custom-call(bf16[4,6,2,512]{3,2,1,0:T(2,128)(2,1)S(1)} %pad_maximum_fusion.q_ref, s32[256,128]{1,0:T(8,128)S(1)} %copy-done.3, s32[256,128]{1,0:T(8,128)S(1)} %copy-done.4, s32[8,1536]{1,0:T(8,128)S(1)} %copy-done.8, bf16[24,64,512]{2,1,0:T(8,128)(2,1)S(1)} %bitcast.12), custom_call_target="tpu_custom_call" | custom-call | tf_op jit(solution)/shard_map/prefix_keys/pallas_call | solution.py:288
  21.0 0.0 copy-start.5
  21.0 0.6 %copy-done.5 = bf16[4,32,384]{2,1,0:T(8,128)(2,1)} copy-done((bf16[4,32,384]{2,1,0:T(8,128)(2,1)}, bf16[4,32,384]{2,1,0:T(8,128)(2,1)S(1)}, u32[]{:S(2)}) %copy-start.5) | copy-done | bytes 98328
  21.6 0.0 collective-permute-done.4.b_ref
  21.6 0.0 copy-start.10
  21.6 0.6 %copy-done.10 = bf16[4,32,384]{2,1,0:T(8,128)(2,1)} copy-done((bf16[4,32,384]{2,1,0:T(8,128)(2,1)}, bf16[4,32,384]{2,1,0:T(8,128)(2,1)S(1)}, u32[]{:S(2)}) %copy-start.10) | copy-done | bytes 98328
  22.3 1.9 %merge_cores.1 = (bf16[32,384]{1,0:T(8,128)(2,1)}, bf16[32,384]{1,0:T(8,128)(2,1)}, bf16[32,384]{1,0:T(8,128)(2,1)}, bf16[32,384]{1,0:T(8,128)(2,1)}) custom-call(bf16[4,32,384]{2,1,0:T(8,128)(2,1)} %copy-done.5, bf16[4,32,384]{2,1,0:T(8,128)(2,1)} %copy-done.10), custom_call_target="tpu_custom_call" | custom-call | tf_op jit(solution)/shard_map/merge_cores/pallas_call | solution.py:315
  24.2 0.0 collective-permute-start.5
  24.2 0.7 %collective-permute-start.6 = (bf16[32,384]{1,0:T(8,128)(2,1)}, bf16[32,384]{1,0:T(8,128)(2,1)S(1)}, u32[]{:S(2)}, u32[]{:S(2)}) collective-permute-start(bf16[32,384]{1,0:T(8,128)(2,1)} %get-tuple-element.16), channel_id=1, source_target_pairs={{0,4},{1,5},{2,6},{3,7},{4,0},{5,1},{6,2},{7,3},{8,12},{9,13},{10,... | collective-permute-start | bytes 73736 | tf_op jit(solution)/shard_map/ppermute | solution.py:251
  24.9 3.7 %collective-permute-start.7 = (bf16[32,384]{1,0:T(8,128)(2,1)}, bf16[32,384]{1,0:T(8,128)(2,1)S(1)}, u32[]{:S(2)}, u32[]{:S(2)}) collective-permute-start(bf16[32,384]{1,0:T(8,128)(2,1)} %get-tuple-element.17), channel_id=1, source_target_pairs={{0,6},{1,7},{2,4},{3,5},{4,2},{5,3},{6,0},{7,1},{8,14},{9,15},{10,... | collective-permute-start | bytes 73736 | tf_op jit(solution)/shard_map/ppermute | solution.py:251
  28.5 2.3 %own_keys.1.refs_0_ = f32[32,384]{1,0:T(8,128)} custom-call(s32[6]{0:T(128)} %len_ref.2, bf16[6,2,512]{2,1,0:T(2,128)(2,1)} %q_ref.1, bf16[6,128,512]{2,1,0:T(8,128)(2,1)} %bitcast.13, bf16[6,2,512]{2,1,0:T(2,128)(2,1)} %bitcast.18), custom_call_target="tpu_custom_call" | custom-call | tf_op jit(solution)/shard_map/own_keys/pallas_call | solution.py:271
  30.9 0.0 collective-permute-done.5.refs_2_
  30.9 0.0 collective-permute-done.6.refs_3_
  30.9 0.0 collective-permute-done.7.refs_4_
  30.9 0.0 copy-done.2
  30.9 0.0 copy-start.7
  30.9 0.8 %copy-done.7 = f32[32,384]{1,0:T(8,128)S(1)} copy-done((f32[32,384]{1,0:T(8,128)S(1)}, f32[32,384]{1,0:T(8,128)}, u32[]{:S(2)}) %copy-start.7) | copy-done | bytes 49176
  31.7 0.0 copy-start.9
  31.7 0.7 %copy-done.9 = bf16[32,384]{1,0:T(8,128)(2,1)S(1)} copy-done((bf16[32,384]{1,0:T(8,128)(2,1)S(1)}, bf16[32,384]{1,0:T(8,128)(2,1)}, u32[]{:S(2)}) %copy-start.9) | copy-done | bytes 24600
  32.4 0.5 %combine_project.1.refs_0_ = bf16[6,2,2048]{2,1,0:T(2,128)(2,1)S(1)} custom-call(f32[32,384]{1,0:T(8,128)S(1)} %copy-done.7, bf16[32,384]{1,0:T(8,128)(2,1)S(1)} %copy-done.9, bf16[32,384]{1,0:T(8,128)(2,1)S(1)} %collective-permute-done.5.refs_2_, bf16[32,384]{1,0:T(8,128)(2,1)S(1)} %collective-permute-done.6.refs_3_, ...), custom_call_target="tpu_custom_call" | custom-call | tf_op jit(solution)/shard_map/combine_project/pallas_call | solution.py:323
  32.9 0.0 copy-start.6
  32.9 2.5 %collective-permute-start.10 = (bf16[6,2,2048]{2,1,0:T(2,128)(2,1)S(1)}, bf16[6,2,2048]{2,1,0:T(2,128)(2,1)S(1)}, u32[]{:S(2)}, u32[]{:S(2)}) collective-permute-start(bf16[6,2,2048]{2,1,0:T(2,128)(2,1)S(1)} %combine_project.1.refs_0_), channel_id=1, source_target_pairs={{0,24},{8,16},{16,8},{24,0},{1,25},{9,17},{17,9},{25,1},{2,26},{10... | collective-permute-start | bytes 147464 | tf_op jit(solution)/shard_map/ppermute | solution.py:251
  35.5 0.5 %collective-permute-start.8 = (bf16[6,2,2048]{2,1,0:T(2,128)(2,1)S(1)}, bf16[6,2,2048]{2,1,0:T(2,128)(2,1)S(1)}, u32[]{:S(2)}, u32[]{:S(2)}) collective-permute-start(bf16[6,2,2048]{2,1,0:T(2,128)(2,1)S(1)} %combine_project.1.refs_0_), channel_id=1, source_target_pairs={{0,8},{8,0},{16,24},{24,16},{1,9},{9,1},{17,25},{25,17},{2,10},{10... | collective-permute-start | bytes 147464 | tf_op jit(solution)/shard_map/ppermute | solution.py:251
  36.0 0.5 %collective-permute-start.9 = (bf16[6,2,2048]{2,1,0:T(2,128)(2,1)S(1)}, bf16[6,2,2048]{2,1,0:T(2,128)(2,1)S(1)}, u32[]{:S(2)}, u32[]{:S(2)}) collective-permute-start(bf16[6,2,2048]{2,1,0:T(2,128)(2,1)S(1)} %combine_project.1.refs_0_), channel_id=1, source_target_pairs={{0,16},{8,24},{16,0},{24,8},{1,17},{9,25},{17,1},{25,9},{2,18},{10... | collective-permute-start | bytes 147464 | tf_op jit(solution)/shard_map/ppermute | solution.py:251
  36.5 2.0 %collective-permute-done.10.refs_3_ = bf16[6,2,2048]{2,1,0:T(2,128)(2,1)S(1)} collective-permute-done((bf16[6,2,2048]{2,1,0:T(2,128)(2,1)S(1)}, bf16[6,2,2048]{2,1,0:T(2,128)(2,1)S(1)}, u32[]{:S(2)}, u32[]{:S(2)}) %collective-permute-start.10) | collective-permute-done | bytes 49184 | tf_op jit(solution)/shard_map/ppermute | solution.py:251
  38.5 0.0 copy-start.11
  38.5 1.1 %collective-permute-done.8.refs_1_ = bf16[6,2,2048]{2,1,0:T(2,128)(2,1)S(1)} collective-permute-done((bf16[6,2,2048]{2,1,0:T(2,128)(2,1)S(1)}, bf16[6,2,2048]{2,1,0:T(2,128)(2,1)S(1)}, u32[]{:S(2)}, u32[]{:S(2)}) %collective-permute-start.8) | collective-permute-done | bytes 49184 | tf_op jit(solution)/shard_map/ppermute | solution.py:251
  39.5 0.0 copy-start.12
  39.5 0.5 %collective-permute-done.9.refs_2_ = bf16[6,2,2048]{2,1,0:T(2,128)(2,1)S(1)} collective-permute-done((bf16[6,2,2048]{2,1,0:T(2,128)(2,1)S(1)}, bf16[6,2,2048]{2,1,0:T(2,128)(2,1)S(1)}, u32[]{:S(2)}, u32[]{:S(2)}) %collective-permute-start.9) | collective-permute-done | bytes 49184 | tf_op jit(solution)/shard_map/ppermute | solution.py:251
  40.1 0.0 copy-start.13
  40.1 0.0 copy-done.6
  40.1 0.0 copy-done.11
  40.1 0.1 copy-done.12
  40.2 0.5 %copy-done.13 = bf16[6,2,2048]{2,1,0:T(2,128)(2,1)} copy-done((bf16[6,2,2048]{2,1,0:T(2,128)(2,1)}, bf16[6,2,2048]{2,1,0:T(2,128)(2,1)S(1)}, u32[]{:S(2)}) %copy-start.13) | copy-done | bytes 49176
  40.7 1.7 %residual_scores.1 = (bf16[6,2,2048]{2,1,0:T(2,128)(2,1)}, f32[1,128]{1,0:T(1,128)}) custom-call(bf16[6,2,2048]{2,1,0:T(2,128)(2,1)} %copy-done.6, bf16[6,2,2048]{2,1,0:T(2,128)(2,1)} %copy-done.12, bf16[6,2,2048]{2,1,0:T(2,128)(2,1)} %copy-done.13, bf16[6,2,2048]{2,1,0:T(2,128)(2,1)} %copy-done.11, bf16[6,2,2048]{2,1,0:T(2,128)(2,1)} %refs_4_.1, ...), custom_call_target="tpu_custom_call" | custom-call | tf_op jit(solution)/shard_map/residual_scores/pallas_call | solution.py:346
  42.4 1.1 %slice_bitcast_fusion = f32[6]{0:T(128)} fusion(f32[1,128]{1,0:T(1,128)} %get-tuple-element.19), kind=kLoop, calls=%fused_computation.1 | loop fusion | bytes 48 | tf_op jit(solution)/shard_map/squeeze | solution.py:356
Async XLA Ops:
  0.6 5.7 %collective-permute-start = (bf16[6,2,512]{2,1,0:T(2,128)(2,1)}, bf16[6,2,512]{2,1,0:T(2,128)(2,1)S(1)}, u32[]{:S(2)}, u32[]{:S(2)}) collective-permute-start(bf16[6,2,512]{2,1,0:T(2,128)(2,1)} %q_ref.1), channel_id=1, source_target_pairs={{0,2},{1,3},{2,0},{3,1},{4,6},{5,7},{6,4},{7,5},{8,10},{9,11},{10,... | collective-permute-start | bytes 36872 | tf_op jit(solution)/shard_map/ppermute | solution.py:251
  3.7 4.8 %collective-permute-start.1 = (bf16[6,2,512]{2,1,0:T(2,128)(2,1)}, bf16[6,2,512]{2,1,0:T(2,128)(2,1)S(1)}, u32[]{:S(2)}, u32[]{:S(2)}) collective-permute-start(bf16[6,2,512]{2,1,0:T(2,128)(2,1)} %q_ref.1), channel_id=1, source_target_pairs={{0,4},{1,5},{2,6},{3,7},{4,0},{5,1},{6,2},{7,3},{8,12},{9,13},{10,... | collective-permute-start | bytes 36872 | tf_op jit(solution)/shard_map/ppermute | solution.py:251
  6.3 5.7 %collective-permute-start.2 = (bf16[6,2,512]{2,1,0:T(2,128)(2,1)}, bf16[6,2,512]{2,1,0:T(2,128)(2,1)S(1)}, u32[]{:S(2)}, u32[]{:S(2)}) collective-permute-start(bf16[6,2,512]{2,1,0:T(2,128)(2,1)} %q_ref.1), channel_id=1, source_target_pairs={{0,6},{1,7},{2,4},{3,5},{4,2},{5,3},{6,0},{7,1},{8,14},{9,15},{10,... | collective-permute-start | bytes 36872 | tf_op jit(solution)/shard_map/ppermute | solution.py:251
  12.8 1.8 %collective-permute-start.3 = (bf16[4,6,2,512]{3,2,1,0:T(2,128)(2,1)S(1)}, bf16[4,6,2,512]{3,2,1,0:T(2,128)(2,1)S(1)}, u32[]{:S(2)}, u32[]{:S(2)}) collective-permute-start(bf16[4,6,2,512]{3,2,1,0:T(2,128)(2,1)S(1)} %pad_maximum_fusion.q_ref), channel_id=1, source_target_pairs={{0,1},{1,0},{2,3},{3,2},{4,5},{5,4},{6,7},{7,6},{8,9},{9,8},{10,11... | collective-permute-start | bytes 147464 | tf_op jit(solution)/shard_map/ppermute | solution.py:251
  14.6 1.4 %copy-start = (bf16[1,24,64,512]{3,2,1,0:T(8,128)(2,1)S(1)}, bf16[1,24,64,512]{3,2,1,0:T(8,128)(2,1)}, u32[]{:S(2)}) copy-start(bf16[1,24,64,512]{3,2,1,0:T(8,128)(2,1)} %param.12) | copy-start | bytes 4718596
  16.0 0.9 %copy-start.3 = (s32[256,128]{1,0:T(8,128)S(1)}, s32[256,128]{1,0:T(8,128)}, u32[]{:S(2)}) copy-start(s32[256,128]{1,0:T(8,128)} %get-tuple-element.11.low_ref) | copy-start | bytes 393220
  16.9 0.9 %copy-start.4 = (s32[256,128]{1,0:T(8,128)S(1)}, s32[256,128]{1,0:T(8,128)}, u32[]{:S(2)}) copy-start(s32[256,128]{1,0:T(8,128)} %get-tuple-element.12.high_ref) | copy-start | bytes 393220
  17.8 0.8 %copy-start.8 = (s32[8,1536]{1,0:T(8,128)S(1)}, s32[8,1536]{1,0:T(8,128)}, u32[]{:S(2)}) copy-start(s32[8,1536]{1,0:T(8,128)} %get-tuple-element.13.key_ref) | copy-start | bytes 147460
  18.6 1.5 %copy-start.1 = (bf16[1,24,64,512]{3,2,1,0:T(8,128)(2,1)S(1)}, bf16[1,24,64,512]{3,2,1,0:T(8,128)(2,1)}, u32[]{:S(2)}) copy-start(bf16[1,24,64,512]{3,2,1,0:T(8,128)(2,1)} %param.12) | copy-start | bytes 4718596
  18.6 12.2 %copy-start.2 = (bf16[512,2048]{1,0:T(8,128)(2,1)S(1)}, bf16[512,2048]{1,0:T(8,128)(2,1)}, u32[]{:S(2)}) copy-start(bf16[512,2048]{1,0:T(8,128)(2,1)} %refs_5_.1) | copy-start | bytes 6291460
  19.5 2.1 %collective-permute-start.4 = (bf16[4,32,384]{2,1,0:T(8,128)(2,1)S(1)}, bf16[4,32,384]{2,1,0:T(8,128)(2,1)S(1)}, u32[]{:S(2)}, u32[]{:S(2)}) collective-permute-start(bf16[4,32,384]{2,1,0:T(8,128)(2,1)S(1)} %prefix_keys.3), channel_id=1, source_target_pairs={{0,1},{1,0},{2,3},{3,2},{4,5},{5,4},{6,7},{7,6},{8,9},{9,8},{10,11... | collective-permute-start | bytes 294920 | tf_op jit(solution)/shard_map/ppermute | solution.py:251
  21.0 0.6 %copy-start.5 = (bf16[4,32,384]{2,1,0:T(8,128)(2,1)}, bf16[4,32,384]{2,1,0:T(8,128)(2,1)S(1)}, u32[]{:S(2)}) copy-start(bf16[4,32,384]{2,1,0:T(8,128)(2,1)S(1)} %prefix_keys.2.a_ref) | copy-start | bytes 294916
  21.6 0.6 %copy-start.10 = (bf16[4,32,384]{2,1,0:T(8,128)(2,1)}, bf16[4,32,384]{2,1,0:T(8,128)(2,1)S(1)}, u32[]{:S(2)}) copy-start(bf16[4,32,384]{2,1,0:T(8,128)(2,1)S(1)} %collective-permute-done.4.b_ref) | copy-start | bytes 294916
  24.2 6.7 %collective-permute-start.5 = (bf16[32,384]{1,0:T(8,128)(2,1)}, bf16[32,384]{1,0:T(8,128)(2,1)S(1)}, u32[]{:S(2)}, u32[]{:S(2)}) collective-permute-start(bf16[32,384]{1,0:T(8,128)(2,1)} %get-tuple-element.15), channel_id=1, source_target_pairs={{0,2},{1,3},{2,0},{3,1},{4,6},{5,7},{6,4},{7,5},{8,10},{9,11},{10,... | collective-permute-start | bytes 73736 | tf_op jit(solution)/shard_map/ppermute | solution.py:251
  24.2 6.7 %collective-permute-start.6 = (bf16[32,384]{1,0:T(8,128)(2,1)}, bf16[32,384]{1,0:T(8,128)(2,1)S(1)}, u32[]{:S(2)}, u32[]{:S(2)}) collective-permute-start(bf16[32,384]{1,0:T(8,128)(2,1)} %get-tuple-element.16), channel_id=1, source_target_pairs={{0,4},{1,5},{2,6},{3,7},{4,0},{5,1},{6,2},{7,3},{8,12},{9,13},{10,... | collective-permute-start | bytes 73736 | tf_op jit(solution)/shard_map/ppermute | solution.py:251
  24.9 6.0 %collective-permute-start.7 = (bf16[32,384]{1,0:T(8,128)(2,1)}, bf16[32,384]{1,0:T(8,128)(2,1)S(1)}, u32[]{:S(2)}, u32[]{:S(2)}) collective-permute-start(bf16[32,384]{1,0:T(8,128)(2,1)} %get-tuple-element.17), channel_id=1, source_target_pairs={{0,6},{1,7},{2,4},{3,5},{4,2},{5,3},{6,0},{7,1},{8,14},{9,15},{10,... | collective-permute-start | bytes 73736 | tf_op jit(solution)/shard_map/ppermute | solution.py:251
  30.9 0.8 %copy-start.7 = (f32[32,384]{1,0:T(8,128)S(1)}, f32[32,384]{1,0:T(8,128)}, u32[]{:S(2)}) copy-start(f32[32,384]{1,0:T(8,128)} %own_keys.1.refs_0_) | copy-start | bytes 147460
  31.7 0.7 %copy-start.9 = (bf16[32,384]{1,0:T(8,128)(2,1)S(1)}, bf16[32,384]{1,0:T(8,128)(2,1)}, u32[]{:S(2)}) copy-start(bf16[32,384]{1,0:T(8,128)(2,1)} %get-tuple-element.14.refs_1_) | copy-start | bytes 73732
  32.9 7.2 %copy-start.6 = (bf16[6,2,2048]{2,1,0:T(2,128)(2,1)}, bf16[6,2,2048]{2,1,0:T(2,128)(2,1)S(1)}, u32[]{:S(2)}) copy-start(bf16[6,2,2048]{2,1,0:T(2,128)(2,1)S(1)} %combine_project.1.refs_0_) | copy-start | bytes 147460
  32.9 5.5 %collective-permute-start.10 = (bf16[6,2,2048]{2,1,0:T(2,128)(2,1)S(1)}, bf16[6,2,2048]{2,1,0:T(2,128)(2,1)S(1)}, u32[]{:S(2)}, u32[]{:S(2)}) collective-permute-start(bf16[6,2,2048]{2,1,0:T(2,128)(2,1)S(1)} %combine_project.1.refs_0_), channel_id=1, source_target_pairs={{0,24},{8,16},{16,8},{24,0},{1,25},{9,17},{17,9},{25,1},{2,26},{10... | collective-permute-start | bytes 147464 | tf_op jit(solution)/shard_map/ppermute | solution.py:251
  35.5 4.1 %collective-permute-start.8 = (bf16[6,2,2048]{2,1,0:T(2,128)(2,1)S(1)}, bf16[6,2,2048]{2,1,0:T(2,128)(2,1)S(1)}, u32[]{:S(2)}, u32[]{:S(2)}) collective-permute-start(bf16[6,2,2048]{2,1,0:T(2,128)(2,1)S(1)} %combine_project.1.refs_0_), channel_id=1, source_target_pairs={{0,8},{8,0},{16,24},{24,16},{1,9},{9,1},{17,25},{25,17},{2,10},{10... | collective-permute-start | bytes 147464 | tf_op jit(solution)/shard_map/ppermute | solution.py:251
  36.0 4.1 %collective-permute-start.9 = (bf16[6,2,2048]{2,1,0:T(2,128)(2,1)S(1)}, bf16[6,2,2048]{2,1,0:T(2,128)(2,1)S(1)}, u32[]{:S(2)}, u32[]{:S(2)}) collective-permute-start(bf16[6,2,2048]{2,1,0:T(2,128)(2,1)S(1)} %combine_project.1.refs_0_), channel_id=1, source_target_pairs={{0,16},{8,24},{16,0},{24,8},{1,17},{9,25},{17,1},{25,9},{2,18},{10... | collective-permute-start | bytes 147464 | tf_op jit(solution)/shard_map/ppermute | solution.py:251
  38.5 1.6 %copy-start.11 = (bf16[6,2,2048]{2,1,0:T(2,128)(2,1)}, bf16[6,2,2048]{2,1,0:T(2,128)(2,1)S(1)}, u32[]{:S(2)}) copy-start(bf16[6,2,2048]{2,1,0:T(2,128)(2,1)S(1)} %collective-permute-done.10.refs_3_) | copy-start | bytes 147460
  39.5 0.6 %copy-start.12 = (bf16[6,2,2048]{2,1,0:T(2,128)(2,1)}, bf16[6,2,2048]{2,1,0:T(2,128)(2,1)S(1)}, u32[]{:S(2)}) copy-start(bf16[6,2,2048]{2,1,0:T(2,128)(2,1)S(1)} %collective-permute-done.8.refs_1_) | copy-start | bytes 147460
  40.1 0.6 %copy-start.13 = (bf16[6,2,2048]{2,1,0:T(2,128)(2,1)}, bf16[6,2,2048]{2,1,0:T(2,128)(2,1)S(1)}, u32[]{:S(2)}) copy-start(bf16[6,2,2048]{2,1,0:T(2,128)(2,1)S(1)} %collective-permute-done.9.refs_2_) | copy-start | bytes 147460

commit v2 on v1

--- a/solution.py
+++ b/solution.py
@@ -17,6 +17,14 @@
 
 def round_up(value, unit):
     return (value + unit - 1) // unit * unit
+
+
+def cost(flops, size):
+    return pl.CostEstimate(flops=flops, bytes_accessed=size, transcendentals=0)
+
+
+def vmem(mebibytes):
+    return pltpu.CompilerParams(vmem_limit_bytes=mebibytes * 1024 * 1024)
 
 
 def iota(shape, dim):
@@ -228,7 +236,7 @@
         square = jnp.sum(last * last, axis=1, keepdims=True) / width
         score = jnp.sum(last * mix, axis=1, keepdims=True) * lax.rsqrt(square + 1e-06)
         scores = jnp.where(lane == r, score, scores)
-    scores_ref[...] = scores
+    scores_ref[...] = scores[0, :reqs]
 
 
 def body(sizes, prefix_pool, slot_page, prompt_len, request_ids, tail_len, tail_cache, queries, new_kv, hidden,
@@ -265,6 +273,8 @@
         in_specs=[SMEM] * 3,
         out_specs=(VMEM,) * 3,
         scratch_shapes=[pltpu.SMEM(prompt_len.shape, jnp.int32)],
+        compiler_params=vmem(8),
+        cost_estimate=cost(1, 2 * blk * per * LANES * 4),
         name="key_ranges",
     )(request_ids, prompt_len, slot_page)
 
@@ -277,6 +287,8 @@
             pltpu.VMEM((per, head_size), jnp.bfloat16),
             pltpu.VMEM((2 * rows, head_size), jnp.bfloat16),
         ],
+        compiler_params=vmem(8),
+        cost_estimate=cost(4 * per * local * tail_cache.shape[2] * head_size, 2 * tail_cache.size),
         name="own_keys",
     )(tail_len, queries, tail_cache[0], new_kv[0])
 
@@ -298,12 +310,12 @@
             ],
             out_specs=pl.BlockSpec((step, per, head_size + LANES), lambda i: (i, 0, 0)),
             scratch_shapes=[pltpu.VMEM((step * per, head_size), jnp.bfloat16)],
-            compiler_params=pltpu.CompilerParams(vmem_limit_bytes=32 * 1024 * 1024),
+            compiler_params=vmem(16),
+            cost_estimate=cost(4 * slots * per * keys * head_size, 2 * pool.size),
             name="prefix_keys",
         )(block, low, high, key, pool)
 
     partial_shape = jax.ShapeDtypeStruct((local, drafts, width), jnp.bfloat16)
-    limit = pltpu.CompilerParams(vmem_limit_bytes=32 * 1024 * 1024)
     if paired:
         column = [queries] + [swap(queries, "blk", blk, 2 * j) for j in range(1, half)]
         mine = jnp.stack(column)
@@ -317,6 +329,8 @@
             out_shape=(block_shape,) * half,
             in_specs=[VMEM] * 2,
             out_specs=(VMEM,) * half,
+            compiler_params=vmem(8),
+            cost_estimate=cost(1, 6 * half * per * head_size),
             name="merge_cores",
         )(sums_mine, back)
         blocks = [merged[0]] + [swap(merged[j], "blk", blk, 2 * j) for j in range(1, half)]
@@ -325,7 +339,8 @@
             out_shape=partial_shape,
             in_specs=[VMEM] * (half + 2),
             out_specs=VMEM,
-            compiler_params=limit,
+            compiler_params=vmem(12),
+            cost_estimate=cost(2 * per * head_size * width, 2 * out_weight.size),
             name="combine_project",
         )(own, *blocks, out_weight)
     else:
@@ -336,7 +351,8 @@
             out_shape=partial_shape,
             in_specs=[VMEM] * 3,
             out_specs=VMEM,
-            compiler_params=limit,
+            compiler_params=vmem(12),
+            cost_estimate=cost(2 * per * head_size * width, 2 * out_weight.size),
             name="combine_project",
         )(own, blocks, out_weight)
     if kv in (2, 4):
@@ -347,13 +363,15 @@
         final_kernel,
         out_shape=(
             jax.ShapeDtypeStruct(hidden.shape, hidden.dtype),
-            jax.ShapeDtypeStruct((1, LANES), jnp.float32),
+            jax.ShapeDtypeStruct((local,), jnp.float32),
         ),
         in_specs=[VMEM] * (len(shares) + 3),
         out_specs=(VMEM, VMEM),
+        compiler_params=vmem(8),
+        cost_estimate=cost(1, 2 * hidden.size * 6),
         name="residual_scores",
     )(*shares, hidden, norm_gain.reshape(1, width), score_weight.reshape(1, width))
-    return hidden_out, scores[0, :local]
+    return hidden_out, scores
 
 
 def solution(mesh):

time: 44 us -> 35.4 us (0.80)
  Pallas kernels: 9.92 us -> 5.46 us
  local copies, waits for them, and re-layouts: 8.55 us -> 4.53 us
    unnamed x28 -> x26, local copies, waits for them, and re-layouts: 7.43 us -> 4.53 us
    pallas_call x1, Pallas kernels: 1.89 us -> 0.34 us  [body(): pl.pallas_call(functools.partial(merge_kernel, head_size), out_shape=(blo...]
    pallas_call x1, Pallas kernels: 2.31 us -> 1.08 us  [body(): pl.pallas_call(functools.partial(own_kernel, heads, rows, scale), out_sha...]
    squeeze x1 -> x0, local copies, waits for them, and re-layouts: 1.12 us -> none  [body(): return (hidden_out, scores[0, :local])]
    pallas_call x1, Pallas kernels: 1.69 us -> 0.77 us  [body(): pl.pallas_call(final_kernel, out_shape=(jax.ShapeDtypeStruct(hidden.shape...]
    pallas_call x1, Pallas kernels: 1.74 us -> 0.99 us  [body(): pl.pallas_call(functools.partial(layout_kernel, device_of, blk, local, ro...]
  transfers between devices with their start and end apart: 11 -> 11, of which waited for: 5 -> 5; matrix products, arithmetic and copies ran while one was open for 0% -> 0% of each run, Pallas kernels for 11% -> 8%
where the time goes in v2:
time: 35.4 us; the launch traced here: 35.2 us
  starting transfers between devices  14.3 us (40%)
  waiting for transfers between devices  9.31 us (26%)
  Pallas kernels  5.46 us (15%)
  local copies, waits for them, and re-layouts  4.53 us (13%)
  other arithmetic  0.79 us (2%)
  between operations  0.78 us (2%)
    ppermute x11, starting transfers between devices, swap(): return lax.ppermute(x, axis, [(i, i ^ mask) for i in range(size)])  14.3 us
    ppermute x11, waiting for transfers between devices, swap(): return lax.ppermute(x, axis, [(i, i ^ mask) for i in range(size)])  9.31 us
    unnamed x26, local copies, waits for them, and re-layouts  4.53 us
    pallas_call x2, Pallas kernels, prefix(): pl.pallas_call(functools.partial(prefix_kernel, heads, rows, scale), out_...  1.77 us
    pallas_call x1, Pallas kernels, body(): pl.pallas_call(functools.partial(own_kernel, heads, rows, scale), out_sha...  1.08 us
    pallas_call x1, Pallas kernels, body(): pl.pallas_call(functools.partial(layout_kernel, device_of, blk, local, ro...  0.99 us
    another operation x1, other arithmetic, body(): mine = jnp.stack(column)  0.79 us
    pallas_call x1, Pallas kernels, body(): pl.pallas_call(final_kernel, out_shape=(jax.ShapeDtypeStruct(hidden.shape...  0.77 us
  transfers between devices with their start and end apart: 11, of which 5 were waited for; matrix products, arithmetic and copies ran while one was open for 0% of the time, Pallas kernels for 8%

profile of v2, /device:TPU:0, one launch (start us, length us, event | category | flops | bytes accessed | tf_op | source)
XLA Modules:
  0.0 35.2 jit_solution(4773587852572469919)
XLA Ops:
  0.6 3.1 %collective-permute-start = (bf16[6,2,512]{2,1,0:T(2,128)(2,1)}, bf16[6,2,512]{2,1,0:T(2,128)(2,1)S(1)}, u32[]{:S(2)}, u32[]{:S(2)}) collective-permute-start(bf16[6,2,512]{2,1,0:T(2,128)(2,1)} %q_ref.1), channel_id=1, source_target_pairs={{0,2},{1,3},{2,0},{3,1},{4,6},{5,7},{6,4},{7,5},{8,10},{9,11},{10,... | collective-permute-start | bytes 36872 | tf_op jit(solution)/shard_map/ppermute | solution.py:259
  3.7 2.6 %collective-permute-start.1 = (bf16[6,2,512]{2,1,0:T(2,128)(2,1)}, bf16[6,2,512]{2,1,0:T(2,128)(2,1)S(1)}, u32[]{:S(2)}, u32[]{:S(2)}) collective-permute-start(bf16[6,2,512]{2,1,0:T(2,128)(2,1)} %q_ref.1), channel_id=1, source_target_pairs={{0,4},{1,5},{2,6},{3,7},{4,0},{5,1},{6,2},{7,3},{8,12},{9,13},{10,... | collective-permute-start | bytes 36872 | tf_op jit(solution)/shard_map/ppermute | solution.py:259
  6.3 0.0 collective-permute-start.2
  6.3 0.0 collective-permute-done
  6.3 2.2 %collective-permute-done.1 = bf16[6,2,512]{2,1,0:T(2,128)(2,1)S(1)} collective-permute-done((bf16[6,2,512]{2,1,0:T(2,128)(2,1)}, bf16[6,2,512]{2,1,0:T(2,128)(2,1)S(1)}, u32[]{:S(2)}, u32[]{:S(2)}) %collective-permute-start.1) | collective-permute-done | bytes 12320 | tf_op jit(solution)/shard_map/ppermute | solution.py:259
  8.5 3.5 %collective-permute-done.2 = bf16[6,2,512]{2,1,0:T(2,128)(2,1)S(1)} collective-permute-done((bf16[6,2,512]{2,1,0:T(2,128)(2,1)}, bf16[6,2,512]{2,1,0:T(2,128)(2,1)S(1)}, u32[]{:S(2)}, u32[]{:S(2)}) %collective-permute-start.2) | collective-permute-done | bytes 12320 | tf_op jit(solution)/shard_map/ppermute | solution.py:259
  12.0 0.8 %pad_maximum_fusion.q_ref = bf16[4,6,2,512]{3,2,1,0:T(2,128)(2,1)S(1)} fusion(bf16[1,6,2,512]{3,2,1,0:T(2,128)(2,1)S(1)} %bitcast.18, bf16[1,6,2,512]{3,2,1,0:T(2,128)(2,1)S(1)} %bitcast.17, bf16[1,6,2,512]{3,2,1,0:T(2,128)(2,1)S(1)} %bitcast.16, bf16[1,6,2,512]{3,2,1,0:T(2,128)(2,1)} %bitcast.12), kind=kLoop, calls=%fused_computation | loop fusion | flops 73728 | bytes 98304 | tf_op jit(solution)/shard_map/stack | solution.py:321
  12.8 0.1 collective-permute-start.3
  12.9 0.0 copy-start.10
  12.9 0.6 %copy-done.10 = s32[48]{0:T(128)S(1)} copy-done((s32[48]{0:T(128)S(1)}, s32[48]{0:T(128)}, u32[]{:S(2)}) %copy-start.10) | copy-done | bytes 216
  13.5 0.0 copy-start.11
  13.5 0.7 %copy-done.11 = s32[3]{0:T(128)S(1)} copy-done((s32[3]{0:T(128)S(1)}, s32[3]{0:T(128)}, u32[]{:S(2)}) %copy-start.11) | copy-done | bytes 36
  14.2 0.0 copy-start.12
  14.2 0.7 %copy-done.12 = s32[24]{0:T(128)S(1)} copy-done((s32[24]{0:T(128)S(1)}, s32[24]{0:T(128)}, u32[]{:S(2)}) %copy-start.12) | copy-done | bytes 120
  14.9 1.0 %key_ranges.1 = (s32[256,128]{1,0:T(8,128)S(1)}, s32[256,128]{1,0:T(8,128)S(1)}, s32[8,1536]{1,0:T(8,128)S(1)}) custom-call(s32[48]{0:T(128)S(1)} %copy-done.10, s32[3]{0:T(128)S(1)} %copy-done.11, s32[24]{0:T(128)S(1)} %copy-done.12), custom_call_target="tpu_custom_call" | custom-call | flops 1 | bytes 262144 | tf_op jit(solution)/shard_map/key_ranges/pallas_call | solution.py:266
  15.8 0.0 collective-permute-done.3.q_ref
  15.8 0.0 copy-start
  15.9 1.4 %copy-done = bf16[1,24,64,512]{3,2,1,0:T(8,128)(2,1)S(1)} copy-done((bf16[1,24,64,512]{3,2,1,0:T(8,128)(2,1)S(1)}, bf16[1,24,64,512]{3,2,1,0:T(8,128)(2,1)}, u32[]{:S(2)}) %copy-start) | copy-done | bytes 1572888
  17.3 0.0 copy-start.1
  17.3 0.0 copy-start.5
  17.3 0.0 copy-start.6
  17.3 0.0 copy-start.9
  17.3 0.0 copy-start.2
  17.3 0.9 %prefix_keys.3 = bf16[4,32,384]{2,1,0:T(8,128)(2,1)S(1)} custom-call(bf16[4,6,2,512]{3,2,1,0:T(2,128)(2,1)S(1)} %collective-permute-done.3.q_ref, s32[256,128]{1,0:T(8,128)S(1)} %get-tuple-element.9.low_ref, s32[256,128]{1,0:T(8,128)S(1)} %get-tuple-element.10.high_ref, s32[8,1536]{1,0:T(8,128)S(1)} %get-tuple-element.11.key_ref, ...), custom_call_target="tpu_custom_call" | custom-call | flops 201326592 | bytes 1572864 | tf_op jit(solution)/shard_map/prefix_keys/pallas_call | solution.py:300
  18.2 0.6 %collective-permute-start.4 = (bf16[4,32,384]{2,1,0:T(8,128)(2,1)S(1)}, bf16[4,32,384]{2,1,0:T(8,128)(2,1)S(1)}, u32[]{:S(2)}, u32[]{:S(2)}) collective-permute-start(bf16[4,32,384]{2,1,0:T(8,128)(2,1)S(1)} %prefix_keys.3), channel_id=1, source_target_pairs={{0,1},{1,0},{2,3},{3,2},{4,5},{5,4},{6,7},{7,6},{8,9},{9,8},{10,11... | collective-permute-start | bytes 294920 | tf_op jit(solution)/shard_map/ppermute | solution.py:259
  18.7 0.0 copy-done.1
  18.7 0.9 %prefix_keys.2.a_ref = bf16[4,32,384]{2,1,0:T(8,128)(2,1)S(1)} custom-call(bf16[4,6,2,512]{3,2,1,0:T(2,128)(2,1)S(1)} %pad_maximum_fusion.q_ref, s32[256,128]{1,0:T(8,128)S(1)} %get-tuple-element.9.low_ref, s32[256,128]{1,0:T(8,128)S(1)} %get-tuple-element.10.high_ref, s32[8,1536]{1,0:T(8,128)S(1)} %get-tuple-element.11.key_ref, ...), custom_call_target="tpu_custom_call" | custom-call | flops 201326592 | bytes 1572864 | tf_op jit(solution)/shard_map/prefix_keys/pallas_call | solution.py:300
  19.6 0.0 copy-start.4
  19.6 0.0 copy-start.7
  19.6 0.0 copy-start.8
  19.7 0.0 collective-permute-done.4.b_ref
  19.7 0.3 merge_cores.1
  20.0 0.1 collective-permute-start.5
  20.1 0.7 %collective-permute-start.6 = (bf16[32,384]{1,0:T(8,128)(2,1)S(1)}, bf16[32,384]{1,0:T(8,128)(2,1)S(1)}, u32[]{:S(2)}, u32[]{:S(2)}) collective-permute-start(bf16[32,384]{1,0:T(8,128)(2,1)S(1)} %get-tuple-element.14), channel_id=1, source_target_pairs={{0,4},{1,5},{2,6},{3,7},{4,0},{5,1},{6,2},{7,3},{8,12},{9,13},{10,... | collective-permute-start | bytes 73736 | tf_op jit(solution)/shard_map/ppermute | solution.py:259
  20.8 3.7 %collective-permute-start.7 = (bf16[32,384]{1,0:T(8,128)(2,1)S(1)}, bf16[32,384]{1,0:T(8,128)(2,1)S(1)}, u32[]{:S(2)}, u32[]{:S(2)}) collective-permute-start(bf16[32,384]{1,0:T(8,128)(2,1)S(1)} %get-tuple-element.15), channel_id=1, source_target_pairs={{0,6},{1,7},{2,4},{3,5},{4,2},{5,3},{6,0},{7,1},{8,14},{9,15},{10,... | collective-permute-start | bytes 73736 | tf_op jit(solution)/shard_map/ppermute | solution.py:259
  24.5 0.0 copy-done.5
  24.5 0.0 copy-done.6
  24.5 0.0 copy-done.9
  24.5 0.0 copy-start.3
  24.5 1.1 %copy-done.3 = bf16[1,6,128,512]{3,2,1,0:T(8,128)(2,1)S(1)} copy-done((bf16[1,6,128,512]{3,2,1,0:T(8,128)(2,1)S(1)}, bf16[1,6,128,512]{3,2,1,0:T(8,128)(2,1)}, u32[]{:S(2)}) %copy-start.3) | copy-done | bytes 786456
  25.6 1.1 %own_keys.1.refs_0_ = f32[32,384]{1,0:T(8,128)S(1)} custom-call(s32[6]{0:T(128)S(1)} %copy-done.9, bf16[6,2,512]{2,1,0:T(2,128)(2,1)S(1)} %copy-done.5, bf16[6,128,512]{2,1,0:T(8,128)(2,1)S(1)} %bitcast.11, bf16[6,2,512]{2,1,0:T(2,128)(2,1)S(1)} %bitcast.13), custom_call_target="tpu_custom_call" | custom-call | flops 25165824 | bytes 786432 | tf_op jit(solution)/shard_map/own_keys/pallas_call | solution.py:281
  26.7 0.0 collective-permute-done.5.refs_2_
  26.7 0.0 collective-permute-done.6.refs_3_
  26.7 0.0 collective-permute-done.7.refs_4_
  26.7 0.0 copy-done.2
  26.7 0.5 %combine_project.1.refs_0_ = bf16[6,2,2048]{2,1,0:T(2,128)(2,1)S(1)} custom-call(f32[32,384]{1,0:T(8,128)S(1)} %own_keys.1.refs_0_, bf16[32,384]{1,0:T(8,128)(2,1)S(1)} %get-tuple-element.12.refs_1_, bf16[32,384]{1,0:T(8,128)(2,1)S(1)} %collective-permute-done.5.refs_2_, bf16[32,384]{1,0:T(8,128)(2,1)S(1)} %collective-permute-done.6.refs_3_, ...), custom_call_target="tpu_custom_call" | custom-call | flops 33554432 | bytes 2097152 | tf_op jit(solution)/shard_map/combine_project/pallas_call | solution.py:337
  27.3 2.5 %collective-permute-start.10 = (bf16[6,2,2048]{2,1,0:T(2,128)(2,1)S(1)}, bf16[6,2,2048]{2,1,0:T(2,128)(2,1)S(1)}, u32[]{:S(2)}, u32[]{:S(2)}) collective-permute-start(bf16[6,2,2048]{2,1,0:T(2,128)(2,1)S(1)} %combine_project.1.refs_0_), channel_id=1, source_target_pairs={{0,24},{8,16},{16,8},{24,0},{1,25},{9,17},{17,9},{25,1},{2,26},{10... | collective-permute-start | bytes 147464 | tf_op jit(solution)/shard_map/ppermute | solution.py:259
  29.8 0.5 %collective-permute-start.8 = (bf16[6,2,2048]{2,1,0:T(2,128)(2,1)S(1)}, bf16[6,2,2048]{2,1,0:T(2,128)(2,1)S(1)}, u32[]{:S(2)}, u32[]{:S(2)}) collective-permute-start(bf16[6,2,2048]{2,1,0:T(2,128)(2,1)S(1)} %combine_project.1.refs_0_), channel_id=1, source_target_pairs={{0,8},{8,0},{16,24},{24,16},{1,9},{9,1},{17,25},{25,17},{2,10},{10... | collective-permute-start | bytes 147464 | tf_op jit(solution)/shard_map/ppermute | solution.py:259
  30.3 0.5 %collective-permute-start.9 = (bf16[6,2,2048]{2,1,0:T(2,128)(2,1)S(1)}, bf16[6,2,2048]{2,1,0:T(2,128)(2,1)S(1)}, u32[]{:S(2)}, u32[]{:S(2)}) collective-permute-start(bf16[6,2,2048]{2,1,0:T(2,128)(2,1)S(1)} %combine_project.1.refs_0_), channel_id=1, source_target_pairs={{0,16},{8,24},{16,0},{24,8},{1,17},{9,25},{17,1},{25,9},{2,18},{10... | collective-permute-start | bytes 147464 | tf_op jit(solution)/shard_map/ppermute | solution.py:259
  30.8 2.0 %collective-permute-done.10.refs_3_ = bf16[6,2,2048]{2,1,0:T(2,128)(2,1)S(1)} collective-permute-done((bf16[6,2,2048]{2,1,0:T(2,128)(2,1)S(1)}, bf16[6,2,2048]{2,1,0:T(2,128)(2,1)S(1)}, u32[]{:S(2)}, u32[]{:S(2)}) %collective-permute-start.10) | collective-permute-done | bytes 49184 | tf_op jit(solution)/shard_map/ppermute | solution.py:259
  32.8 1.1 %collective-permute-done.8.refs_1_ = bf16[6,2,2048]{2,1,0:T(2,128)(2,1)S(1)} collective-permute-done((bf16[6,2,2048]{2,1,0:T(2,128)(2,1)S(1)}, bf16[6,2,2048]{2,1,0:T(2,128)(2,1)S(1)}, u32[]{:S(2)}, u32[]{:S(2)}) %collective-permute-start.8) | collective-permute-done | bytes 49184 | tf_op jit(solution)/shard_map/ppermute | solution.py:259
  33.9 0.5 %collective-permute-done.9.refs_2_ = bf16[6,2,2048]{2,1,0:T(2,128)(2,1)S(1)} collective-permute-done((bf16[6,2,2048]{2,1,0:T(2,128)(2,1)S(1)}, bf16[6,2,2048]{2,1,0:T(2,128)(2,1)S(1)}, u32[]{:S(2)}, u32[]{:S(2)}) %collective-permute-start.9) | collective-permute-done | bytes 49184 | tf_op jit(solution)/shard_map/ppermute | solution.py:259
  34.4 0.0 copy-done.4
  34.4 0.0 copy-done.7
  34.4 0.0 copy-done.8
  34.4 0.8 %residual_scores.1 = (bf16[6,2,2048]{2,1,0:T(2,128)(2,1)}, f32[6]{0:T(128)}) custom-call(bf16[6,2,2048]{2,1,0:T(2,128)(2,1)S(1)} %combine_project.1.refs_0_, bf16[6,2,2048]{2,1,0:T(2,128)(2,1)S(1)} %collective-permute-done.8.refs_1_, bf16[6,2,2048]{2,1,0:T(2,128)(2,1)S(1)} %collective-permute-done.9.refs_2_, ...), custom_call_target="tpu_custom_call" | custom-call | flops 1 | bytes 294912 | tf_op jit(solution)/shard_map/residual_scores/pallas_call | solution.py:362
Async XLA Ops:
  0.6 5.7 %collective-permute-start = (bf16[6,2,512]{2,1,0:T(2,128)(2,1)}, bf16[6,2,512]{2,1,0:T(2,128)(2,1)S(1)}, u32[]{:S(2)}, u32[]{:S(2)}) collective-permute-start(bf16[6,2,512]{2,1,0:T(2,128)(2,1)} %q_ref.1), channel_id=1, source_target_pairs={{0,2},{1,3},{2,0},{3,1},{4,6},{5,7},{6,4},{7,5},{8,10},{9,11},{10,... | collective-permute-start | bytes 36872 | tf_op jit(solution)/shard_map/ppermute | solution.py:259
  3.7 4.8 %collective-permute-start.1 = (bf16[6,2,512]{2,1,0:T(2,128)(2,1)}, bf16[6,2,512]{2,1,0:T(2,128)(2,1)S(1)}, u32[]{:S(2)}, u32[]{:S(2)}) collective-permute-start(bf16[6,2,512]{2,1,0:T(2,128)(2,1)} %q_ref.1), channel_id=1, source_target_pairs={{0,4},{1,5},{2,6},{3,7},{4,0},{5,1},{6,2},{7,3},{8,12},{9,13},{10,... | collective-permute-start | bytes 36872 | tf_op jit(solution)/shard_map/ppermute | solution.py:259
  6.3 5.7 %collective-permute-start.2 = (bf16[6,2,512]{2,1,0:T(2,128)(2,1)}, bf16[6,2,512]{2,1,0:T(2,128)(2,1)S(1)}, u32[]{:S(2)}, u32[]{:S(2)}) collective-permute-start(bf16[6,2,512]{2,1,0:T(2,128)(2,1)} %q_ref.1), channel_id=1, source_target_pairs={{0,6},{1,7},{2,4},{3,5},{4,2},{5,3},{6,0},{7,1},{8,14},{9,15},{10,... | collective-permute-start | bytes 36872 | tf_op jit(solution)/shard_map/ppermute | solution.py:259
  12.8 3.0 %collective-permute-start.3 = (bf16[4,6,2,512]{3,2,1,0:T(2,128)(2,1)S(1)}, bf16[4,6,2,512]{3,2,1,0:T(2,128)(2,1)S(1)}, u32[]{:S(2)}, u32[]{:S(2)}) collective-permute-start(bf16[4,6,2,512]{3,2,1,0:T(2,128)(2,1)S(1)} %pad_maximum_fusion.q_ref), channel_id=1, source_target_pairs={{0,1},{1,0},{2,3},{3,2},{4,5},{5,4},{6,7},{7,6},{8,9},{9,8},{10,11... | collective-permute-start | bytes 147464 | tf_op jit(solution)/shard_map/ppermute | solution.py:259
  12.9 0.7 %copy-start.10 = (s32[48]{0:T(128)S(1)}, s32[48]{0:T(128)}, u32[]{:S(2)}) copy-start(s32[48]{0:T(128)} %ids_ref.1) | copy-start | bytes 580
  13.5 0.7 %copy-start.11 = (s32[3]{0:T(128)S(1)}, s32[3]{0:T(128)}, u32[]{:S(2)}) copy-start(s32[3]{0:T(128)} %len_ref.3) | copy-start | bytes 40
  14.2 0.7 %copy-start.12 = (s32[24]{0:T(128)S(1)}, s32[24]{0:T(128)}, u32[]{:S(2)}) copy-start(s32[24]{0:T(128)} %page_ref.1) | copy-start | bytes 292
  15.8 1.4 %copy-start = (bf16[1,24,64,512]{3,2,1,0:T(8,128)(2,1)S(1)}, bf16[1,24,64,512]{3,2,1,0:T(8,128)(2,1)}, u32[]{:S(2)}) copy-start(bf16[1,24,64,512]{3,2,1,0:T(8,128)(2,1)} %param.12) | copy-start | bytes 4718596
  17.3 1.5 %copy-start.1 = (bf16[1,24,64,512]{3,2,1,0:T(8,128)(2,1)S(1)}, bf16[1,24,64,512]{3,2,1,0:T(8,128)(2,1)}, u32[]{:S(2)}) copy-start(bf16[1,24,64,512]{3,2,1,0:T(8,128)(2,1)} %param.12) | copy-start | bytes 4718596
  17.3 7.2 %copy-start.5 = (bf16[6,2,512]{2,1,0:T(2,128)(2,1)S(1)}, bf16[6,2,512]{2,1,0:T(2,128)(2,1)}, u32[]{:S(2)}) copy-start(bf16[6,2,512]{2,1,0:T(2,128)(2,1)} %q_ref.1) | copy-start | bytes 36868
  17.3 7.2 %copy-start.6 = (bf16[1,6,2,512]{3,2,1,0:T(2,128)(2,1)S(1)}, bf16[1,6,2,512]{3,2,1,0:T(2,128)(2,1)}, u32[]{:S(2)}) copy-start(bf16[1,6,2,512]{3,2,1,0:T(2,128)(2,1)} %param.19) | copy-start | bytes 36868
  17.3 7.2 %copy-start.9 = (s32[6]{0:T(128)S(1)}, s32[6]{0:T(128)}, u32[]{:S(2)}) copy-start(s32[6]{0:T(128)} %len_ref.2) | copy-start | bytes 76
  17.3 9.5 %copy-start.2 = (bf16[512,2048]{1,0:T(8,128)(2,1)S(1)}, bf16[512,2048]{1,0:T(8,128)(2,1)}, u32[]{:S(2)}) copy-start(bf16[512,2048]{1,0:T(8,128)(2,1)} %refs_5_.1) | copy-start | bytes 6291460
  18.2 1.5 %collective-permute-start.4 = (bf16[4,32,384]{2,1,0:T(8,128)(2,1)S(1)}, bf16[4,32,384]{2,1,0:T(8,128)(2,1)S(1)}, u32[]{:S(2)}, u32[]{:S(2)}) collective-permute-start(bf16[4,32,384]{2,1,0:T(8,128)(2,1)S(1)} %prefix_keys.3), channel_id=1, source_target_pairs={{0,1},{1,0},{2,3},{3,2},{4,5},{5,4},{6,7},{7,6},{8,9},{9,8},{10,11... | collective-permute-start | bytes 294920 | tf_op jit(solution)/shard_map/ppermute | solution.py:259
  19.6 14.8 %copy-start.4 = (bf16[6,2,2048]{2,1,0:T(2,128)(2,1)S(1)}, bf16[6,2,2048]{2,1,0:T(2,128)(2,1)}, u32[]{:S(2)}) copy-start(bf16[6,2,2048]{2,1,0:T(2,128)(2,1)} %refs_4_.1) | copy-start | bytes 147460
  19.6 14.8 %copy-start.7 = (f32[2048]{0:T(1024)S(1)}, f32[2048]{0:T(1024)}, u32[]{:S(2)}) copy-start(f32[2048]{0:T(1024)} %param.22) | copy-start | bytes 24580
  19.6 14.7 %copy-start.8 = (f32[2048]{0:T(1024)S(1)}, f32[2048]{0:T(1024)}, u32[]{:S(2)}) copy-start(f32[2048]{0:T(1024)} %param.23) | copy-start | bytes 24580
  20.0 6.7 %collective-permute-start.5 = (bf16[32,384]{1,0:T(8,128)(2,1)S(1)}, bf16[32,384]{1,0:T(8,128)(2,1)S(1)}, u32[]{:S(2)}, u32[]{:S(2)}) collective-permute-start(bf16[32,384]{1,0:T(8,128)(2,1)S(1)} %get-tuple-element.13), channel_id=1, source_target_pairs={{0,2},{1,3},{2,0},{3,1},{4,6},{5,7},{6,4},{7,5},{8,10},{9,11},{10,... | collective-permute-start | bytes 73736 | tf_op jit(solution)/shard_map/ppermute | solution.py:259
  20.1 6.6 %collective-permute-start.6 = (bf16[32,384]{1,0:T(8,128)(2,1)S(1)}, bf16[32,384]{1,0:T(8,128)(2,1)S(1)}, u32[]{:S(2)}, u32[]{:S(2)}) collective-permute-start(bf16[32,384]{1,0:T(8,128)(2,1)S(1)} %get-tuple-element.14), channel_id=1, source_target_pairs={{0,4},{1,5},{2,6},{3,7},{4,0},{5,1},{6,2},{7,3},{8,12},{9,13},{10,... | collective-permute-start | bytes 73736 | tf_op jit(solution)/shard_map/ppermute | solution.py:259
  20.8 5.9 %collective-permute-start.7 = (bf16[32,384]{1,0:T(8,128)(2,1)S(1)}, bf16[32,384]{1,0:T(8,128)(2,1)S(1)}, u32[]{:S(2)}, u32[]{:S(2)}) collective-permute-start(bf16[32,384]{1,0:T(8,128)(2,1)S(1)} %get-tuple-element.15), channel_id=1, source_target_pairs={{0,6},{1,7},{2,4},{3,5},{4,2},{5,3},{6,0},{7,1},{8,14},{9,15},{10,... | collective-permute-start | bytes 73736 | tf_op jit(solution)/shard_map/ppermute | solution.py:259
  24.5 1.1 %copy-start.3 = (bf16[1,6,128,512]{3,2,1,0:T(8,128)(2,1)S(1)}, bf16[1,6,128,512]{3,2,1,0:T(8,128)(2,1)}, u32[]{:S(2)}) copy-start(bf16[1,6,128,512]{3,2,1,0:T(8,128)(2,1)} %param.17) | copy-start | bytes 2359300
  27.3 5.5 %collective-permute-start.10 = (bf16[6,2,2048]{2,1,0:T(2,128)(2,1)S(1)}, bf16[6,2,2048]{2,1,0:T(2,128)(2,1)S(1)}, u32[]{:S(2)}, u32[]{:S(2)}) collective-permute-start(bf16[6,2,2048]{2,1,0:T(2,128)(2,1)S(1)} %combine_project.1.refs_0_), channel_id=1, source_target_pairs={{0,24},{8,16},{16,8},{24,0},{1,25},{9,17},{17,9},{25,1},{2,26},{10... | collective-permute-start | bytes 147464 | tf_op jit(solution)/shard_map/ppermute | solution.py:259
  29.8 4.1 %collective-permute-start.8 = (bf16[6,2,2048]{2,1,0:T(2,128)(2,1)S(1)}, bf16[6,2,2048]{2,1,0:T(2,128)(2,1)S(1)}, u32[]{:S(2)}, u32[]{:S(2)}) collective-permute-start(bf16[6,2,2048]{2,1,0:T(2,128)(2,1)S(1)} %combine_project.1.refs_0_), channel_id=1, source_target_pairs={{0,8},{8,0},{16,24},{24,16},{1,9},{9,1},{17,25},{25,17},{2,10},{10... | collective-permute-start | bytes 147464 | tf_op jit(solution)/shard_map/ppermute | solution.py:259
  30.3 4.1 %collective-permute-start.9 = (bf16[6,2,2048]{2,1,0:T(2,128)(2,1)S(1)}, bf16[6,2,2048]{2,1,0:T(2,128)(2,1)S(1)}, u32[]{:S(2)}, u32[]{:S(2)}) collective-permute-start(bf16[6,2,2048]{2,1,0:T(2,128)(2,1)S(1)} %combine_project.1.refs_0_), channel_id=1, source_target_pairs={{0,16},{8,24},{16,0},{24,8},{1,17},{9,25},{17,1},{25,9},{2,18},{10... | collective-permute-start | bytes 147464 | tf_op jit(solution)/shard_map/ppermute | solution.py:259

commit v3 on v2

--- a/solution.py
+++ b/solution.py
@@ -11,6 +11,7 @@
 LANES = 128
 FLOOR = -(2.0**100)
 LOG2E = 1.4426950408889634
+ANY = pl.BlockSpec(memory_space=pl.ANY)
 VMEM = pl.BlockSpec(memory_space=pltpu.VMEM)
 SMEM = pl.BlockSpec(memory_space=pltpu.SMEM)
 
@@ -65,7 +66,14 @@
 
 
 def layout_kernel(device_of, slots, local, rows, heads, drafts, page_tokens,
-                  ids_ref, len_ref, page_ref, low_ref, high_ref, key_ref, start_ref):
+                  ids_ref, len_ref, page_ref, q_ref, pool_ref,
+                  low_ref, high_ref, key_ref, q_out_ref, pool_out_ref, start_ref, sems):
+    copies = [
+        pltpu.make_async_copy(q_ref, q_out_ref, sems.at[0]),
+        pltpu.make_async_copy(pool_ref, pool_out_ref, sems.at[1]),
+    ]
+    for copy in copies:
+        copy.start()
     me = lax.axis_index("blk")
     prompts = len_ref.shape[0]
 
@@ -95,6 +103,8 @@
     lane = iota((8, page_tokens), 1)
     for s in range(page_ref.shape[0]):
         key_ref[:, pl.ds(s * page_tokens, page_tokens)] = lane + page_ref[s] * page_tokens
+    for copy in copies:
+        copy.wait()
 
 
 def prefix_kernel(heads, rows, scale, q_ref, low_ref, high_ref, key_ref, pool_ref, *rest):
@@ -263,20 +273,23 @@
             return j
         return me ^ (j * 2) if isinstance(j, int) and j < half else me ^ (j % half * 2 + j // half)
 
-    low, high, key = pl.pallas_call(
+    in_hbm = functools.partial(pltpu.with_memory_space_constraint, memory_space=pltpu.HBM)
+    low, high, key, near_queries, pool = pl.pallas_call(
         functools.partial(layout_kernel, device_of, blk, local, rows, heads, drafts, page_tokens),
         out_shape=(
             jax.ShapeDtypeStruct((blk * per, LANES), jnp.int32),
             jax.ShapeDtypeStruct((blk * per, LANES), jnp.int32),
             jax.ShapeDtypeStruct((8, keys), jnp.int32),
+            jax.ShapeDtypeStruct(queries.shape, queries.dtype),
+            jax.ShapeDtypeStruct(pool.shape, pool.dtype),
         ),
-        in_specs=[SMEM] * 3,
-        out_specs=(VMEM,) * 3,
-        scratch_shapes=[pltpu.SMEM(prompt_len.shape, jnp.int32)],
+        in_specs=[SMEM] * 3 + [ANY] * 2,
+        out_specs=(VMEM,) * 3 + (ANY,) * 2,
+        scratch_shapes=[pltpu.SMEM(prompt_len.shape, jnp.int32), pltpu.SemaphoreType.DMA((2,))],
         compiler_params=vmem(8),
         cost_estimate=cost(1, 2 * blk * per * LANES * 4),
         name="key_ranges",
-    )(request_ids, prompt_len, slot_page)
+    )(*map(in_hbm, (request_ids, prompt_len, slot_page, queries, pool)))
 
     own = pl.pallas_call(
         functools.partial(own_kernel, heads, rows, scale),
@@ -317,7 +330,7 @@
 
     partial_shape = jax.ShapeDtypeStruct((local, drafts, width), jnp.bfloat16)
     if paired:
-        column = [queries] + [swap(queries, "blk", blk, 2 * j) for j in range(1, half)]
+        column = [near_queries] + [swap(queries, "blk", blk, 2 * j) for j in range(1, half)]
         mine = jnp.stack(column)
         theirs = swap(mine, "blk", blk, 1)
         sums_mine = prefix(mine, 0)

time: 35.4 us -> 31.3 us (0.88)
  local copies, waits for them, and re-layouts: 4.53 us -> 0.05 us
  Pallas kernels: 5.46 us -> 6.6 us
  other arithmetic: 0.79 us -> 0.08 us
    unnamed x26 -> x16, local copies, waits for them, and re-layouts: 4.53 us -> 0.05 us
    pallas_call x1, Pallas kernels: 0.99 us -> 2.12 us  [body(): pl.pallas_call(functools.partial(layout_kernel, device_of, blk, local, ro...]
    another operation x1, other arithmetic: 0.79 us -> 0.08 us  [body(): mine = jnp.stack(column)]
  transfers between devices with their start and end apart: 11 -> 11, of which waited for: 5 -> 8; matrix products, arithmetic and copies ran while one was open for 0% -> 0% of each run, Pallas kernels for 8% -> 13%
where the time goes in v3:
time: 31.3 us; the launch traced here: 31 us
  starting transfers between devices  14 us (45%)
  waiting for transfers between devices  9.55 us (31%)
  Pallas kernels  6.6 us (21%)
  between operations  0.78 us (2%)
    ppermute x11, starting transfers between devices, swap(): return lax.ppermute(x, axis, [(i, i ^ mask) for i in range(size)])  14 us
    ppermute x11, waiting for transfers between devices, swap(): return lax.ppermute(x, axis, [(i, i ^ mask) for i in range(size)])  9.55 us
    pallas_call x1, Pallas kernels, body(): pl.pallas_call(functools.partial(layout_kernel, device_of, blk, local, ro...  2.12 us
    pallas_call x2, Pallas kernels, prefix(): pl.pallas_call(functools.partial(prefix_kernel, heads, rows, scale), out_...  1.77 us
    pallas_call x1, Pallas kernels, body(): pl.pallas_call(functools.partial(own_kernel, heads, rows, scale), out_sha...  1.08 us
    pallas_call x1, Pallas kernels, body(): pl.pallas_call(final_kernel, out_shape=(jax.ShapeDtypeStruct(hidden.shape...  0.77 us
  transfers between devices with their start and end apart: 11, of which 8 were waited for; matrix products, arithmetic and copies ran while one was open for 0% of the time, Pallas kernels for 13%

profile of v3, /device:TPU:0, one launch (start us, length us, event | category | flops | bytes accessed | tf_op | source)
XLA Modules:
  0.0 31.0 jit_solution(1614312795613205892)
XLA Ops:
  0.6 3.1 %collective-permute-start = (bf16[6,2,512]{2,1,0:T(2,128)(2,1)}, bf16[6,2,512]{2,1,0:T(2,128)(2,1)S(1)}, u32[]{:S(2)}, u32[]{:S(2)}) collective-permute-start(bf16[6,2,512]{2,1,0:T(2,128)(2,1)} %q_ref.3), channel_id=1, source_target_pairs={{0,2},{1,3},{2,0},{3,1},{4,6},{5,7},{6,4},{7,5},{8,10},{9,11},{10,... | collective-permute-start | bytes 36872 | tf_op jit(solution)/shard_map/ppermute | solution.py:269
  3.7 2.6 %collective-permute-start.1 = (bf16[6,2,512]{2,1,0:T(2,128)(2,1)}, bf16[6,2,512]{2,1,0:T(2,128)(2,1)S(1)}, u32[]{:S(2)}, u32[]{:S(2)}) collective-permute-start(bf16[6,2,512]{2,1,0:T(2,128)(2,1)} %q_ref.3), channel_id=1, source_target_pairs={{0,4},{1,5},{2,6},{3,7},{4,0},{5,1},{6,2},{7,3},{8,12},{9,13},{10,... | collective-permute-start | bytes 36872 | tf_op jit(solution)/shard_map/ppermute | solution.py:269
  6.3 0.0 collective-permute-start.2
  6.3 2.1 %key_ranges.1 = (s32[256,128]{1,0:T(8,128)S(1)}, s32[256,128]{1,0:T(8,128)S(1)}, s32[8,1536]{1,0:T(8,128)S(1)}, bf16[6,2,512]{2,1,0:T(2,128)(2,1)S(1)}, bf16[24,64,512]{2,1,0:T(8,128)(2,1)S(1)}) custom-call(s32[48]{0:T(128)} %ids_ref.1, s32[3]{0:T(128)} %len_ref.3, s32[24]{0:T(128)} %page_ref.1, bf16[6,2,512]{2,1,0:T(2,128)(2,1)} %q_ref.3, ...), custom_call_target="tpu_custom_call" | custom-call | flops 1 | bytes 262144 | tf_op jit(solution)/shard_map/key_ranges/pallas_call | solution.py:277
  8.4 0.0 collective-permute-done
  8.5 0.1 collective-permute-done.1
  8.5 3.5 %collective-permute-done.2 = bf16[6,2,512]{2,1,0:T(2,128)(2,1)S(1)} collective-permute-done((bf16[6,2,512]{2,1,0:T(2,128)(2,1)}, bf16[6,2,512]{2,1,0:T(2,128)(2,1)S(1)}, u32[]{:S(2)}, u32[]{:S(2)}) %collective-permute-start.2) | collective-permute-done | bytes 12320 | tf_op jit(solution)/shard_map/ppermute | solution.py:269
  12.0 0.1 pad_maximum_fusion.q_ref
  12.1 0.1 collective-permute-start.3
  12.2 1.2 %collective-permute-done.3.q_ref = bf16[4,6,2,512]{3,2,1,0:T(2,128)(2,1)S(1)} collective-permute-done((bf16[4,6,2,512]{3,2,1,0:T(2,128)(2,1)S(1)}, bf16[4,6,2,512]{3,2,1,0:T(2,128)(2,1)S(1)}, u32[]{:S(2)}, u32[]{:S(2)}) %collective-permute-start.3) | collective-permute-done | bytes 49184 | tf_op jit(solution)/shard_map/ppermute | solution.py:269
  13.4 0.0 copy-start.1
  13.4 0.9 %prefix_keys.3 = bf16[4,32,384]{2,1,0:T(8,128)(2,1)S(1)} custom-call(bf16[4,6,2,512]{3,2,1,0:T(2,128)(2,1)S(1)} %collective-permute-done.3.q_ref, s32[256,128]{1,0:T(8,128)S(1)} %get-tuple-element.12.low_ref, s32[256,128]{1,0:T(8,128)S(1)} %get-tuple-element.13.high_ref, s32[8,1536]{1,0:T(8,128)S(1)} %get-tuple-element.14.key_ref, ...), custom_call_target="tpu_custom_call" | custom-call | flops 201326592 | bytes 1572864 | tf_op jit(solution)/shard_map/prefix_keys/pallas_call | solution.py:313
  14.3 0.0 copy-start.2
  14.3 0.0 copy-start.4
  14.3 0.0 copy-start.7
  14.3 0.0 copy-start
  14.3 0.2 collective-permute-start.4
  14.6 0.9 %prefix_keys.2.a_ref = bf16[4,32,384]{2,1,0:T(8,128)(2,1)S(1)} custom-call(bf16[4,6,2,512]{3,2,1,0:T(2,128)(2,1)S(1)} %pad_maximum_fusion.q_ref, s32[256,128]{1,0:T(8,128)S(1)} %get-tuple-element.12.low_ref, s32[256,128]{1,0:T(8,128)S(1)} %get-tuple-element.13.high_ref, s32[8,1536]{1,0:T(8,128)S(1)} %get-tuple-element.14.key_ref, ...), custom_call_target="tpu_custom_call" | custom-call | flops 201326592 | bytes 1572864 | tf_op jit(solution)/shard_map/prefix_keys/pallas_call | solution.py:313
  15.5 0.2 collective-permute-done.4.b_ref
  15.7 0.3 %merge_cores.1 = (bf16[32,384]{1,0:T(8,128)(2,1)S(1)}, bf16[32,384]{1,0:T(8,128)(2,1)S(1)}, bf16[32,384]{1,0:T(8,128)(2,1)S(1)}, bf16[32,384]{1,0:T(8,128)(2,1)S(1)}) custom-call(bf16[4,32,384]{2,1,0:T(8,128)(2,1)S(1)} %prefix_keys.2.a_ref, bf16[4,32,384]{2,1,0:T(8,128)(2,1)S(1)} %collective-permute-done.4.b_ref), custom_call_target="tpu_custom_call" | custom-call | flops 1 | bytes 196608 | tf_op jit(solution)/shard_map/merge_cores/pallas_call | solution.py:340
  16.1 0.1 collective-permute-start.5
  16.1 0.8 %collective-permute-start.6 = (bf16[32,384]{1,0:T(8,128)(2,1)S(1)}, bf16[32,384]{1,0:T(8,128)(2,1)S(1)}, u32[]{:S(2)}, u32[]{:S(2)}) collective-permute-start(bf16[32,384]{1,0:T(8,128)(2,1)S(1)} %get-tuple-element.18), channel_id=1, source_target_pairs={{0,4},{1,5},{2,6},{3,7},{4,0},{5,1},{6,2},{7,3},{8,12},{9,13},{10,... | collective-permute-start | bytes 73736 | tf_op jit(solution)/shard_map/ppermute | solution.py:269
  17.0 3.5 %collective-permute-start.7 = (bf16[32,384]{1,0:T(8,128)(2,1)S(1)}, bf16[32,384]{1,0:T(8,128)(2,1)S(1)}, u32[]{:S(2)}, u32[]{:S(2)}) collective-permute-start(bf16[32,384]{1,0:T(8,128)(2,1)S(1)} %get-tuple-element.19), channel_id=1, source_target_pairs={{0,6},{1,7},{2,4},{3,5},{4,2},{5,3},{6,0},{7,1},{8,14},{9,15},{10,... | collective-permute-start | bytes 73736 | tf_op jit(solution)/shard_map/ppermute | solution.py:269
  20.5 0.0 copy-done.1
  20.5 0.0 copy-done.2
  20.5 0.0 copy-done.4
  20.5 0.0 copy-done.7
  20.5 0.0 copy-start.3
  20.5 0.0 copy-start.5
  20.5 0.0 copy-start.6
  20.6 1.1 %own_keys.1.refs_0_ = f32[32,384]{1,0:T(8,128)S(1)} custom-call(s32[6]{0:T(128)S(1)} %copy-done.7, bf16[6,2,512]{2,1,0:T(2,128)(2,1)S(1)} %copy-done.2, bf16[6,128,512]{2,1,0:T(8,128)(2,1)S(1)} %bitcast.9, bf16[6,2,512]{2,1,0:T(2,128)(2,1)S(1)} %bitcast.11), custom_call_target="tpu_custom_call" | custom-call | flops 25165824 | bytes 786432 | tf_op jit(solution)/shard_map/own_keys/pallas_call | solution.py:294
  21.6 0.0 collective-permute-done.5.refs_2_
  21.7 0.0 collective-permute-done.6.refs_3_
  21.7 0.9 %collective-permute-done.7.refs_4_ = bf16[32,384]{1,0:T(8,128)(2,1)S(1)} collective-permute-done((bf16[32,384]{1,0:T(8,128)(2,1)S(1)}, bf16[32,384]{1,0:T(8,128)(2,1)S(1)}, u32[]{:S(2)}, u32[]{:S(2)}) %collective-permute-start.7) | collective-permute-done | bytes 24608 | tf_op jit(solution)/shard_map/ppermute | solution.py:269
  22.6 0.0 copy-done
  22.6 0.5 %combine_project.1.refs_0_ = bf16[6,2,2048]{2,1,0:T(2,128)(2,1)S(1)} custom-call(f32[32,384]{1,0:T(8,128)S(1)} %own_keys.1.refs_0_, bf16[32,384]{1,0:T(8,128)(2,1)S(1)} %get-tuple-element.16.refs_1_, bf16[32,384]{1,0:T(8,128)(2,1)S(1)} %collective-permute-done.5.refs_2_, bf16[32,384]{1,0:T(8,128)(2,1)S(1)} %collective-permute-done.6.refs_3_, ...), custom_call_target="tpu_custom_call" | custom-call | flops 33554432 | bytes 2097152 | tf_op jit(solution)/shard_map/combine_project/pallas_call | solution.py:350
  23.1 2.5 %collective-permute-start.10 = (bf16[6,2,2048]{2,1,0:T(2,128)(2,1)S(1)}, bf16[6,2,2048]{2,1,0:T(2,128)(2,1)S(1)}, u32[]{:S(2)}, u32[]{:S(2)}) collective-permute-start(bf16[6,2,2048]{2,1,0:T(2,128)(2,1)S(1)} %combine_project.1.refs_0_), channel_id=1, source_target_pairs={{0,24},{8,16},{16,8},{24,0},{1,25},{9,17},{17,9},{25,1},{2,26},{10... | collective-permute-start | bytes 147464 | tf_op jit(solution)/shard_map/ppermute | solution.py:269
  25.6 0.5 %collective-permute-start.8 = (bf16[6,2,2048]{2,1,0:T(2,128)(2,1)S(1)}, bf16[6,2,2048]{2,1,0:T(2,128)(2,1)S(1)}, u32[]{:S(2)}, u32[]{:S(2)}) collective-permute-start(bf16[6,2,2048]{2,1,0:T(2,128)(2,1)S(1)} %combine_project.1.refs_0_), channel_id=1, source_target_pairs={{0,8},{8,0},{16,24},{24,16},{1,9},{9,1},{17,25},{25,17},{2,10},{10... | collective-permute-start | bytes 147464 | tf_op jit(solution)/shard_map/ppermute | solution.py:269
  26.1 0.5 %collective-permute-start.9 = (bf16[6,2,2048]{2,1,0:T(2,128)(2,1)S(1)}, bf16[6,2,2048]{2,1,0:T(2,128)(2,1)S(1)}, u32[]{:S(2)}, u32[]{:S(2)}) collective-permute-start(bf16[6,2,2048]{2,1,0:T(2,128)(2,1)S(1)} %combine_project.1.refs_0_), channel_id=1, source_target_pairs={{0,16},{8,24},{16,0},{24,8},{1,17},{9,25},{17,1},{25,9},{2,18},{10... | collective-permute-start | bytes 147464 | tf_op jit(solution)/shard_map/ppermute | solution.py:269
  26.7 1.5 %collective-permute-done.10.refs_3_ = bf16[6,2,2048]{2,1,0:T(2,128)(2,1)S(1)} collective-permute-done((bf16[6,2,2048]{2,1,0:T(2,128)(2,1)S(1)}, bf16[6,2,2048]{2,1,0:T(2,128)(2,1)S(1)}, u32[]{:S(2)}, u32[]{:S(2)}) %collective-permute-start.10) | collective-permute-done | bytes 49184 | tf_op jit(solution)/shard_map/ppermute | solution.py:269
  28.2 1.6 %collective-permute-done.8.refs_1_ = bf16[6,2,2048]{2,1,0:T(2,128)(2,1)S(1)} collective-permute-done((bf16[6,2,2048]{2,1,0:T(2,128)(2,1)S(1)}, bf16[6,2,2048]{2,1,0:T(2,128)(2,1)S(1)}, u32[]{:S(2)}, u32[]{:S(2)}) %collective-permute-start.8) | collective-permute-done | bytes 49184 | tf_op jit(solution)/shard_map/ppermute | solution.py:269
  29.7 0.5 %collective-permute-done.9.refs_2_ = bf16[6,2,2048]{2,1,0:T(2,128)(2,1)S(1)} collective-permute-done((bf16[6,2,2048]{2,1,0:T(2,128)(2,1)S(1)}, bf16[6,2,2048]{2,1,0:T(2,128)(2,1)S(1)}, u32[]{:S(2)}, u32[]{:S(2)}) %collective-permute-start.9) | collective-permute-done | bytes 49184 | tf_op jit(solution)/shard_map/ppermute | solution.py:269
  30.2 0.0 copy-done.3
  30.2 0.0 copy-done.5
  30.2 0.0 copy-done.6
  30.2 0.8 %residual_scores.1 = (bf16[6,2,2048]{2,1,0:T(2,128)(2,1)}, f32[6]{0:T(128)}) custom-call(bf16[6,2,2048]{2,1,0:T(2,128)(2,1)S(1)} %combine_project.1.refs_0_, bf16[6,2,2048]{2,1,0:T(2,128)(2,1)S(1)} %collective-permute-done.8.refs_1_, bf16[6,2,2048]{2,1,0:T(2,128)(2,1)S(1)} %collective-permute-done.9.refs_2_, ...), custom_call_target="tpu_custom_call" | custom-call | flops 1 | bytes 294912 | tf_op jit(solution)/shard_map/residual_scores/pallas_call | solution.py:375
Async XLA Ops:
  0.6 7.8 %collective-permute-start = (bf16[6,2,512]{2,1,0:T(2,128)(2,1)}, bf16[6,2,512]{2,1,0:T(2,128)(2,1)S(1)}, u32[]{:S(2)}, u32[]{:S(2)}) collective-permute-start(bf16[6,2,512]{2,1,0:T(2,128)(2,1)} %q_ref.3), channel_id=1, source_target_pairs={{0,2},{1,3},{2,0},{3,1},{4,6},{5,7},{6,4},{7,5},{8,10},{9,11},{10,... | collective-permute-start | bytes 36872 | tf_op jit(solution)/shard_map/ppermute | solution.py:269
  3.7 4.8 %collective-permute-start.1 = (bf16[6,2,512]{2,1,0:T(2,128)(2,1)}, bf16[6,2,512]{2,1,0:T(2,128)(2,1)S(1)}, u32[]{:S(2)}, u32[]{:S(2)}) collective-permute-start(bf16[6,2,512]{2,1,0:T(2,128)(2,1)} %q_ref.3), channel_id=1, source_target_pairs={{0,4},{1,5},{2,6},{3,7},{4,0},{5,1},{6,2},{7,3},{8,12},{9,13},{10,... | collective-permute-start | bytes 36872 | tf_op jit(solution)/shard_map/ppermute | solution.py:269
  6.3 5.7 %collective-permute-start.2 = (bf16[6,2,512]{2,1,0:T(2,128)(2,1)}, bf16[6,2,512]{2,1,0:T(2,128)(2,1)S(1)}, u32[]{:S(2)}, u32[]{:S(2)}) collective-permute-start(bf16[6,2,512]{2,1,0:T(2,128)(2,1)} %q_ref.3), channel_id=1, source_target_pairs={{0,6},{1,7},{2,4},{3,5},{4,2},{5,3},{6,0},{7,1},{8,14},{9,15},{10,... | collective-permute-start | bytes 36872 | tf_op jit(solution)/shard_map/ppermute | solution.py:269
  12.1 1.3 %collective-permute-start.3 = (bf16[4,6,2,512]{3,2,1,0:T(2,128)(2,1)S(1)}, bf16[4,6,2,512]{3,2,1,0:T(2,128)(2,1)S(1)}, u32[]{:S(2)}, u32[]{:S(2)}) collective-permute-start(bf16[4,6,2,512]{3,2,1,0:T(2,128)(2,1)S(1)} %pad_maximum_fusion.q_ref), channel_id=1, source_target_pairs={{0,1},{1,0},{2,3},{3,2},{4,5},{5,4},{6,7},{7,6},{8,9},{9,8},{10,11... | collective-permute-start | bytes 147464 | tf_op jit(solution)/shard_map/ppermute | solution.py:269
  13.4 7.1 %copy-start.1 = (bf16[1,6,128,512]{3,2,1,0:T(8,128)(2,1)S(1)}, bf16[1,6,128,512]{3,2,1,0:T(8,128)(2,1)}, u32[]{:S(2)}) copy-start(bf16[1,6,128,512]{3,2,1,0:T(8,128)(2,1)} %param.17) | copy-start | bytes 2359300
  14.3 6.2 %copy-start.2 = (bf16[6,2,512]{2,1,0:T(2,128)(2,1)S(1)}, bf16[6,2,512]{2,1,0:T(2,128)(2,1)}, u32[]{:S(2)}) copy-start(bf16[6,2,512]{2,1,0:T(2,128)(2,1)} %q_ref.3) | copy-start | bytes 36868
  14.3 6.2 %copy-start.4 = (bf16[1,6,2,512]{3,2,1,0:T(2,128)(2,1)S(1)}, bf16[1,6,2,512]{3,2,1,0:T(2,128)(2,1)}, u32[]{:S(2)}) copy-start(bf16[1,6,2,512]{3,2,1,0:T(2,128)(2,1)} %param.19) | copy-start | bytes 36868
  14.3 6.2 %copy-start.7 = (s32[6]{0:T(128)S(1)}, s32[6]{0:T(128)}, u32[]{:S(2)}) copy-start(s32[6]{0:T(128)} %len_ref.2) | copy-start | bytes 76
  14.3 8.3 %copy-start = (bf16[512,2048]{1,0:T(8,128)(2,1)S(1)}, bf16[512,2048]{1,0:T(8,128)(2,1)}, u32[]{:S(2)}) copy-start(bf16[512,2048]{1,0:T(8,128)(2,1)} %refs_5_.1) | copy-start | bytes 6291460
  14.3 1.4 %collective-permute-start.4 = (bf16[4,32,384]{2,1,0:T(8,128)(2,1)S(1)}, bf16[4,32,384]{2,1,0:T(8,128)(2,1)S(1)}, u32[]{:S(2)}, u32[]{:S(2)}) collective-permute-start(bf16[4,32,384]{2,1,0:T(8,128)(2,1)S(1)} %prefix_keys.3), channel_id=1, source_target_pairs={{0,1},{1,0},{2,3},{3,2},{4,5},{5,4},{6,7},{7,6},{8,9},{9,8},{10,11... | collective-permute-start | bytes 294920 | tf_op jit(solution)/shard_map/ppermute | solution.py:269
  16.1 5.6 %collective-permute-start.5 = (bf16[32,384]{1,0:T(8,128)(2,1)S(1)}, bf16[32,384]{1,0:T(8,128)(2,1)S(1)}, u32[]{:S(2)}, u32[]{:S(2)}) collective-permute-start(bf16[32,384]{1,0:T(8,128)(2,1)S(1)} %get-tuple-element.17), channel_id=1, source_target_pairs={{0,2},{1,3},{2,0},{3,1},{4,6},{5,7},{6,4},{7,5},{8,10},{9,11},{10,... | collective-permute-start | bytes 73736 | tf_op jit(solution)/shard_map/ppermute | solution.py:269
  16.1 5.5 %collective-permute-start.6 = (bf16[32,384]{1,0:T(8,128)(2,1)S(1)}, bf16[32,384]{1,0:T(8,128)(2,1)S(1)}, u32[]{:S(2)}, u32[]{:S(2)}) collective-permute-start(bf16[32,384]{1,0:T(8,128)(2,1)S(1)} %get-tuple-element.18), channel_id=1, source_target_pairs={{0,4},{1,5},{2,6},{3,7},{4,0},{5,1},{6,2},{7,3},{8,12},{9,13},{10,... | collective-permute-start | bytes 73736 | tf_op jit(solution)/shard_map/ppermute | solution.py:269
  17.0 5.6 %collective-permute-start.7 = (bf16[32,384]{1,0:T(8,128)(2,1)S(1)}, bf16[32,384]{1,0:T(8,128)(2,1)S(1)}, u32[]{:S(2)}, u32[]{:S(2)}) collective-permute-start(bf16[32,384]{1,0:T(8,128)(2,1)S(1)} %get-tuple-element.19), channel_id=1, source_target_pairs={{0,6},{1,7},{2,4},{3,5},{4,2},{5,3},{6,0},{7,1},{8,14},{9,15},{10,... | collective-permute-start | bytes 73736 | tf_op jit(solution)/shard_map/ppermute | solution.py:269
  20.5 9.7 %copy-start.3 = (bf16[6,2,2048]{2,1,0:T(2,128)(2,1)S(1)}, bf16[6,2,2048]{2,1,0:T(2,128)(2,1)}, u32[]{:S(2)}) copy-start(bf16[6,2,2048]{2,1,0:T(2,128)(2,1)} %refs_4_.1) | copy-start | bytes 147460
  20.5 9.7 %copy-start.5 = (f32[2048]{0:T(1024)S(1)}, f32[2048]{0:T(1024)}, u32[]{:S(2)}) copy-start(f32[2048]{0:T(1024)} %param.22) | copy-start | bytes 24580
  20.5 9.7 %copy-start.6 = (f32[2048]{0:T(1024)S(1)}, f32[2048]{0:T(1024)}, u32[]{:S(2)}) copy-start(f32[2048]{0:T(1024)} %param.23) | copy-start | bytes 24580
  23.1 5.0 %collective-permute-start.10 = (bf16[6,2,2048]{2,1,0:T(2,128)(2,1)S(1)}, bf16[6,2,2048]{2,1,0:T(2,128)(2,1)S(1)}, u32[]{:S(2)}, u32[]{:S(2)}) collective-permute-start(bf16[6,2,2048]{2,1,0:T(2,128)(2,1)S(1)} %combine_project.1.refs_0_), channel_id=1, source_target_pairs={{0,24},{8,16},{16,8},{24,0},{1,25},{9,17},{17,9},{25,1},{2,26},{10... | collective-permute-start | bytes 147464 | tf_op jit(solution)/shard_map/ppermute | solution.py:269
  25.6 4.1 %collective-permute-start.8 = (bf16[6,2,2048]{2,1,0:T(2,128)(2,1)S(1)}, bf16[6,2,2048]{2,1,0:T(2,128)(2,1)S(1)}, u32[]{:S(2)}, u32[]{:S(2)}) collective-permute-start(bf16[6,2,2048]{2,1,0:T(2,128)(2,1)S(1)} %combine_project.1.refs_0_), channel_id=1, source_target_pairs={{0,8},{8,0},{16,24},{24,16},{1,9},{9,1},{17,25},{25,17},{2,10},{10... | collective-permute-start | bytes 147464 | tf_op jit(solution)/shard_map/ppermute | solution.py:269
  26.1 4.1 %collective-permute-start.9 = (bf16[6,2,2048]{2,1,0:T(2,128)(2,1)S(1)}, bf16[6,2,2048]{2,1,0:T(2,128)(2,1)S(1)}, u32[]{:S(2)}, u32[]{:S(2)}) collective-permute-start(bf16[6,2,2048]{2,1,0:T(2,128)(2,1)S(1)} %combine_project.1.refs_0_), channel_id=1, source_target_pairs={{0,16},{8,24},{16,0},{24,8},{1,17},{9,25},{17,1},{25,9},{2,18},{10... | collective-permute-start | bytes 147464 | tf_op jit(solution)/shard_map/ppermute | solution.py:269

commit v4 on v3

--- a/solution.py
+++ b/solution.py
@@ -8,6 +8,9 @@
 from jax.sharding import PartitionSpec as P
 
 SAMPLES = 16
+ORDER_A = (2, 3, 1)
+ORDER_B = (3, 2, 1)
+ORDER_C = (1, 2, 3)
 LANES = 128
 FLOOR = -(2.0**100)
 LOG2E = 1.4426950408889634
@@ -65,23 +68,31 @@
             dest[pl.ds(base + c * rows + reqs * drafts, pad), :] = jnp.zeros((pad, head_size), dest.dtype)
 
 
+def write_keys(page_ref, key_ref, page_tokens):
+    lane = iota((8, page_tokens), 1)
+    for s in range(page_ref.shape[0]):
+        key_ref[:, pl.ds(s * page_tokens, page_tokens)] = lane + page_ref[s] * page_tokens
+
+
 def layout_kernel(device_of, slots, local, rows, heads, drafts, page_tokens,
-                  ids_ref, len_ref, page_ref, q_ref, pool_ref,
-                  low_ref, high_ref, key_ref, q_out_ref, pool_out_ref, start_ref, sems):
-    copies = [
-        pltpu.make_async_copy(q_ref, q_out_ref, sems.at[0]),
-        pltpu.make_async_copy(pool_ref, pool_out_ref, sems.at[1]),
-    ]
+                  ids_hbm, len_hbm, page_hbm, q_ref, pool_ref,
+                  low_ref, high_ref, key_ref, q_out_ref, pool_out_ref,
+                  ids_ref, len_ref, page_ref, start_ref, sems):
+    pairs = [(ids_hbm, ids_ref), (len_hbm, len_ref), (page_hbm, page_ref), (pool_ref, pool_out_ref), (q_ref, q_out_ref)]
+    copies = [pltpu.make_async_copy(a, b, sems.at[i]) for i, (a, b) in enumerate(pairs)]
     for copy in copies:
         copy.start()
     me = lax.axis_index("blk")
     prompts = len_ref.shape[0]
+    shift = SAMPLES.bit_length() - 1
+    for copy in copies[:3]:
+        copy.wait()
 
     def place(p, start):
         start_ref[p] = start
-        return start + (len_ref[p] + page_tokens - 1) // page_tokens * page_tokens
-
-    lax.fori_loop(0, prompts, place, jnp.int32(0))
+        return start + lax.div(len_ref[p] + page_tokens - 1, page_tokens) * page_tokens
+
+    lax.fori_loop(0, prompts, place, jnp.int32(0), unroll=prompts <= 4)
     request = iota((rows, LANES), 0) // drafts
 
     def one(j, _):
@@ -89,45 +100,65 @@
         low = jnp.zeros((rows, LANES), jnp.int32)
         high = low
         for r in range(local):
-            prompt = ids_ref[device * local + r] // SAMPLES
+            prompt = lax.shift_right_logical(ids_ref[device * local + r], shift)
             start = start_ref[prompt]
             low = jnp.where(request == r, start, low)
             high = jnp.where(request == r, start + len_ref[prompt], high)
         for c in range(heads):
-            place_at = pl.ds(pl.multiple_of((j * heads + c) * rows, rows), rows)
+            place_at = pl.ds((j * heads + c) * rows, rows)
             low_ref[place_at, :] = low
             high_ref[place_at, :] = high
         return 0
 
-    lax.fori_loop(0, slots, one, 0, unroll=slots <= 8)
-    lane = iota((8, page_tokens), 1)
-    for s in range(page_ref.shape[0]):
-        key_ref[:, pl.ds(s * page_tokens, page_tokens)] = lane + page_ref[s] * page_tokens
-    for copy in copies:
+    if slots <= 8:
+        for j in range(slots):
+            one(j, 0)
+    else:
+        lax.fori_loop(0, slots, one, 0)
+    write_keys(page_ref, key_ref, page_tokens)
+    for copy in copies[3:]:
         copy.wait()
 
 
-def prefix_kernel(heads, rows, scale, q_ref, low_ref, high_ref, key_ref, pool_ref, *rest):
-    out_ref, q_rows = rest
+def key_row(ref, at, page_tokens):
+    if ref.shape[0] > 1:
+        return ref[0:1, at:at + LANES]
+    lane = iota((1, LANES), 1)
+    first = at // page_tokens
+    page = ref[:, first:first + 1]
+    for n in range(1, LANES // page_tokens):
+        page = jnp.where(lane >= n * page_tokens, ref[:, first + n:first + n + 1], page)
+    return page * page_tokens + lane % page_tokens
+
+
+def prefix_kernel(heads, rows, scale, q_ref, low_ref, high_ref, *rest):
+    *both_refs, out_ref, q_rows = rest
+    key_refs, pool_refs = both_refs[:len(both_refs) // 2], both_refs[len(both_refs) // 2:]
     slots = q_ref.shape[0]
-    head_size = pool_ref.shape[2] // 2
-    keys = pool_ref.shape[0] * pool_ref.shape[1]
+    pages, page_tokens, head_pair = pool_refs[0].shape
+    head_size = head_pair // 2
+    keys = pages * page_tokens
     for j in range(slots):
         spread_rows(q_rows, j * heads * rows, q_ref.at[j], heads, head_size, rows)
-    logits = lax.dot_general(
-        q_rows[...], pool_ref[:, :, :head_size].reshape(keys, head_size),
-        (((1,), (1,)), ((), ())), preferred_element_type=jnp.float32,
-    )
     low, high = low_ref[...], high_ref[...]
     parts = []
-    for k in range(0, keys, LANES):
-        key = key_ref[0:1, k:k + LANES]
-        live = (key >= low) & (key < high)
-        parts.append(jnp.where(live, logits[:, k:k + LANES] * scale, FLOOR))
+    for key_ref, pool_ref in zip(key_refs, pool_refs):
+        logits = lax.dot_general(
+            q_rows[...], pool_ref[:, :, :head_size].reshape(keys, head_size),
+            (((1,), (1,)), ((), ())), preferred_element_type=jnp.float32,
+        )
+        for k in range(0, keys, LANES):
+            key = key_row(key_ref, k, page_tokens)
+            live = (key >= low) & (key < high)
+            parts.append(jnp.where(live, logits[:, k:k + LANES] * scale, FLOOR))
     peak, weights, den = softmax_parts(jnp.concatenate(parts, axis=1))
-    num = jnp.dot(
-        weights.astype(jnp.bfloat16), pool_ref[:, :, head_size:].reshape(keys, head_size),
-        preferred_element_type=jnp.float32,
+    weights = weights.astype(jnp.bfloat16)
+    num = sum(
+        jnp.dot(
+            weights[:, n * keys:(n + 1) * keys], pool_ref[:, :, head_size:].reshape(keys, head_size),
+            preferred_element_type=jnp.float32,
+        )
+        for n, pool_ref in enumerate(pool_refs)
     )
     per = heads * rows
     out_ref[:, :, :head_size] = num.reshape(slots, per, head_size).astype(out_ref.dtype)
@@ -187,13 +218,6 @@
     num = sum(n * f for n, f in zip(nums, factors))
     den = sum(s[1] * f for s, f in zip(stats, factors))
     return num, peak, den
-
-
-def merge_kernel(head_size, a_ref, b_ref, *out_refs):
-    for j, out_ref in enumerate(out_refs):
-        num, peak, den = summed_parts([a_ref[j], b_ref[j]], head_size)
-        out_ref[:, :head_size] = num.astype(out_ref.dtype)
-        out_ref[:, head_size:] = pack_stats(peak, den).astype(out_ref.dtype)
 
 
 def project(num, den, weight_ref, out_ref, heads, rows):
@@ -264,32 +288,46 @@
     scale = head_size ** (-0.5) * LOG2E
     paired = blk in (2, 4, 8)
     half = blk // 2
+    partners = [0] + [j for j in ORDER_A if j < half]
 
     def swap(x, axis, size, mask):
         return lax.ppermute(x, axis, [(i, i ^ mask) for i in range(size)])
 
     def device_of(j, me):
-        if not paired:
-            return j
-        return me ^ (j * 2) if isinstance(j, int) and j < half else me ^ (j % half * 2 + j // half)
+        return me ^ (partners[j] * 2) if paired else j
+
+    slots = half if paired else blk
+    pools = [pool]
+    if paired:
+        pools.append(swap(pool, "blk", blk, 1))
+        far_pages = swap(slot_page, "blk", blk, 1)
 
     in_hbm = functools.partial(pltpu.with_memory_space_constraint, memory_space=pltpu.HBM)
-    low, high, key, near_queries, pool = pl.pallas_call(
-        functools.partial(layout_kernel, device_of, blk, local, rows, heads, drafts, page_tokens),
+    low, high, near_keys, near_queries, pools[0] = pl.pallas_call(
+        functools.partial(layout_kernel, device_of, slots, local, rows, heads, drafts, page_tokens),
         out_shape=(
-            jax.ShapeDtypeStruct((blk * per, LANES), jnp.int32),
-            jax.ShapeDtypeStruct((blk * per, LANES), jnp.int32),
+            jax.ShapeDtypeStruct((slots * per, LANES), jnp.int32),
+            jax.ShapeDtypeStruct((slots * per, LANES), jnp.int32),
             jax.ShapeDtypeStruct((8, keys), jnp.int32),
             jax.ShapeDtypeStruct(queries.shape, queries.dtype),
             jax.ShapeDtypeStruct(pool.shape, pool.dtype),
         ),
-        in_specs=[SMEM] * 3 + [ANY] * 2,
+        in_specs=[ANY] * 5,
         out_specs=(VMEM,) * 3 + (ANY,) * 2,
-        scratch_shapes=[pltpu.SMEM(prompt_len.shape, jnp.int32), pltpu.SemaphoreType.DMA((2,))],
+        scratch_shapes=[
+            pltpu.SMEM(request_ids.shape, jnp.int32),
+            pltpu.SMEM(prompt_len.shape, jnp.int32),
+            pltpu.SMEM(slot_page.shape, jnp.int32),
+            pltpu.SMEM(prompt_len.shape, jnp.int32),
+            pltpu.SemaphoreType.DMA((5,)),
+        ],
         compiler_params=vmem(8),
-        cost_estimate=cost(1, 2 * blk * per * LANES * 4),
+        cost_estimate=cost(1, 2 * slots * per * LANES * 4),
         name="key_ranges",
     )(*map(in_hbm, (request_ids, prompt_len, slot_page, queries, pool)))
+    key_lists = [near_keys]
+    if paired:
+        key_lists.append(far_pages.reshape(1, page_count))
 
     own = pl.pallas_call(
         functools.partial(own_kernel, heads, rows, scale),
@@ -305,48 +343,32 @@
         name="own_keys",
     )(tail_len, queries, tail_cache[0], new_kv[0])
 
-    def prefix(block, first):
+    def prefix(block):
         slots = block.shape[0]
         step = min(slots, 4)
-        grid = slots // step
-        offset = first // step
         return pl.pallas_call(
             functools.partial(prefix_kernel, heads, rows, scale),
             out_shape=jax.ShapeDtypeStruct((slots, per, head_size + LANES), jnp.bfloat16),
-            grid=(grid,),
+            grid=(slots // step,),
             in_specs=[
                 pl.BlockSpec((step, local, drafts, head_width), lambda i: (i, 0, 0, 0)),
-                pl.BlockSpec((step * per, LANES), lambda i: (i + offset, 0)),
-                pl.BlockSpec((step * per, LANES), lambda i: (i + offset, 0)),
-                pl.BlockSpec((8, keys), lambda i: (0, 0)),
-                pl.BlockSpec((page_count, page_tokens, head_pair), lambda i: (0, 0, 0)),
-            ],
+                pl.BlockSpec((step * per, LANES), lambda i: (i, 0)),
+                pl.BlockSpec((step * per, LANES), lambda i: (i, 0)),
+            ] + [pl.BlockSpec(k.shape, lambda i: (0, 0)) for k in key_lists] + [pl.BlockSpec((page_count, page_tokens, head_pair), lambda i: (0, 0, 0))] * len(pools),
             out_specs=pl.BlockSpec((step, per, head_size + LANES), lambda i: (i, 0, 0)),
             scratch_shapes=[pltpu.VMEM((step * per, head_size), jnp.bfloat16)],
-            compiler_params=vmem(16),
-            cost_estimate=cost(4 * slots * per * keys * head_size, 2 * pool.size),
+            compiler_params=vmem(24),
+            cost_estimate=cost(4 * slots * per * keys * len(pools) * head_size, 2 * pool.size * len(pools)),
             name="prefix_keys",
-        )(block, low, high, key, pool)
+        )(block, low, high, *key_lists, *pools)
 
     partial_shape = jax.ShapeDtypeStruct((local, drafts, width), jnp.bfloat16)
     if paired:
-        column = [near_queries] + [swap(queries, "blk", blk, 2 * j) for j in range(1, half)]
-        mine = jnp.stack(column)
-        theirs = swap(mine, "blk", blk, 1)
-        sums_mine = prefix(mine, 0)
-        sums_theirs = prefix(theirs, half)
-        back = swap(sums_theirs, "blk", blk, 1)
-        block_shape = jax.ShapeDtypeStruct((per, head_size + LANES), jnp.bfloat16)
-        merged = pl.pallas_call(
-            functools.partial(merge_kernel, head_size),
-            out_shape=(block_shape,) * half,
-            in_specs=[VMEM] * 2,
-            out_specs=(VMEM,) * half,
-            compiler_params=vmem(8),
-            cost_estimate=cost(1, 6 * half * per * head_size),
-            name="merge_cores",
-        )(sums_mine, back)
-        blocks = [merged[0]] + [swap(merged[j], "blk", blk, 2 * j) for j in range(1, half)]
+        column = [near_queries] + [swap(queries, "blk", blk, 2 * j) for j in partners[1:]]
+        sums = prefix(jnp.stack(column))
+        blocks = [sums[0]] + [
+            swap(sums[partners.index(j)], "blk", blk, 2 * j) for j in ORDER_B if j < half
+        ]
         share = pl.pallas_call(
             functools.partial(combine_kernel, heads, rows, head_size),
             out_shape=partial_shape,
@@ -358,7 +380,7 @@
         )(own, *blocks, out_weight)
     else:
         gathered = lax.all_gather(queries, "blk", axis=0)
-        blocks = lax.all_to_all(prefix(gathered, 0), "blk", 0, 0)
+        blocks = lax.all_to_all(prefix(gathered), "blk", 0, 0)
         share = pl.pallas_call(
             functools.partial(combine_many_kernel, heads, rows, head_size),
             out_shape=partial_shape,
@@ -369,7 +391,7 @@
             name="combine_project",
         )(own, blocks, out_weight)
     if kv in (2, 4):
-        shares = [share] + [swap(share, "kv", kv, j) for j in range(1, kv)]
+        shares = [share] + [swap(share, "kv", kv, j) for j in ORDER_C if j < kv]
     else:
         shares = [lax.psum(share, "kv")]
     hidden_out, scores = pl.pallas_call(

time: 31.3 us -> 27.7 us (0.88)
  waiting for transfers between devices: 9.55 us -> 7.48 us
  Pallas kernels: 6.6 us -> 5.43 us
    ppermute x11, waiting for transfers between devices: 9.55 us -> 7.48 us  [swap(): return lax.ppermute(x, axis, [(i, i ^ mask) for i in range(size)])]
    pallas_call x2 -> x1, Pallas kernels: 2.47 us -> 1.45 us  [body(): pl.pallas_call(functools.partial(layout_kernel, device_of, slots, local,...]
    pallas_call x2 -> x1, Pallas kernels: 1.77 us -> 1.61 us  [prefix(): pl.pallas_call(functools.partial(prefix_kernel, heads, rows, scale), out_...]
  transfers between devices with their start and end apart: 11 -> 11, of which waited for: 8 -> 6; matrix products, arithmetic and copies ran while one was open for 0% -> 0% of each run, Pallas kernels for 13% -> 9%
where the time goes in v4:
time: 27.7 us; the launch traced here: 27.6 us
  starting transfers between devices  13.8 us (50%)
  waiting for transfers between devices  7.48 us (27%)
  Pallas kernels  5.43 us (20%)
  between operations  0.77 us (3%)
    ppermute x11, starting transfers between devices, swap(): return lax.ppermute(x, axis, [(i, i ^ mask) for i in range(size)])  13.8 us
    ppermute x11, waiting for transfers between devices, swap(): return lax.ppermute(x, axis, [(i, i ^ mask) for i in range(size)])  7.48 us
    pallas_call x1, Pallas kernels, prefix(): pl.pallas_call(functools.partial(prefix_kernel, heads, rows, scale), out_...  1.61 us
    pallas_call x1, Pallas kernels, body(): pl.pallas_call(functools.partial(layout_kernel, device_of, slots, local,...  1.45 us
    pallas_call x1, Pallas kernels, body(): pl.pallas_call(functools.partial(own_kernel, heads, rows, scale), out_sha...  1.08 us
    pallas_call x1, Pallas kernels, body(): pl.pallas_call(final_kernel, out_shape=(jax.ShapeDtypeStruct(hidden.shape...  0.77 us
  transfers between devices with their start and end apart: 11, of which 6 were waited for; matrix products, arithmetic and copies ran while one was open for 0% of the time, Pallas kernels for 9%

profile of v4, /device:TPU:0, one launch (start us, length us, event | category | flops | bytes accessed | tf_op | source)
XLA Modules:
  0.0 27.6 jit_solution(8854867529353636725)
XLA Ops:
  0.6 0.5 %collective-permute-start.4 = (bf16[24,64,512]{2,1,0:T(8,128)(2,1)}, bf16[24,64,512]{2,1,0:T(8,128)(2,1)S(1)}, u32[]{:S(2)}, u32[]{:S(2)}) collective-permute-start(bf16[24,64,512]{2,1,0:T(8,128)(2,1)} %bitcast.24), channel_id=1, source_target_pairs={{0,1},{1,0},{2,3},{3,2},{4,5},{5,4},{6,7},{7,6},{8,9},{9,8},{10,11... | collective-permute-start | bytes 4718600 | tf_op jit(solution)/shard_map/ppermute | solution.py:294
  1.1 3.7 %collective-permute-start = (bf16[6,2,512]{2,1,0:T(2,128)(2,1)}, bf16[6,2,512]{2,1,0:T(2,128)(2,1)S(1)}, u32[]{:S(2)}, u32[]{:S(2)}) collective-permute-start(bf16[6,2,512]{2,1,0:T(2,128)(2,1)} %q_ref.3), channel_id=1, source_target_pairs={{0,4},{1,5},{2,6},{3,7},{4,0},{5,1},{6,2},{7,3},{8,12},{9,13},{10,... | collective-permute-start | bytes 36872 | tf_op jit(solution)/shard_map/ppermute | solution.py:294
  4.8 1.3 %collective-permute-start.1 = (bf16[6,2,512]{2,1,0:T(2,128)(2,1)}, bf16[6,2,512]{2,1,0:T(2,128)(2,1)S(1)}, u32[]{:S(2)}, u32[]{:S(2)}) collective-permute-start(bf16[6,2,512]{2,1,0:T(2,128)(2,1)} %q_ref.3), channel_id=1, source_target_pairs={{0,6},{1,7},{2,4},{3,5},{4,2},{5,3},{6,0},{7,1},{8,14},{9,15},{10,... | collective-permute-start | bytes 36872 | tf_op jit(solution)/shard_map/ppermute | solution.py:294
  6.2 0.2 collective-permute-start.2
  6.4 0.0 collective-permute-start.3
  6.4 1.5 %key_ranges.1 = (s32[128,128]{1,0:T(8,128)S(1)}, s32[128,128]{1,0:T(8,128)S(1)}, s32[8,1536]{1,0:T(8,128)S(1)}, bf16[6,2,512]{2,1,0:T(2,128)(2,1)S(1)}, bf16[24,64,512]{2,1,0:T(8,128)(2,1)S(1)}) custom-call(s32[48]{0:T(128)} %ids_hbm.1, s32[3]{0:T(128)} %len_hbm.1, s32[24]{0:T(128)} %page_hbm.1, bf16[6,2,512]{2,1,0:T(2,128)(2,1)} %q_ref.3, ...), custom_call_target="tpu_custom_call" | custom-call | flops 1 | bytes 131072 | tf_op jit(solution)/shard_map/key_ranges/pallas_call | solution.py:306
  7.9 0.0 collective-permute-done
  7.9 2.6 %collective-permute-done.1 = bf16[6,2,512]{2,1,0:T(2,128)(2,1)S(1)} collective-permute-done((bf16[6,2,512]{2,1,0:T(2,128)(2,1)}, bf16[6,2,512]{2,1,0:T(2,128)(2,1)S(1)}, u32[]{:S(2)}, u32[]{:S(2)}) %collective-permute-start.1) | collective-permute-done | bytes 12320 | tf_op jit(solution)/shard_map/ppermute | solution.py:294
  10.5 0.0 collective-permute-done.2
  10.5 0.1 pad_maximum_fusion.q_ref
  10.6 0.0 collective-permute-done.3
  10.6 0.0 collective-permute-done.4.rest_3_
  10.6 0.0 copy-start.1
  10.6 0.0 copy-start.2
  10.7 0.0 copy-start.4
  10.7 0.0 copy-start.7
  10.7 0.0 copy-start
  10.7 1.6 %prefix_keys.1 = bf16[4,32,384]{2,1,0:T(8,128)(2,1)S(1)} custom-call(bf16[4,6,2,512]{3,2,1,0:T(2,128)(2,1)S(1)} %pad_maximum_fusion.q_ref, s32[128,128]{1,0:T(8,128)S(1)} %get-tuple-element.8.low_ref, s32[128,128]{1,0:T(8,128)S(1)} %get-tuple-element.9.high_ref, s32[8,1536]{1,0:T(8,128)S(1)} %get-tuple-element.10.rest_0_, s32[1,24]{1,0:T(1,128)S(1)} %bitcast.23, ...), custom_call_target="tpu_custom_call" | custom-call | flops 402653184 | bytes 3145728 | tf_op jit(solution)/shard_map/prefix_keys/pallas_call | solution.py:349
  12.3 2.1 %collective-permute-start.5 = (bf16[32,384]{1,0:T(8,128)(2,1)S(1)}, bf16[32,384]{1,0:T(8,128)(2,1)S(1)}, u32[]{:S(2)}, u32[]{:S(2)}) collective-permute-start(bf16[32,384]{1,0:T(8,128)(2,1)S(1)} %get-tuple-element.14), channel_id=1, source_target_pairs={{0,6},{1,7},{2,4},{3,5},{4,2},{5,3},{6,0},{7,1},{8,14},{9,15},{10,... | collective-permute-start | bytes 73736 | tf_op jit(solution)/shard_map/ppermute | solution.py:294
  14.4 0.0 collective-permute-start.6
  14.4 2.4 %collective-permute-start.7 = (bf16[32,384]{1,0:T(8,128)(2,1)S(1)}, bf16[32,384]{1,0:T(8,128)(2,1)S(1)}, u32[]{:S(2)}, u32[]{:S(2)}) collective-permute-start(bf16[32,384]{1,0:T(8,128)(2,1)S(1)} %get-tuple-element.12), channel_id=1, source_target_pairs={{0,2},{1,3},{2,0},{3,1},{4,6},{5,7},{6,4},{7,5},{8,10},{9,11},{10,... | collective-permute-start | bytes 73736 | tf_op jit(solution)/shard_map/ppermute | solution.py:294
  16.8 0.0 copy-done.1
  16.8 0.0 copy-done.2
  16.8 0.0 copy-done.4
  16.8 0.0 copy-done.7
  16.8 0.0 copy-start.3
  16.8 0.0 copy-start.5
  16.8 0.0 copy-start.6
  16.8 1.1 %own_keys.1.refs_0_ = f32[32,384]{1,0:T(8,128)S(1)} custom-call(s32[6]{0:T(128)S(1)} %copy-done.7, bf16[6,2,512]{2,1,0:T(2,128)(2,1)S(1)} %copy-done.2, bf16[6,128,512]{2,1,0:T(8,128)(2,1)S(1)} %bitcast.18, bf16[6,2,512]{2,1,0:T(2,128)(2,1)S(1)} %bitcast.20), custom_call_target="tpu_custom_call" | custom-call | flops 25165824 | bytes 786432 | tf_op jit(solution)/shard_map/own_keys/pallas_call | solution.py:332
  17.9 0.3 %collective-permute-done.5.refs_2_ = bf16[32,384]{1,0:T(8,128)(2,1)S(1)} collective-permute-done((bf16[32,384]{1,0:T(8,128)(2,1)S(1)}, bf16[32,384]{1,0:T(8,128)(2,1)S(1)}, u32[]{:S(2)}, u32[]{:S(2)}) %collective-permute-start.5) | collective-permute-done | bytes 24608 | tf_op jit(solution)/shard_map/ppermute | solution.py:294
  18.2 1.0 %collective-permute-done.6.refs_3_ = bf16[32,384]{1,0:T(8,128)(2,1)S(1)} collective-permute-done((bf16[32,384]{1,0:T(8,128)(2,1)S(1)}, bf16[32,384]{1,0:T(8,128)(2,1)S(1)}, u32[]{:S(2)}, u32[]{:S(2)}) %collective-permute-start.6) | collective-permute-done | bytes 24608 | tf_op jit(solution)/shard_map/ppermute | solution.py:294
  19.1 0.0 collective-permute-done.7.refs_4_
  19.1 0.0 copy-done
  19.1 0.5 %combine_project.1.refs_0_ = bf16[6,2,2048]{2,1,0:T(2,128)(2,1)S(1)} custom-call(f32[32,384]{1,0:T(8,128)S(1)} %own_keys.1.refs_0_, bf16[32,384]{1,0:T(8,128)(2,1)S(1)} %get-tuple-element.15.refs_1_, bf16[32,384]{1,0:T(8,128)(2,1)S(1)} %collective-permute-done.5.refs_2_, bf16[32,384]{1,0:T(8,128)(2,1)S(1)} %collective-permute-done.6.refs_3_, ...), custom_call_target="tpu_custom_call" | custom-call | flops 33554432 | bytes 2097152 | tf_op jit(solution)/shard_map/combine_project/pallas_call | solution.py:372
  19.7 2.5 %collective-permute-start.10 = (bf16[6,2,2048]{2,1,0:T(2,128)(2,1)S(1)}, bf16[6,2,2048]{2,1,0:T(2,128)(2,1)S(1)}, u32[]{:S(2)}, u32[]{:S(2)}) collective-permute-start(bf16[6,2,2048]{2,1,0:T(2,128)(2,1)S(1)} %combine_project.1.refs_0_), channel_id=1, source_target_pairs={{0,24},{8,16},{16,8},{24,0},{1,25},{9,17},{17,9},{25,1},{2,26},{10... | collective-permute-start | bytes 147464 | tf_op jit(solution)/shard_map/ppermute | solution.py:294
  22.2 0.5 %collective-permute-start.8 = (bf16[6,2,2048]{2,1,0:T(2,128)(2,1)S(1)}, bf16[6,2,2048]{2,1,0:T(2,128)(2,1)S(1)}, u32[]{:S(2)}, u32[]{:S(2)}) collective-permute-start(bf16[6,2,2048]{2,1,0:T(2,128)(2,1)S(1)} %combine_project.1.refs_0_), channel_id=1, source_target_pairs={{0,8},{8,0},{16,24},{24,16},{1,9},{9,1},{17,25},{25,17},{2,10},{10... | collective-permute-start | bytes 147464 | tf_op jit(solution)/shard_map/ppermute | solution.py:294
  22.7 0.5 %collective-permute-start.9 = (bf16[6,2,2048]{2,1,0:T(2,128)(2,1)S(1)}, bf16[6,2,2048]{2,1,0:T(2,128)(2,1)S(1)}, u32[]{:S(2)}, u32[]{:S(2)}) collective-permute-start(bf16[6,2,2048]{2,1,0:T(2,128)(2,1)S(1)} %combine_project.1.refs_0_), channel_id=1, source_target_pairs={{0,16},{8,24},{16,0},{24,8},{1,17},{9,25},{17,1},{25,9},{2,18},{10... | collective-permute-start | bytes 147464 | tf_op jit(solution)/shard_map/ppermute | solution.py:294
  23.2 1.5 %collective-permute-done.10.refs_3_ = bf16[6,2,2048]{2,1,0:T(2,128)(2,1)S(1)} collective-permute-done((bf16[6,2,2048]{2,1,0:T(2,128)(2,1)S(1)}, bf16[6,2,2048]{2,1,0:T(2,128)(2,1)S(1)}, u32[]{:S(2)}, u32[]{:S(2)}) %collective-permute-start.10) | collective-permute-done | bytes 49184 | tf_op jit(solution)/shard_map/ppermute | solution.py:294
  24.7 1.6 %collective-permute-done.8.refs_1_ = bf16[6,2,2048]{2,1,0:T(2,128)(2,1)S(1)} collective-permute-done((bf16[6,2,2048]{2,1,0:T(2,128)(2,1)S(1)}, bf16[6,2,2048]{2,1,0:T(2,128)(2,1)S(1)}, u32[]{:S(2)}, u32[]{:S(2)}) %collective-permute-start.8) | collective-permute-done | bytes 49184 | tf_op jit(solution)/shard_map/ppermute | solution.py:294
  26.3 0.5 %collective-permute-done.9.refs_2_ = bf16[6,2,2048]{2,1,0:T(2,128)(2,1)S(1)} collective-permute-done((bf16[6,2,2048]{2,1,0:T(2,128)(2,1)S(1)}, bf16[6,2,2048]{2,1,0:T(2,128)(2,1)S(1)}, u32[]{:S(2)}, u32[]{:S(2)}) %collective-permute-start.9) | collective-permute-done | bytes 49184 | tf_op jit(solution)/shard_map/ppermute | solution.py:294
  26.8 0.0 copy-done.3
  26.8 0.0 copy-done.5
  26.8 0.0 copy-done.6
  26.8 0.8 %residual_scores.1 = (bf16[6,2,2048]{2,1,0:T(2,128)(2,1)}, f32[6]{0:T(128)}) custom-call(bf16[6,2,2048]{2,1,0:T(2,128)(2,1)S(1)} %combine_project.1.refs_0_, bf16[6,2,2048]{2,1,0:T(2,128)(2,1)S(1)} %collective-permute-done.8.refs_1_, bf16[6,2,2048]{2,1,0:T(2,128)(2,1)S(1)} %collective-permute-done.9.refs_2_, ...), custom_call_target="tpu_custom_call" | custom-call | flops 1 | bytes 294912 | tf_op jit(solution)/shard_map/residual_scores/pallas_call | solution.py:397
  (1 shorter events, 0.0 us)
Async XLA Ops:
  0.6 10.0 %collective-permute-start.4 = (bf16[24,64,512]{2,1,0:T(8,128)(2,1)}, bf16[24,64,512]{2,1,0:T(8,128)(2,1)S(1)}, u32[]{:S(2)}, u32[]{:S(2)}) collective-permute-start(bf16[24,64,512]{2,1,0:T(8,128)(2,1)} %bitcast.24), channel_id=1, source_target_pairs={{0,1},{1,0},{2,3},{3,2},{4,5},{5,4},{6,7},{7,6},{8,9},{9,8},{10,11... | collective-permute-start | bytes 4718600 | tf_op jit(solution)/shard_map/ppermute | solution.py:294
  1.1 6.7 %collective-permute-start = (bf16[6,2,512]{2,1,0:T(2,128)(2,1)}, bf16[6,2,512]{2,1,0:T(2,128)(2,1)S(1)}, u32[]{:S(2)}, u32[]{:S(2)}) collective-permute-start(bf16[6,2,512]{2,1,0:T(2,128)(2,1)} %q_ref.3), channel_id=1, source_target_pairs={{0,4},{1,5},{2,6},{3,7},{4,0},{5,1},{6,2},{7,3},{8,12},{9,13},{10,... | collective-permute-start | bytes 36872 | tf_op jit(solution)/shard_map/ppermute | solution.py:294
  4.8 5.7 %collective-permute-start.1 = (bf16[6,2,512]{2,1,0:T(2,128)(2,1)}, bf16[6,2,512]{2,1,0:T(2,128)(2,1)S(1)}, u32[]{:S(2)}, u32[]{:S(2)}) collective-permute-start(bf16[6,2,512]{2,1,0:T(2,128)(2,1)} %q_ref.3), channel_id=1, source_target_pairs={{0,6},{1,7},{2,4},{3,5},{4,2},{5,3},{6,0},{7,1},{8,14},{9,15},{10,... | collective-permute-start | bytes 36872 | tf_op jit(solution)/shard_map/ppermute | solution.py:294
  6.2 4.4 %collective-permute-start.2 = (bf16[6,2,512]{2,1,0:T(2,128)(2,1)}, bf16[6,2,512]{2,1,0:T(2,128)(2,1)S(1)}, u32[]{:S(2)}, u32[]{:S(2)}) collective-permute-start(bf16[6,2,512]{2,1,0:T(2,128)(2,1)} %q_ref.3), channel_id=1, source_target_pairs={{0,2},{1,3},{2,0},{3,1},{4,6},{5,7},{6,4},{7,5},{8,10},{9,11},{10,... | collective-permute-start | bytes 36872 | tf_op jit(solution)/shard_map/ppermute | solution.py:294
  6.4 4.2 %collective-permute-start.3 = (s32[24]{0:T(128)}, s32[24]{0:T(128)S(1)}, u32[]{:S(2)}, u32[]{:S(2)}) collective-permute-start(s32[24]{0:T(128)} %page_hbm.1), channel_id=1, source_target_pairs={{0,1},{1,0},{2,3},{3,2},{4,5},{5,4},{6,7},{7,6},{8,9},{9,8},{10,11... | collective-permute-start | bytes 296 | tf_op jit(solution)/shard_map/ppermute | solution.py:294
  10.6 6.2 %copy-start.1 = (bf16[1,6,128,512]{3,2,1,0:T(8,128)(2,1)S(1)}, bf16[1,6,128,512]{3,2,1,0:T(8,128)(2,1)}, u32[]{:S(2)}) copy-start(bf16[1,6,128,512]{3,2,1,0:T(8,128)(2,1)} %param.17) | copy-start | bytes 2359300
  10.6 6.1 %copy-start.2 = (bf16[6,2,512]{2,1,0:T(2,128)(2,1)S(1)}, bf16[6,2,512]{2,1,0:T(2,128)(2,1)}, u32[]{:S(2)}) copy-start(bf16[6,2,512]{2,1,0:T(2,128)(2,1)} %q_ref.3) | copy-start | bytes 36868
  10.7 6.1 %copy-start.4 = (bf16[1,6,2,512]{3,2,1,0:T(2,128)(2,1)S(1)}, bf16[1,6,2,512]{3,2,1,0:T(2,128)(2,1)}, u32[]{:S(2)}) copy-start(bf16[1,6,2,512]{3,2,1,0:T(2,128)(2,1)} %param.19) | copy-start | bytes 36868
  10.7 6.1 %copy-start.7 = (s32[6]{0:T(128)S(1)}, s32[6]{0:T(128)}, u32[]{:S(2)}) copy-start(s32[6]{0:T(128)} %len_ref.1) | copy-start | bytes 76
  10.7 8.5 %copy-start = (bf16[512,2048]{1,0:T(8,128)(2,1)S(1)}, bf16[512,2048]{1,0:T(8,128)(2,1)}, u32[]{:S(2)}) copy-start(bf16[512,2048]{1,0:T(8,128)(2,1)} %refs_5_.1) | copy-start | bytes 6291460
  12.3 5.9 %collective-permute-start.5 = (bf16[32,384]{1,0:T(8,128)(2,1)S(1)}, bf16[32,384]{1,0:T(8,128)(2,1)S(1)}, u32[]{:S(2)}, u32[]{:S(2)}) collective-permute-start(bf16[32,384]{1,0:T(8,128)(2,1)S(1)} %get-tuple-element.14), channel_id=1, source_target_pairs={{0,6},{1,7},{2,4},{3,5},{4,2},{5,3},{6,0},{7,1},{8,14},{9,15},{10,... | collective-permute-start | bytes 73736 | tf_op jit(solution)/shard_map/ppermute | solution.py:294
  14.4 4.7 %collective-permute-start.6 = (bf16[32,384]{1,0:T(8,128)(2,1)S(1)}, bf16[32,384]{1,0:T(8,128)(2,1)S(1)}, u32[]{:S(2)}, u32[]{:S(2)}) collective-permute-start(bf16[32,384]{1,0:T(8,128)(2,1)S(1)} %get-tuple-element.13), channel_id=1, source_target_pairs={{0,4},{1,5},{2,6},{3,7},{4,0},{5,1},{6,2},{7,3},{8,12},{9,13},{10,... | collective-permute-start | bytes 73736 | tf_op jit(solution)/shard_map/ppermute | solution.py:294
  14.4 4.7 %collective-permute-start.7 = (bf16[32,384]{1,0:T(8,128)(2,1)S(1)}, bf16[32,384]{1,0:T(8,128)(2,1)S(1)}, u32[]{:S(2)}, u32[]{:S(2)}) collective-permute-start(bf16[32,384]{1,0:T(8,128)(2,1)S(1)} %get-tuple-element.12), channel_id=1, source_target_pairs={{0,2},{1,3},{2,0},{3,1},{4,6},{5,7},{6,4},{7,5},{8,10},{9,11},{10,... | collective-permute-start | bytes 73736 | tf_op jit(solution)/shard_map/ppermute | solution.py:294
  16.8 10.0 %copy-start.3 = (bf16[6,2,2048]{2,1,0:T(2,128)(2,1)S(1)}, bf16[6,2,2048]{2,1,0:T(2,128)(2,1)}, u32[]{:S(2)}) copy-start(bf16[6,2,2048]{2,1,0:T(2,128)(2,1)} %refs_4_.1) | copy-start | bytes 147460
  16.8 10.0 %copy-start.5 = (f32[2048]{0:T(1024)S(1)}, f32[2048]{0:T(1024)}, u32[]{:S(2)}) copy-start(f32[2048]{0:T(1024)} %param.22) | copy-start | bytes 24580
  16.8 10.0 %copy-start.6 = (f32[2048]{0:T(1024)S(1)}, f32[2048]{0:T(1024)}, u32[]{:S(2)}) copy-start(f32[2048]{0:T(1024)} %param.23) | copy-start | bytes 24580
  19.7 5.0 %collective-permute-start.10 = (bf16[6,2,2048]{2,1,0:T(2,128)(2,1)S(1)}, bf16[6,2,2048]{2,1,0:T(2,128)(2,1)S(1)}, u32[]{:S(2)}, u32[]{:S(2)}) collective-permute-start(bf16[6,2,2048]{2,1,0:T(2,128)(2,1)S(1)} %combine_project.1.refs_0_), channel_id=1, source_target_pairs={{0,24},{8,16},{16,8},{24,0},{1,25},{9,17},{17,9},{25,1},{2,26},{10... | collective-permute-start | bytes 147464 | tf_op jit(solution)/shard_map/ppermute | solution.py:294
  22.2 4.1 %collective-permute-start.8 = (bf16[6,2,2048]{2,1,0:T(2,128)(2,1)S(1)}, bf16[6,2,2048]{2,1,0:T(2,128)(2,1)S(1)}, u32[]{:S(2)}, u32[]{:S(2)}) collective-permute-start(bf16[6,2,2048]{2,1,0:T(2,128)(2,1)S(1)} %combine_project.1.refs_0_), channel_id=1, source_target_pairs={{0,8},{8,0},{16,24},{24,16},{1,9},{9,1},{17,25},{25,17},{2,10},{10... | collective-permute-start | bytes 147464 | tf_op jit(solution)/shard_map/ppermute | solution.py:294
  22.7 4.1 %collective-permute-start.9 = (bf16[6,2,2048]{2,1,0:T(2,128)(2,1)S(1)}, bf16[6,2,2048]{2,1,0:T(2,128)(2,1)S(1)}, u32[]{:S(2)}, u32[]{:S(2)}) collective-permute-start(bf16[6,2,2048]{2,1,0:T(2,128)(2,1)S(1)} %combine_project.1.refs_0_), channel_id=1, source_target_pairs={{0,16},{8,24},{16,0},{24,8},{1,17},{9,25},{17,1},{25,9},{2,18},{10... | collective-permute-start | bytes 147464 | tf_op jit(solution)/shard_map/ppermute | solution.py:294

commit v5 on v4

--- a/solution.py
+++ b/solution.py
@@ -8,8 +8,9 @@
 from jax.sharding import PartitionSpec as P
 
 SAMPLES = 16
+CHUNK = 6
 ORDER_A = (2, 3, 1)
-ORDER_B = (3, 2, 1)
+ORDER_B = (3, 1, 2)
 ORDER_C = (1, 2, 3)
 LANES = 128
 FLOOR = -(2.0**100)
@@ -37,12 +38,6 @@
 
 def rounded_peak(peak):
     return peak.astype(jnp.bfloat16).astype(jnp.float32)
-
-
-def softmax_parts(logits):
-    peak = rounded_peak(jnp.max(logits, axis=1, keepdims=True))
-    weights = jnp.exp2(logits - peak)
-    return peak, weights, jnp.sum(weights, axis=1, keepdims=True)
 
 
 def pack_stats(peak, den):
@@ -131,38 +126,52 @@
     return page * page_tokens + lane % page_tokens
 
 
-def prefix_kernel(heads, rows, scale, q_ref, low_ref, high_ref, *rest):
-    *both_refs, out_ref, q_rows = rest
+def prefix_kernel(heads, rows, scale, sources, parts_out, *refs):
+    q_refs, refs = refs[:sources], refs[sources:]
+    (low_ref, high_ref), refs = refs[:2], refs[2:]
+    both_refs, out_refs, q_rows = refs[:-parts_out - 1], refs[-parts_out - 1:-1], refs[-1]
     key_refs, pool_refs = both_refs[:len(both_refs) // 2], both_refs[len(both_refs) // 2:]
-    slots = q_ref.shape[0]
+    blocks = list(q_refs) if len(q_refs[0].shape) == 3 else [q_refs[0].at[j] for j in range(q_refs[0].shape[0])]
+    slots = len(blocks)
     pages, page_tokens, head_pair = pool_refs[0].shape
     head_size = head_pair // 2
-    keys = pages * page_tokens
-    for j in range(slots):
-        spread_rows(q_rows, j * heads * rows, q_ref.at[j], heads, head_size, rows)
+    for j, block in enumerate(blocks):
+        spread_rows(q_rows, j * heads * rows, block, heads, head_size, rows)
     low, high = low_ref[...], high_ref[...]
-    parts = []
+    queries = q_rows[...]
+    chunk = CHUNK if pages % CHUNK == 0 else pages
+    masked = []
     for key_ref, pool_ref in zip(key_refs, pool_refs):
-        logits = lax.dot_general(
-            q_rows[...], pool_ref[:, :, :head_size].reshape(keys, head_size),
-            (((1,), (1,)), ((), ())), preferred_element_type=jnp.float32,
-        )
-        for k in range(0, keys, LANES):
-            key = key_row(key_ref, k, page_tokens)
-            live = (key >= low) & (key < high)
-            parts.append(jnp.where(live, logits[:, k:k + LANES] * scale, FLOOR))
-    peak, weights, den = softmax_parts(jnp.concatenate(parts, axis=1))
-    weights = weights.astype(jnp.bfloat16)
-    num = sum(
-        jnp.dot(
-            weights[:, n * keys:(n + 1) * keys], pool_ref[:, :, head_size:].reshape(keys, head_size),
-            preferred_element_type=jnp.float32,
-        )
-        for n, pool_ref in enumerate(pool_refs)
-    )
+        for first in range(0, pages, chunk):
+            keys = pool_ref[first:first + chunk, :, :head_size].reshape(chunk * page_tokens, head_size)
+            logits = lax.dot_general(queries, keys, (((1,), (1,)), ((), ())), preferred_element_type=jnp.float32)
+            parts = []
+            for k in range(0, chunk * page_tokens, LANES):
+                key = key_row(key_ref, first * page_tokens + k, page_tokens)
+                live = (key >= low) & (key < high)
+                parts.append(jnp.where(live, logits[:, k:k + LANES] * scale, FLOOR))
+            masked.append((pool_ref, first, jnp.concatenate(parts, axis=1)))
+    num = den = peak = None
+    for pool_ref, first, logits in masked:
+        top = rounded_peak(jnp.max(logits, axis=1, keepdims=True))
+        if peak is not None:
+            top = jnp.maximum(top, peak)
+        weights = jnp.exp2(logits - top)
+        chunk_den = jnp.sum(weights, axis=1, keepdims=True)
+        values = pool_ref[first:first + chunk, :, head_size:].reshape(chunk * page_tokens, head_size)
+        chunk_num = jnp.dot(weights.astype(jnp.bfloat16), values, preferred_element_type=jnp.float32)
+        if peak is None:
+            num, den = chunk_num, chunk_den
+        else:
+            kept = jnp.exp2(peak - top)
+            num, den = num * kept + chunk_num, den * kept + chunk_den
+        peak = top
     per = heads * rows
-    out_ref[:, :, :head_size] = num.reshape(slots, per, head_size).astype(out_ref.dtype)
-    out_ref[:, :, head_size:] = pack_stats(peak, den).reshape(slots, per, LANES).astype(out_ref.dtype)
+    stats = pack_stats(peak, den)
+    outs = list(out_refs) if len(out_refs[0].shape) == 2 else [out_refs[0].at[j] for j in range(slots)]
+    for j, out_ref in enumerate(outs):
+        out_ref[:, :head_size] = num[j * per:(j + 1) * per].astype(out_ref.dtype)
+        out_ref[:, head_size:] = stats[j * per:(j + 1) * per].astype(out_ref.dtype)
 
 
 def own_kernel(heads, rows, scale, len_ref, q_ref, tail_ref, fresh_ref, out_ref, q_rows, f_rows):
@@ -289,12 +298,13 @@
     paired = blk in (2, 4, 8)
     half = blk // 2
     partners = [0] + [j for j in ORDER_A if j < half]
+    masks = [0] + [2 * j + 1 for j in partners[1:]]
 
     def swap(x, axis, size, mask):
         return lax.ppermute(x, axis, [(i, i ^ mask) for i in range(size)])
 
     def device_of(j, me):
-        return me ^ (partners[j] * 2) if paired else j
+        return me ^ masks[j] if paired else j
 
     slots = half if paired else blk
     pools = [pool]
@@ -343,31 +353,48 @@
         name="own_keys",
     )(tail_len, queries, tail_cache[0], new_kv[0])
 
-    def prefix(block):
-        slots = block.shape[0]
+    block_shape = jax.ShapeDtypeStruct((per, head_size + LANES), jnp.bfloat16)
+    scratch = [pltpu.VMEM((min(slots, 4) * per, head_size), jnp.bfloat16)]
+    price = cost(4 * slots * per * keys * len(pools) * head_size, 2 * pool.size * len(pools))
+
+    def prefix_column(blocks):
+        return pl.pallas_call(
+            functools.partial(prefix_kernel, heads, rows, scale, slots, slots),
+            out_shape=(block_shape,) * slots,
+            in_specs=[VMEM] * (slots + 2 + 2 * len(pools)),
+            out_specs=(VMEM,) * slots,
+            scratch_shapes=scratch,
+            compiler_params=vmem(24),
+            cost_estimate=price,
+            name="prefix_keys",
+        )(*blocks, low, high, *key_lists, *pools)
+
+    def prefix_many(block):
         step = min(slots, 4)
         return pl.pallas_call(
-            functools.partial(prefix_kernel, heads, rows, scale),
-            out_shape=jax.ShapeDtypeStruct((slots, per, head_size + LANES), jnp.bfloat16),
+            functools.partial(prefix_kernel, heads, rows, scale, 1, 1),
+            out_shape=jax.ShapeDtypeStruct((slots,) + block_shape.shape, jnp.bfloat16),
             grid=(slots // step,),
             in_specs=[
                 pl.BlockSpec((step, local, drafts, head_width), lambda i: (i, 0, 0, 0)),
                 pl.BlockSpec((step * per, LANES), lambda i: (i, 0)),
                 pl.BlockSpec((step * per, LANES), lambda i: (i, 0)),
-            ] + [pl.BlockSpec(k.shape, lambda i: (0, 0)) for k in key_lists] + [pl.BlockSpec((page_count, page_tokens, head_pair), lambda i: (0, 0, 0))] * len(pools),
-            out_specs=pl.BlockSpec((step, per, head_size + LANES), lambda i: (i, 0, 0)),
-            scratch_shapes=[pltpu.VMEM((step * per, head_size), jnp.bfloat16)],
+                pl.BlockSpec((8, keys), lambda i: (0, 0)),
+                pl.BlockSpec((page_count, page_tokens, head_pair), lambda i: (0, 0, 0)),
+            ],
+            out_specs=pl.BlockSpec((step,) + block_shape.shape, lambda i: (i, 0, 0)),
+            scratch_shapes=scratch,
             compiler_params=vmem(24),
-            cost_estimate=cost(4 * slots * per * keys * len(pools) * head_size, 2 * pool.size * len(pools)),
+            cost_estimate=price,
             name="prefix_keys",
         )(block, low, high, *key_lists, *pools)
 
     partial_shape = jax.ShapeDtypeStruct((local, drafts, width), jnp.bfloat16)
     if paired:
-        column = [near_queries] + [swap(queries, "blk", blk, 2 * j) for j in partners[1:]]
-        sums = prefix(jnp.stack(column))
+        column = [near_queries] + [swap(queries, "blk", blk, mask) for mask in masks[1:]]
+        sums = prefix_column(column)
         blocks = [sums[0]] + [
-            swap(sums[partners.index(j)], "blk", blk, 2 * j) for j in ORDER_B if j < half
+            swap(sums[partners.index(j)], "blk", blk, 2 * j + 1) for j in ORDER_B if j < half
         ]
         share = pl.pallas_call(
             functools.partial(combine_kernel, heads, rows, head_size),
@@ -380,7 +407,7 @@
         )(own, *blocks, out_weight)
     else:
         gathered = lax.all_gather(queries, "blk", axis=0)
-        blocks = lax.all_to_all(prefix(gathered), "blk", 0, 0)
+        blocks = lax.all_to_all(prefix_many(gathered), "blk", 0, 0)
         share = pl.pallas_call(
             functools.partial(combine_many_kernel, heads, rows, head_size),
             out_shape=partial_shape,

time: 27.7 us -> 25.8 us (0.931)
  waiting for transfers between devices: 7.48 us -> 6.5 us
  Pallas kernels: 5.43 us -> 5.02 us
  starting transfers between devices: 13.8 us -> 13.4 us
    ppermute x11, waiting for transfers between devices: 7.48 us -> 6.5 us  [swap(): return lax.ppermute(x, axis, [(i, i ^ mask) for i in range(size)])]
    pallas_call x1, Pallas kernels: 1.61 us -> 1.2 us  [prefix_column(): pl.pallas_call(functools.partial(prefix_kernel, heads, rows, scale, slots...]
    ppermute x11, starting transfers between devices: 13.8 us -> 13.4 us  [swap(): return lax.ppermute(x, axis, [(i, i ^ mask) for i in range(size)])]
  transfers between devices with their start and end apart: 11 -> 11, of which waited for: 6 -> 7; matrix products, arithmetic and copies ran while one was open for 0% -> 0% of each run, Pallas kernels for 9% -> 10%
where the time goes in v5:
time: 25.8 us; the launch traced here: 25.7 us
  starting transfers between devices  13.4 us (52%)
  waiting for transfers between devices  6.5 us (25%)
  Pallas kernels  5.02 us (19%)
  between operations  0.74 us (3%)
    ppermute x11, starting transfers between devices, swap(): return lax.ppermute(x, axis, [(i, i ^ mask) for i in range(size)])  13.4 us
    ppermute x11, waiting for transfers between devices, swap(): return lax.ppermute(x, axis, [(i, i ^ mask) for i in range(size)])  6.5 us
    pallas_call x1, Pallas kernels, body(): pl.pallas_call(functools.partial(layout_kernel, device_of, slots, local,...  1.45 us
    pallas_call x1, Pallas kernels, prefix_column(): pl.pallas_call(functools.partial(prefix_kernel, heads, rows, scale, slots...  1.2 us
    pallas_call x1, Pallas kernels, body(): pl.pallas_call(functools.partial(own_kernel, heads, rows, scale), out_sha...  1.08 us
    pallas_call x1, Pallas kernels, body(): pl.pallas_call(final_kernel, out_shape=(jax.ShapeDtypeStruct(hidden.shape...  0.77 us
    pallas_call x1, Pallas kernels, body(): pl.pallas_call(functools.partial(combine_kernel, heads, rows, head_size),...  0.52 us
  transfers between devices with their start and end apart: 11, of which 7 were waited for; matrix products, arithmetic and copies ran while one was open for 0% of the time, Pallas kernels for 10%

profile of v5, /device:TPU:0, one launch (start us, length us, event | category | flops | bytes accessed | tf_op | source)
XLA Modules:
  0.0 25.7 jit_solution(198654617455662313)
XLA Ops:
  0.6 0.5 %collective-permute-start.4 = (bf16[24,64,512]{2,1,0:T(8,128)(2,1)}, bf16[24,64,512]{2,1,0:T(8,128)(2,1)S(1)}, u32[]{:S(2)}, u32[]{:S(2)}) collective-permute-start(bf16[24,64,512]{2,1,0:T(8,128)(2,1)} %bitcast.11), channel_id=1, source_target_pairs={{0,1},{1,0},{2,3},{3,2},{4,5},{5,4},{6,7},{7,6},{8,9},{9,8},{10,11... | collective-permute-start | bytes 4718600 | tf_op jit(solution)/shard_map/ppermute | solution.py:304
  1.1 3.7 %collective-permute-start = (bf16[6,2,512]{2,1,0:T(2,128)(2,1)}, bf16[6,2,512]{2,1,0:T(2,128)(2,1)S(1)}, u32[]{:S(2)}, u32[]{:S(2)}) collective-permute-start(bf16[6,2,512]{2,1,0:T(2,128)(2,1)} %q_ref.3), channel_id=1, source_target_pairs={{0,5},{1,4},{2,7},{3,6},{4,1},{5,0},{6,3},{7,2},{8,13},{9,12},{10,... | collective-permute-start | bytes 36872 | tf_op jit(solution)/shard_map/ppermute | solution.py:304
  4.9 1.0 %collective-permute-start.1 = (bf16[6,2,512]{2,1,0:T(2,128)(2,1)}, bf16[6,2,512]{2,1,0:T(2,128)(2,1)S(1)}, u32[]{:S(2)}, u32[]{:S(2)}) collective-permute-start(bf16[6,2,512]{2,1,0:T(2,128)(2,1)} %q_ref.3), channel_id=1, source_target_pairs={{0,7},{1,6},{2,5},{3,4},{4,3},{5,2},{6,1},{7,0},{8,15},{9,14},{10,... | collective-permute-start | bytes 36872 | tf_op jit(solution)/shard_map/ppermute | solution.py:304
  5.9 0.2 collective-permute-start.2
  6.1 0.4 %collective-permute-start.3 = (s32[24]{0:T(128)}, s32[24]{0:T(128)S(1)}, u32[]{:S(2)}, u32[]{:S(2)}) collective-permute-start(s32[24]{0:T(128)} %page_hbm.1), channel_id=1, source_target_pairs={{0,1},{1,0},{2,3},{3,2},{4,5},{5,4},{6,7},{7,6},{8,9},{9,8},{10,11... | collective-permute-start | bytes 296 | tf_op jit(solution)/shard_map/ppermute | solution.py:304
  6.6 1.5 %key_ranges.1 = (s32[128,128]{1,0:T(8,128)S(1)}, s32[128,128]{1,0:T(8,128)S(1)}, s32[8,1536]{1,0:T(8,128)S(1)}, bf16[6,2,512]{2,1,0:T(2,128)(2,1)S(1)}, bf16[24,64,512]{2,1,0:T(8,128)(2,1)S(1)}) custom-call(s32[48]{0:T(128)} %ids_hbm.1, s32[3]{0:T(128)} %len_hbm.1, s32[24]{0:T(128)} %page_hbm.1, bf16[6,2,512]{2,1,0:T(2,128)(2,1)} %q_ref.3, ...), custom_call_target="tpu_custom_call" | custom-call | flops 1 | bytes 131072 | tf_op jit(solution)/shard_map/key_ranges/pallas_call | solution.py:316
  8.0 0.0 collective-permute-done.3
  8.0 0.0 collective-permute-done.refs_1_
  8.0 1.9 %collective-permute-done.1.refs_2_ = bf16[6,2,512]{2,1,0:T(2,128)(2,1)S(1)} collective-permute-done((bf16[6,2,512]{2,1,0:T(2,128)(2,1)}, bf16[6,2,512]{2,1,0:T(2,128)(2,1)S(1)}, u32[]{:S(2)}, u32[]{:S(2)}) %collective-permute-start.1) | collective-permute-done | bytes 12320 | tf_op jit(solution)/shard_map/ppermute | solution.py:304
  10.0 0.0 collective-permute-done.2.refs_3_
  10.0 0.0 collective-permute-done.4.refs_9_
  10.0 0.0 copy-start.1
  10.0 0.0 copy-start.2
  10.0 0.0 copy-start.4
  10.0 0.0 copy-start.7
  10.0 0.0 copy-start
  10.1 1.2 %prefix_keys.1 = (bf16[32,384]{1,0:T(8,128)(2,1)S(1)}, bf16[32,384]{1,0:T(8,128)(2,1)S(1)}, bf16[32,384]{1,0:T(8,128)(2,1)S(1)}, bf16[32,384]{1,0:T(8,128)(2,1)S(1)}) custom-call(bf16[6,2,512]{2,1,0:T(2,128)(2,1)S(1)} %get-tuple-element.11.refs_0_, bf16[6,2,512]{2,1,0:T(2,128)(2,1)S(1)} %collective-permute-done.refs_1_, ...), custom_call_target="tpu_custom_call" | custom-call | flops 402653184 | bytes 3145728 | tf_op jit(solution)/shard_map/prefix_keys/pallas_call | solution.py:361
  11.3 1.8 %collective-permute-start.5 = (bf16[32,384]{1,0:T(8,128)(2,1)S(1)}, bf16[32,384]{1,0:T(8,128)(2,1)S(1)}, u32[]{:S(2)}, u32[]{:S(2)}) collective-permute-start(bf16[32,384]{1,0:T(8,128)(2,1)S(1)} %get-tuple-element.17), channel_id=1, source_target_pairs={{0,7},{1,6},{2,5},{3,4},{4,3},{5,2},{6,1},{7,0},{8,15},{9,14},{10,... | collective-permute-start | bytes 73736 | tf_op jit(solution)/shard_map/ppermute | solution.py:304
  13.1 0.0 collective-permute-start.6
  13.1 2.1 %collective-permute-start.7 = (bf16[32,384]{1,0:T(8,128)(2,1)S(1)}, bf16[32,384]{1,0:T(8,128)(2,1)S(1)}, u32[]{:S(2)}, u32[]{:S(2)}) collective-permute-start(bf16[32,384]{1,0:T(8,128)(2,1)S(1)} %get-tuple-element.19), channel_id=1, source_target_pairs={{0,5},{1,4},{2,7},{3,6},{4,1},{5,0},{6,3},{7,2},{8,13},{9,12},{10,... | collective-permute-start | bytes 73736 | tf_op jit(solution)/shard_map/ppermute | solution.py:304
  15.2 0.0 copy-done.1
  15.2 0.0 copy-done.2
  15.2 0.0 copy-done.4
  15.2 0.0 copy-done.7
  15.2 0.0 copy-start.3
  15.2 0.0 copy-start.5
  15.2 0.0 copy-start.6
  15.2 1.1 %own_keys.1.refs_0_ = f32[32,384]{1,0:T(8,128)S(1)} custom-call(s32[6]{0:T(128)S(1)} %copy-done.7, bf16[6,2,512]{2,1,0:T(2,128)(2,1)S(1)} %copy-done.2, bf16[6,128,512]{2,1,0:T(8,128)(2,1)S(1)} %bitcast.6, bf16[6,2,512]{2,1,0:T(2,128)(2,1)S(1)} %bitcast.7), custom_call_target="tpu_custom_call" | custom-call | flops 25165824 | bytes 786432 | tf_op jit(solution)/shard_map/own_keys/pallas_call | solution.py:342
  16.3 0.2 collective-permute-done.5.refs_2_
  16.5 0.4 %collective-permute-done.6.refs_3_ = bf16[32,384]{1,0:T(8,128)(2,1)S(1)} collective-permute-done((bf16[32,384]{1,0:T(8,128)(2,1)S(1)}, bf16[32,384]{1,0:T(8,128)(2,1)S(1)}, u32[]{:S(2)}, u32[]{:S(2)}) %collective-permute-start.6) | collective-permute-done | bytes 24608 | tf_op jit(solution)/shard_map/ppermute | solution.py:304
  16.9 0.3 %collective-permute-done.7.refs_4_ = bf16[32,384]{1,0:T(8,128)(2,1)S(1)} collective-permute-done((bf16[32,384]{1,0:T(8,128)(2,1)S(1)}, bf16[32,384]{1,0:T(8,128)(2,1)S(1)}, u32[]{:S(2)}, u32[]{:S(2)}) %collective-permute-start.7) | collective-permute-done | bytes 24608 | tf_op jit(solution)/shard_map/ppermute | solution.py:304
  17.2 0.0 copy-done
  17.2 0.5 %combine_project.1.refs_0_ = bf16[6,2,2048]{2,1,0:T(2,128)(2,1)S(1)} custom-call(f32[32,384]{1,0:T(8,128)S(1)} %own_keys.1.refs_0_, bf16[32,384]{1,0:T(8,128)(2,1)S(1)} %get-tuple-element.16.refs_1_, bf16[32,384]{1,0:T(8,128)(2,1)S(1)} %collective-permute-done.5.refs_2_, bf16[32,384]{1,0:T(8,128)(2,1)S(1)} %collective-permute-done.6.refs_3_, ...), custom_call_target="tpu_custom_call" | custom-call | flops 33554432 | bytes 2097152 | tf_op jit(solution)/shard_map/combine_project/pallas_call | solution.py:399
  17.8 2.5 %collective-permute-start.10 = (bf16[6,2,2048]{2,1,0:T(2,128)(2,1)S(1)}, bf16[6,2,2048]{2,1,0:T(2,128)(2,1)S(1)}, u32[]{:S(2)}, u32[]{:S(2)}) collective-permute-start(bf16[6,2,2048]{2,1,0:T(2,128)(2,1)S(1)} %combine_project.1.refs_0_), channel_id=1, source_target_pairs={{0,24},{8,16},{16,8},{24,0},{1,25},{9,17},{17,9},{25,1},{2,26},{10... | collective-permute-start | bytes 147464 | tf_op jit(solution)/shard_map/ppermute | solution.py:304
  20.3 0.5 %collective-permute-start.8 = (bf16[6,2,2048]{2,1,0:T(2,128)(2,1)S(1)}, bf16[6,2,2048]{2,1,0:T(2,128)(2,1)S(1)}, u32[]{:S(2)}, u32[]{:S(2)}) collective-permute-start(bf16[6,2,2048]{2,1,0:T(2,128)(2,1)S(1)} %combine_project.1.refs_0_), channel_id=1, source_target_pairs={{0,8},{8,0},{16,24},{24,16},{1,9},{9,1},{17,25},{25,17},{2,10},{10... | collective-permute-start | bytes 147464 | tf_op jit(solution)/shard_map/ppermute | solution.py:304
  20.8 0.5 %collective-permute-start.9 = (bf16[6,2,2048]{2,1,0:T(2,128)(2,1)S(1)}, bf16[6,2,2048]{2,1,0:T(2,128)(2,1)S(1)}, u32[]{:S(2)}, u32[]{:S(2)}) collective-permute-start(bf16[6,2,2048]{2,1,0:T(2,128)(2,1)S(1)} %combine_project.1.refs_0_), channel_id=1, source_target_pairs={{0,16},{8,24},{16,0},{24,8},{1,17},{9,25},{17,1},{25,9},{2,18},{10... | collective-permute-start | bytes 147464 | tf_op jit(solution)/shard_map/ppermute | solution.py:304
  21.3 1.6 %collective-permute-done.10.refs_3_ = bf16[6,2,2048]{2,1,0:T(2,128)(2,1)S(1)} collective-permute-done((bf16[6,2,2048]{2,1,0:T(2,128)(2,1)S(1)}, bf16[6,2,2048]{2,1,0:T(2,128)(2,1)S(1)}, u32[]{:S(2)}, u32[]{:S(2)}) %collective-permute-start.10) | collective-permute-done | bytes 49184 | tf_op jit(solution)/shard_map/ppermute | solution.py:304
  22.9 1.4 %collective-permute-done.8.refs_1_ = bf16[6,2,2048]{2,1,0:T(2,128)(2,1)S(1)} collective-permute-done((bf16[6,2,2048]{2,1,0:T(2,128)(2,1)S(1)}, bf16[6,2,2048]{2,1,0:T(2,128)(2,1)S(1)}, u32[]{:S(2)}, u32[]{:S(2)}) %collective-permute-start.8) | collective-permute-done | bytes 49184 | tf_op jit(solution)/shard_map/ppermute | solution.py:304
  24.3 0.5 %collective-permute-done.9.refs_2_ = bf16[6,2,2048]{2,1,0:T(2,128)(2,1)S(1)} collective-permute-done((bf16[6,2,2048]{2,1,0:T(2,128)(2,1)S(1)}, bf16[6,2,2048]{2,1,0:T(2,128)(2,1)S(1)}, u32[]{:S(2)}, u32[]{:S(2)}) %collective-permute-start.9) | collective-permute-done | bytes 49184 | tf_op jit(solution)/shard_map/ppermute | solution.py:304
  24.9 0.0 copy-done.3
  24.9 0.0 copy-done.5
  24.9 0.0 copy-done.6
  24.9 0.8 %residual_scores.1 = (bf16[6,2,2048]{2,1,0:T(2,128)(2,1)}, f32[6]{0:T(128)}) custom-call(bf16[6,2,2048]{2,1,0:T(2,128)(2,1)S(1)} %combine_project.1.refs_0_, bf16[6,2,2048]{2,1,0:T(2,128)(2,1)S(1)} %collective-permute-done.8.refs_1_, bf16[6,2,2048]{2,1,0:T(2,128)(2,1)S(1)} %collective-permute-done.9.refs_2_, ...), custom_call_target="tpu_custom_call" | custom-call | flops 1 | bytes 294912 | tf_op jit(solution)/shard_map/residual_scores/pallas_call | solution.py:424
Async XLA Ops:
  0.6 9.4 %collective-permute-start.4 = (bf16[24,64,512]{2,1,0:T(8,128)(2,1)}, bf16[24,64,512]{2,1,0:T(8,128)(2,1)S(1)}, u32[]{:S(2)}, u32[]{:S(2)}) collective-permute-start(bf16[24,64,512]{2,1,0:T(8,128)(2,1)} %bitcast.11), channel_id=1, source_target_pairs={{0,1},{1,0},{2,3},{3,2},{4,5},{5,4},{6,7},{7,6},{8,9},{9,8},{10,11... | collective-permute-start | bytes 4718600 | tf_op jit(solution)/shard_map/ppermute | solution.py:304
  1.1 6.9 %collective-permute-start = (bf16[6,2,512]{2,1,0:T(2,128)(2,1)}, bf16[6,2,512]{2,1,0:T(2,128)(2,1)S(1)}, u32[]{:S(2)}, u32[]{:S(2)}) collective-permute-start(bf16[6,2,512]{2,1,0:T(2,128)(2,1)} %q_ref.3), channel_id=1, source_target_pairs={{0,5},{1,4},{2,7},{3,6},{4,1},{5,0},{6,3},{7,2},{8,13},{9,12},{10,... | collective-permute-start | bytes 36872 | tf_op jit(solution)/shard_map/ppermute | solution.py:304
  4.9 5.1 %collective-permute-start.1 = (bf16[6,2,512]{2,1,0:T(2,128)(2,1)}, bf16[6,2,512]{2,1,0:T(2,128)(2,1)S(1)}, u32[]{:S(2)}, u32[]{:S(2)}) collective-permute-start(bf16[6,2,512]{2,1,0:T(2,128)(2,1)} %q_ref.3), channel_id=1, source_target_pairs={{0,7},{1,6},{2,5},{3,4},{4,3},{5,2},{6,1},{7,0},{8,15},{9,14},{10,... | collective-permute-start | bytes 36872 | tf_op jit(solution)/shard_map/ppermute | solution.py:304
  5.9 4.1 %collective-permute-start.2 = (bf16[6,2,512]{2,1,0:T(2,128)(2,1)}, bf16[6,2,512]{2,1,0:T(2,128)(2,1)S(1)}, u32[]{:S(2)}, u32[]{:S(2)}) collective-permute-start(bf16[6,2,512]{2,1,0:T(2,128)(2,1)} %q_ref.3), channel_id=1, source_target_pairs={{0,3},{1,2},{2,1},{3,0},{4,7},{5,6},{6,5},{7,4},{8,11},{9,10},{10,... | collective-permute-start | bytes 36872 | tf_op jit(solution)/shard_map/ppermute | solution.py:304
  6.1 1.9 %collective-permute-start.3 = (s32[24]{0:T(128)}, s32[24]{0:T(128)S(1)}, u32[]{:S(2)}, u32[]{:S(2)}) collective-permute-start(s32[24]{0:T(128)} %page_hbm.1), channel_id=1, source_target_pairs={{0,1},{1,0},{2,3},{3,2},{4,5},{5,4},{6,7},{7,6},{8,9},{9,8},{10,11... | collective-permute-start | bytes 296 | tf_op jit(solution)/shard_map/ppermute | solution.py:304
  10.0 5.2 %copy-start.1 = (bf16[1,6,128,512]{3,2,1,0:T(8,128)(2,1)S(1)}, bf16[1,6,128,512]{3,2,1,0:T(8,128)(2,1)}, u32[]{:S(2)}) copy-start(bf16[1,6,128,512]{3,2,1,0:T(8,128)(2,1)} %param.17) | copy-start | bytes 2359300
  10.0 5.2 %copy-start.2 = (bf16[6,2,512]{2,1,0:T(2,128)(2,1)S(1)}, bf16[6,2,512]{2,1,0:T(2,128)(2,1)}, u32[]{:S(2)}) copy-start(bf16[6,2,512]{2,1,0:T(2,128)(2,1)} %q_ref.3) | copy-start | bytes 36868
  10.0 5.1 %copy-start.4 = (bf16[1,6,2,512]{3,2,1,0:T(2,128)(2,1)S(1)}, bf16[1,6,2,512]{3,2,1,0:T(2,128)(2,1)}, u32[]{:S(2)}) copy-start(bf16[1,6,2,512]{3,2,1,0:T(2,128)(2,1)} %param.19) | copy-start | bytes 36868
  10.0 5.1 %copy-start.7 = (s32[6]{0:T(128)S(1)}, s32[6]{0:T(128)}, u32[]{:S(2)}) copy-start(s32[6]{0:T(128)} %len_ref.1) | copy-start | bytes 76
  10.0 7.2 %copy-start = (bf16[512,2048]{1,0:T(8,128)(2,1)S(1)}, bf16[512,2048]{1,0:T(8,128)(2,1)}, u32[]{:S(2)}) copy-start(bf16[512,2048]{1,0:T(8,128)(2,1)} %refs_5_.1) | copy-start | bytes 6291460
  11.3 5.2 %collective-permute-start.5 = (bf16[32,384]{1,0:T(8,128)(2,1)S(1)}, bf16[32,384]{1,0:T(8,128)(2,1)S(1)}, u32[]{:S(2)}, u32[]{:S(2)}) collective-permute-start(bf16[32,384]{1,0:T(8,128)(2,1)S(1)} %get-tuple-element.17), channel_id=1, source_target_pairs={{0,7},{1,6},{2,5},{3,4},{4,3},{5,2},{6,1},{7,0},{8,15},{9,14},{10,... | collective-permute-start | bytes 73736 | tf_op jit(solution)/shard_map/ppermute | solution.py:304
  13.1 3.9 %collective-permute-start.6 = (bf16[32,384]{1,0:T(8,128)(2,1)S(1)}, bf16[32,384]{1,0:T(8,128)(2,1)S(1)}, u32[]{:S(2)}, u32[]{:S(2)}) collective-permute-start(bf16[32,384]{1,0:T(8,128)(2,1)S(1)} %get-tuple-element.18), channel_id=1, source_target_pairs={{0,3},{1,2},{2,1},{3,0},{4,7},{5,6},{6,5},{7,4},{8,11},{9,10},{10,... | collective-permute-start | bytes 73736 | tf_op jit(solution)/shard_map/ppermute | solution.py:304
  13.1 4.2 %collective-permute-start.7 = (bf16[32,384]{1,0:T(8,128)(2,1)S(1)}, bf16[32,384]{1,0:T(8,128)(2,1)S(1)}, u32[]{:S(2)}, u32[]{:S(2)}) collective-permute-start(bf16[32,384]{1,0:T(8,128)(2,1)S(1)} %get-tuple-element.19), channel_id=1, source_target_pairs={{0,5},{1,4},{2,7},{3,6},{4,1},{5,0},{6,3},{7,2},{8,13},{9,12},{10,... | collective-permute-start | bytes 73736 | tf_op jit(solution)/shard_map/ppermute | solution.py:304
  15.2 9.7 %copy-start.3 = (bf16[6,2,2048]{2,1,0:T(2,128)(2,1)S(1)}, bf16[6,2,2048]{2,1,0:T(2,128)(2,1)}, u32[]{:S(2)}) copy-start(bf16[6,2,2048]{2,1,0:T(2,128)(2,1)} %refs_4_.1) | copy-start | bytes 147460
  15.2 9.7 %copy-start.5 = (f32[2048]{0:T(1024)S(1)}, f32[2048]{0:T(1024)}, u32[]{:S(2)}) copy-start(f32[2048]{0:T(1024)} %param.22) | copy-start | bytes 24580
  15.2 9.7 %copy-start.6 = (f32[2048]{0:T(1024)S(1)}, f32[2048]{0:T(1024)}, u32[]{:S(2)}) copy-start(f32[2048]{0:T(1024)} %param.23) | copy-start | bytes 24580
  17.8 5.2 %collective-permute-start.10 = (bf16[6,2,2048]{2,1,0:T(2,128)(2,1)S(1)}, bf16[6,2,2048]{2,1,0:T(2,128)(2,1)S(1)}, u32[]{:S(2)}, u32[]{:S(2)}) collective-permute-start(bf16[6,2,2048]{2,1,0:T(2,128)(2,1)S(1)} %combine_project.1.refs_0_), channel_id=1, source_target_pairs={{0,24},{8,16},{16,8},{24,0},{1,25},{9,17},{17,9},{25,1},{2,26},{10... | collective-permute-start | bytes 147464 | tf_op jit(solution)/shard_map/ppermute | solution.py:304
  20.3 4.1 %collective-permute-start.8 = (bf16[6,2,2048]{2,1,0:T(2,128)(2,1)S(1)}, bf16[6,2,2048]{2,1,0:T(2,128)(2,1)S(1)}, u32[]{:S(2)}, u32[]{:S(2)}) collective-permute-start(bf16[6,2,2048]{2,1,0:T(2,128)(2,1)S(1)} %combine_project.1.refs_0_), channel_id=1, source_target_pairs={{0,8},{8,0},{16,24},{24,16},{1,9},{9,1},{17,25},{25,17},{2,10},{10... | collective-permute-start | bytes 147464 | tf_op jit(solution)/shard_map/ppermute | solution.py:304
  20.8 4.1 %collective-permute-start.9 = (bf16[6,2,2048]{2,1,0:T(2,128)(2,1)S(1)}, bf16[6,2,2048]{2,1,0:T(2,128)(2,1)S(1)}, u32[]{:S(2)}, u32[]{:S(2)}) collective-permute-start(bf16[6,2,2048]{2,1,0:T(2,128)(2,1)S(1)} %combine_project.1.refs_0_), channel_id=1, source_target_pairs={{0,16},{8,24},{16,0},{24,8},{1,17},{9,25},{17,1},{25,9},{2,18},{10... | collective-permute-start | bytes 147464 | tf_op jit(solution)/shard_map/ppermute | solution.py:304

commit v6 on v5

--- a/solution.py
+++ b/solution.py
@@ -8,7 +8,7 @@
 from jax.sharding import PartitionSpec as P
 
 SAMPLES = 16
-CHUNK = 6
+CHUNK = 8
 ORDER_A = (2, 3, 1)
 ORDER_B = (3, 1, 2)
 ORDER_C = (1, 2, 3)
@@ -70,10 +70,10 @@
 
 
 def layout_kernel(device_of, slots, local, rows, heads, drafts, page_tokens,
-                  ids_hbm, len_hbm, page_hbm, q_ref, pool_ref,
-                  low_ref, high_ref, key_ref, q_out_ref, pool_out_ref,
+                  ids_hbm, len_hbm, page_hbm, q_ref,
+                  low_ref, high_ref, key_ref, q_out_ref,
                   ids_ref, len_ref, page_ref, start_ref, sems):
-    pairs = [(ids_hbm, ids_ref), (len_hbm, len_ref), (page_hbm, page_ref), (pool_ref, pool_out_ref), (q_ref, q_out_ref)]
+    pairs = [(ids_hbm, ids_ref), (len_hbm, len_ref), (page_hbm, page_ref), (q_ref, q_out_ref)]
     copies = [pltpu.make_async_copy(a, b, sems.at[i]) for i, (a, b) in enumerate(pairs)]
     for copy in copies:
         copy.start()
@@ -115,22 +115,23 @@
         copy.wait()
 
 
-def key_row(ref, at, page_tokens):
-    if ref.shape[0] > 1:
-        return ref[0:1, at:at + LANES]
-    lane = iota((1, LANES), 1)
-    first = at // page_tokens
-    page = ref[:, first:first + 1]
-    for n in range(1, LANES // page_tokens):
-        page = jnp.where(lane >= n * page_tokens, ref[:, first + n:first + n + 1], page)
-    return page * page_tokens + lane % page_tokens
+def flip_kernel(page_tokens, *refs):
+    pools = 2 if len(refs) == 6 else 1
+    page_refs, pool_refs, key_refs, flip_refs = refs[:pools - 1], refs[pools - 1:2 * pools - 1], refs[2 * pools - 1:-pools], refs[-pools:]
+    for page_ref, key_ref in zip(page_refs, key_refs):
+        write_keys(page_ref, key_ref, page_tokens)
+    for pool_ref, flip_ref in zip(pool_refs, flip_refs):
+        pages, tokens, head_pair = pool_ref.shape
+        keys = pool_ref[:, :, :head_pair // 2].reshape(pages * tokens, head_pair // 2)
+        flip_ref[...] = keys.T
 
 
 def prefix_kernel(heads, rows, scale, sources, parts_out, *refs):
     q_refs, refs = refs[:sources], refs[sources:]
     (low_ref, high_ref), refs = refs[:2], refs[2:]
     both_refs, out_refs, q_rows = refs[:-parts_out - 1], refs[-parts_out - 1:-1], refs[-1]
-    key_refs, pool_refs = both_refs[:len(both_refs) // 2], both_refs[len(both_refs) // 2:]
+    count = len(both_refs) // 3
+    key_refs, flip_refs, pool_refs = both_refs[:count], both_refs[count:2 * count], both_refs[2 * count:]
     blocks = list(q_refs) if len(q_refs[0].shape) == 3 else [q_refs[0].at[j] for j in range(q_refs[0].shape[0])]
     slots = len(blocks)
     pages, page_tokens, head_pair = pool_refs[0].shape
@@ -141,13 +142,13 @@
     queries = q_rows[...]
     chunk = CHUNK if pages % CHUNK == 0 else pages
     masked = []
-    for key_ref, pool_ref in zip(key_refs, pool_refs):
+    for key_ref, flip_ref, pool_ref in zip(key_refs, flip_refs, pool_refs):
         for first in range(0, pages, chunk):
-            keys = pool_ref[first:first + chunk, :, :head_size].reshape(chunk * page_tokens, head_size)
-            logits = lax.dot_general(queries, keys, (((1,), (1,)), ((), ())), preferred_element_type=jnp.float32)
+            at = first * page_tokens
+            logits = jnp.dot(queries, flip_ref[:, at:at + chunk * page_tokens], preferred_element_type=jnp.float32)
             parts = []
             for k in range(0, chunk * page_tokens, LANES):
-                key = key_row(key_ref, first * page_tokens + k, page_tokens)
+                key = key_ref[0:1, at + k:at + k + LANES]
                 live = (key >= low) & (key < high)
                 parts.append(jnp.where(live, logits[:, k:k + LANES] * scale, FLOOR))
             masked.append((pool_ref, first, jnp.concatenate(parts, axis=1)))
@@ -313,31 +314,38 @@
         far_pages = swap(slot_page, "blk", blk, 1)
 
     in_hbm = functools.partial(pltpu.with_memory_space_constraint, memory_space=pltpu.HBM)
-    low, high, near_keys, near_queries, pools[0] = pl.pallas_call(
+    low, high, near_keys, near_queries = pl.pallas_call(
         functools.partial(layout_kernel, device_of, slots, local, rows, heads, drafts, page_tokens),
         out_shape=(
             jax.ShapeDtypeStruct((slots * per, LANES), jnp.int32),
             jax.ShapeDtypeStruct((slots * per, LANES), jnp.int32),
             jax.ShapeDtypeStruct((8, keys), jnp.int32),
             jax.ShapeDtypeStruct(queries.shape, queries.dtype),
-            jax.ShapeDtypeStruct(pool.shape, pool.dtype),
         ),
-        in_specs=[ANY] * 5,
-        out_specs=(VMEM,) * 3 + (ANY,) * 2,
+        in_specs=[ANY] * 4,
+        out_specs=(VMEM,) * 3 + (ANY,),
         scratch_shapes=[
             pltpu.SMEM(request_ids.shape, jnp.int32),
             pltpu.SMEM(prompt_len.shape, jnp.int32),
             pltpu.SMEM(slot_page.shape, jnp.int32),
             pltpu.SMEM(prompt_len.shape, jnp.int32),
-            pltpu.SemaphoreType.DMA((5,)),
+            pltpu.SemaphoreType.DMA((4,)),
         ],
         compiler_params=vmem(8),
-        cost_estimate=cost(1, 2 * slots * per * LANES * 4),
+        cost_estimate=cost(4 * 10**9, 2 * slots * per * LANES * 4),
         name="key_ranges",
-    )(*map(in_hbm, (request_ids, prompt_len, slot_page, queries, pool)))
-    key_lists = [near_keys]
-    if paired:
-        key_lists.append(far_pages.reshape(1, page_count))
+    )(*map(in_hbm, (request_ids, prompt_len, slot_page, queries)))
+    flipped = pl.pallas_call(
+        functools.partial(flip_kernel, page_tokens),
+        out_shape=(jax.ShapeDtypeStruct((8, keys), jnp.int32),) * (len(pools) - 1)
+        + (jax.ShapeDtypeStruct((head_size, keys), pool.dtype),) * len(pools),
+        in_specs=[SMEM] * (len(pools) - 1) + [VMEM] * len(pools),
+        out_specs=(VMEM,) * (2 * len(pools) - 1),
+        compiler_params=vmem(12),
+        cost_estimate=cost(10**9, 4 * pool.size * len(pools)),
+        name="flip_keys",
+    )(*([far_pages] if paired else []), *pools)
+    key_lists, flips = [near_keys, *flipped[:-len(pools)]], flipped[-len(pools):]
 
     own = pl.pallas_call(
         functools.partial(own_kernel, heads, rows, scale),
@@ -361,13 +369,13 @@
         return pl.pallas_call(
             functools.partial(prefix_kernel, heads, rows, scale, slots, slots),
             out_shape=(block_shape,) * slots,
-            in_specs=[VMEM] * (slots + 2 + 2 * len(pools)),
+            in_specs=[VMEM] * (slots + 2 + 3 * len(pools)),
             out_specs=(VMEM,) * slots,
             scratch_shapes=scratch,
             compiler_params=vmem(24),
             cost_estimate=price,
             name="prefix_keys",
-        )(*blocks, low, high, *key_lists, *pools)
+        )(*blocks, low, high, *key_lists, *flips, *pools)
 
     def prefix_many(block):
         step = min(slots, 4)
@@ -380,6 +388,7 @@
                 pl.BlockSpec((step * per, LANES), lambda i: (i, 0)),
                 pl.BlockSpec((step * per, LANES), lambda i: (i, 0)),
                 pl.BlockSpec((8, keys), lambda i: (0, 0)),
+                pl.BlockSpec((head_size, keys), lambda i: (0, 0)),
                 pl.BlockSpec((page_count, page_tokens, head_pair), lambda i: (0, 0, 0)),
             ],
             out_specs=pl.BlockSpec((step,) + block_shape.shape, lambda i: (i, 0, 0)),
@@ -387,7 +396,7 @@
             compiler_params=vmem(24),
             cost_estimate=price,
             name="prefix_keys",
-        )(block, low, high, *key_lists, *pools)
+        )(block, low, high, *key_lists, *flips, *pools)
 
     partial_shape = jax.ShapeDtypeStruct((local, drafts, width), jnp.bfloat16)
     if paired:

time: 25.8 us -> 25.6 us (level)
  waiting for transfers between devices: 6.5 us -> 6.05 us
    pallas_call x0 -> x1, Pallas kernels: none -> 1.03 us  [body(): pl.pallas_call(functools.partial(flip_kernel, page_tokens), out_shape=(ja...]
    pallas_call x1, Pallas kernels: 1.45 us -> 0.88 us  [body(): pl.pallas_call(functools.partial(layout_kernel, device_of, slots, local,...]
    ppermute x11, waiting for transfers between devices: 6.5 us -> 6.05 us  [swap(): return lax.ppermute(x, axis, [(i, i ^ mask) for i in range(size)])]
  transfers between devices with their start and end apart: 11 -> 11, of which waited for: 7 -> 8; matrix products, arithmetic and copies ran while one was open for 0% -> 0% of each run, Pallas kernels for 10% -> 12%
where the time goes in v6:
time: 25.6 us; the launch traced here: 25.4 us
  starting transfers between devices  13.4 us (52%)
  waiting for transfers between devices  6.05 us (24%)
  Pallas kernels  5.22 us (20%)
  between operations  0.74 us (3%)
    ppermute x11, starting transfers between devices, swap(): return lax.ppermute(x, axis, [(i, i ^ mask) for i in range(size)])  13.4 us
    ppermute x11, waiting for transfers between devices, swap(): return lax.ppermute(x, axis, [(i, i ^ mask) for i in range(size)])  6.05 us
    pallas_call x1, Pallas kernels, body(): pl.pallas_call(functools.partial(own_kernel, heads, rows, scale), out_sha...  1.08 us
    pallas_call x1, Pallas kernels, body(): pl.pallas_call(functools.partial(flip_kernel, page_tokens), out_shape=(ja...  1.03 us
    pallas_call x1, Pallas kernels, prefix_column(): pl.pallas_call(functools.partial(prefix_kernel, heads, rows, scale, slots...  0.95 us
    pallas_call x1, Pallas kernels, body(): pl.pallas_call(functools.partial(layout_kernel, device_of, slots, local,...  0.88 us
    pallas_call x1, Pallas kernels, body(): pl.pallas_call(final_kernel, out_shape=(jax.ShapeDtypeStruct(hidden.shape...  0.77 us
    pallas_call x1, Pallas kernels, body(): pl.pallas_call(functools.partial(combine_kernel, heads, rows, head_size),...  0.52 us
  transfers between devices with their start and end apart: 11, of which 8 were waited for; matrix products, arithmetic and copies ran while one was open for 0% of the time, Pallas kernels for 12%

profile of v6, /device:TPU:0, one launch (start us, length us, event | category | flops | bytes accessed | tf_op | source)
XLA Modules:
  0.0 25.4 jit_solution(1246054261292405767)
XLA Ops:
  0.6 0.0 copy-start.1
  0.6 0.5 %collective-permute-start.4 = (bf16[24,64,512]{2,1,0:T(8,128)(2,1)}, bf16[24,64,512]{2,1,0:T(8,128)(2,1)S(1)}, u32[]{:S(2)}, u32[]{:S(2)}) collective-permute-start(bf16[24,64,512]{2,1,0:T(8,128)(2,1)} %bitcast.5), channel_id=1, source_target_pairs={{0,1},{1,0},{2,3},{3,2},{4,5},{5,4},{6,7},{7,6},{8,9},{9,8},{10,11... | collective-permute-start | bytes 4718600 | tf_op jit(solution)/shard_map/ppermute | solution.py:305
  1.2 3.7 %collective-permute-start = (bf16[6,2,512]{2,1,0:T(2,128)(2,1)}, bf16[6,2,512]{2,1,0:T(2,128)(2,1)S(1)}, u32[]{:S(2)}, u32[]{:S(2)}) collective-permute-start(bf16[6,2,512]{2,1,0:T(2,128)(2,1)} %q_ref.3), channel_id=1, source_target_pairs={{0,5},{1,4},{2,7},{3,6},{4,1},{5,0},{6,3},{7,2},{8,13},{9,12},{10,... | collective-permute-start | bytes 36872 | tf_op jit(solution)/shard_map/ppermute | solution.py:305
  4.9 1.0 %collective-permute-start.1 = (bf16[6,2,512]{2,1,0:T(2,128)(2,1)}, bf16[6,2,512]{2,1,0:T(2,128)(2,1)S(1)}, u32[]{:S(2)}, u32[]{:S(2)}) collective-permute-start(bf16[6,2,512]{2,1,0:T(2,128)(2,1)} %q_ref.3), channel_id=1, source_target_pairs={{0,7},{1,6},{2,5},{3,4},{4,3},{5,2},{6,1},{7,0},{8,15},{9,14},{10,... | collective-permute-start | bytes 36872 | tf_op jit(solution)/shard_map/ppermute | solution.py:305
  5.9 0.2 collective-permute-start.2
  6.1 0.4 %collective-permute-start.3 = (s32[24]{0:T(128)}, s32[24]{0:T(128)S(1)}, u32[]{:S(2)}, u32[]{:S(2)}) collective-permute-start(s32[24]{0:T(128)} %page_hbm.1), channel_id=1, source_target_pairs={{0,1},{1,0},{2,3},{3,2},{4,5},{5,4},{6,7},{7,6},{8,9},{9,8},{10,11... | collective-permute-start | bytes 296 | tf_op jit(solution)/shard_map/ppermute | solution.py:305
  6.6 0.9 %key_ranges.1 = (s32[128,128]{1,0:T(8,128)S(1)}, s32[128,128]{1,0:T(8,128)S(1)}, s32[8,1536]{1,0:T(8,128)S(1)}, bf16[6,2,512]{2,1,0:T(2,128)(2,1)S(1)}) custom-call(s32[48]{0:T(128)} %ids_hbm.1, s32[3]{0:T(128)} %len_hbm.1, s32[24]{0:T(128)} %page_hbm.1, bf16[6,2,512]{2,1,0:T(2,128)(2,1)} %q_ref.3), custom_call_target="tpu_custom_call" | custom-call | flops 4000000000 | bytes 131072 | tf_op jit(solution)/shard_map/key_ranges/pallas_call | solution.py:317
  7.5 0.1 collective-permute-done.3.refs_0_
  7.5 0.0 collective-permute-done.4.refs_2_.refs_11_
  7.5 0.0 copy-done.1
  7.5 1.0 %flip_keys.1 = (s32[8,1536]{1,0:T(8,128)S(1)}, bf16[256,1536]{1,0:T(8,128)(2,1)S(1)}, bf16[256,1536]{1,0:T(8,128)(2,1)S(1)}) custom-call(s32[24]{0:T(128)S(1)} %collective-permute-done.3.refs_0_, bf16[24,64,512]{2,1,0:T(8,128)(2,1)S(1)} %bitcast.6, bf16[24,64,512]{2,1,0:T(8,128)(2,1)S(1)} %collective-permute-done.4.refs_2_.refs_11_), custom_call_target="tpu_custom_call" | custom-call | flops 1000000000 | bytes 6291456 | tf_op jit(solution)/shard_map/flip_keys/pallas_call | solution.py:338
  8.6 0.0 collective-permute-done.refs_1_
  8.6 1.4 %collective-permute-done.1.refs_2_ = bf16[6,2,512]{2,1,0:T(2,128)(2,1)S(1)} collective-permute-done((bf16[6,2,512]{2,1,0:T(2,128)(2,1)}, bf16[6,2,512]{2,1,0:T(2,128)(2,1)S(1)}, u32[]{:S(2)}, u32[]{:S(2)}) %collective-permute-start.1) | collective-permute-done | bytes 12320 | tf_op jit(solution)/shard_map/ppermute | solution.py:305
  10.0 0.0 collective-permute-done.2.refs_3_
  10.0 0.0 copy-start.2
  10.0 0.0 copy-start.4
  10.0 0.0 copy-start.5
  10.0 0.0 copy-start.8
  10.0 0.0 copy-start
  10.0 1.0 %prefix_keys.1 = (bf16[32,384]{1,0:T(8,128)(2,1)S(1)}, bf16[32,384]{1,0:T(8,128)(2,1)S(1)}, bf16[32,384]{1,0:T(8,128)(2,1)S(1)}, bf16[32,384]{1,0:T(8,128)(2,1)S(1)}) custom-call(bf16[6,2,512]{2,1,0:T(2,128)(2,1)S(1)} %get-tuple-element.13.refs_0_, bf16[6,2,512]{2,1,0:T(2,128)(2,1)S(1)} %collective-permute-done.refs_1_, ...), custom_call_target="tpu_custom_call" | custom-call | flops 402653184 | bytes 3145728 | tf_op jit(solution)/shard_map/prefix_keys/pallas_call | solution.py:369
  11.0 1.8 %collective-permute-start.5 = (bf16[32,384]{1,0:T(8,128)(2,1)S(1)}, bf16[32,384]{1,0:T(8,128)(2,1)S(1)}, u32[]{:S(2)}, u32[]{:S(2)}) collective-permute-start(bf16[32,384]{1,0:T(8,128)(2,1)S(1)} %get-tuple-element.21), channel_id=1, source_target_pairs={{0,7},{1,6},{2,5},{3,4},{4,3},{5,2},{6,1},{7,0},{8,15},{9,14},{10,... | collective-permute-start | bytes 73736 | tf_op jit(solution)/shard_map/ppermute | solution.py:305
  12.8 0.0 collective-permute-start.6
  12.8 2.1 %collective-permute-start.7 = (bf16[32,384]{1,0:T(8,128)(2,1)S(1)}, bf16[32,384]{1,0:T(8,128)(2,1)S(1)}, u32[]{:S(2)}, u32[]{:S(2)}) collective-permute-start(bf16[32,384]{1,0:T(8,128)(2,1)S(1)} %get-tuple-element.23), channel_id=1, source_target_pairs={{0,5},{1,4},{2,7},{3,6},{4,1},{5,0},{6,3},{7,2},{8,13},{9,12},{10,... | collective-permute-start | bytes 73736 | tf_op jit(solution)/shard_map/ppermute | solution.py:305
  14.9 0.0 copy-done.2
  14.9 0.0 copy-done.4
  14.9 0.0 copy-done.5
  14.9 0.0 copy-done.8
  14.9 0.0 copy-start.3
  14.9 0.0 copy-start.6
  14.9 0.0 copy-start.7
  14.9 1.1 %own_keys.1.refs_0_ = f32[32,384]{1,0:T(8,128)S(1)} custom-call(s32[6]{0:T(128)S(1)} %copy-done.8, bf16[6,2,512]{2,1,0:T(2,128)(2,1)S(1)} %copy-done.4, bf16[6,128,512]{2,1,0:T(8,128)(2,1)S(1)} %bitcast.8, bf16[6,2,512]{2,1,0:T(2,128)(2,1)S(1)} %bitcast.9), custom_call_target="tpu_custom_call" | custom-call | flops 25165824 | bytes 786432 | tf_op jit(solution)/shard_map/own_keys/pallas_call | solution.py:350
  16.0 0.2 collective-permute-done.5.refs_2_
  16.2 0.4 %collective-permute-done.6.refs_3_ = bf16[32,384]{1,0:T(8,128)(2,1)S(1)} collective-permute-done((bf16[32,384]{1,0:T(8,128)(2,1)S(1)}, bf16[32,384]{1,0:T(8,128)(2,1)S(1)}, u32[]{:S(2)}, u32[]{:S(2)}) %collective-permute-start.6) | collective-permute-done | bytes 24608 | tf_op jit(solution)/shard_map/ppermute | solution.py:305
  16.7 0.3 %collective-permute-done.7.refs_4_ = bf16[32,384]{1,0:T(8,128)(2,1)S(1)} collective-permute-done((bf16[32,384]{1,0:T(8,128)(2,1)S(1)}, bf16[32,384]{1,0:T(8,128)(2,1)S(1)}, u32[]{:S(2)}, u32[]{:S(2)}) %collective-permute-start.7) | collective-permute-done | bytes 24608 | tf_op jit(solution)/shard_map/ppermute | solution.py:305
  17.0 0.0 copy-done
  17.0 0.5 %combine_project.1.refs_0_ = bf16[6,2,2048]{2,1,0:T(2,128)(2,1)S(1)} custom-call(f32[32,384]{1,0:T(8,128)S(1)} %own_keys.1.refs_0_, bf16[32,384]{1,0:T(8,128)(2,1)S(1)} %get-tuple-element.20.refs_1_, bf16[32,384]{1,0:T(8,128)(2,1)S(1)} %collective-permute-done.5.refs_2_, bf16[32,384]{1,0:T(8,128)(2,1)S(1)} %collective-permute-done.6.refs_3_, ...), custom_call_target="tpu_custom_call" | custom-call | flops 33554432 | bytes 2097152 | tf_op jit(solution)/shard_map/combine_project/pallas_call | solution.py:408
  17.5 2.5 %collective-permute-start.10 = (bf16[6,2,2048]{2,1,0:T(2,128)(2,1)S(1)}, bf16[6,2,2048]{2,1,0:T(2,128)(2,1)S(1)}, u32[]{:S(2)}, u32[]{:S(2)}) collective-permute-start(bf16[6,2,2048]{2,1,0:T(2,128)(2,1)S(1)} %combine_project.1.refs_0_), channel_id=1, source_target_pairs={{0,24},{8,16},{16,8},{24,0},{1,25},{9,17},{17,9},{25,1},{2,26},{10... | collective-permute-start | bytes 147464 | tf_op jit(solution)/shard_map/ppermute | solution.py:305
  20.0 0.5 %collective-permute-start.8 = (bf16[6,2,2048]{2,1,0:T(2,128)(2,1)S(1)}, bf16[6,2,2048]{2,1,0:T(2,128)(2,1)S(1)}, u32[]{:S(2)}, u32[]{:S(2)}) collective-permute-start(bf16[6,2,2048]{2,1,0:T(2,128)(2,1)S(1)} %combine_project.1.refs_0_), channel_id=1, source_target_pairs={{0,8},{8,0},{16,24},{24,16},{1,9},{9,1},{17,25},{25,17},{2,10},{10... | collective-permute-start | bytes 147464 | tf_op jit(solution)/shard_map/ppermute | solution.py:305
  20.5 0.5 %collective-permute-start.9 = (bf16[6,2,2048]{2,1,0:T(2,128)(2,1)S(1)}, bf16[6,2,2048]{2,1,0:T(2,128)(2,1)S(1)}, u32[]{:S(2)}, u32[]{:S(2)}) collective-permute-start(bf16[6,2,2048]{2,1,0:T(2,128)(2,1)S(1)} %combine_project.1.refs_0_), channel_id=1, source_target_pairs={{0,16},{8,24},{16,0},{24,8},{1,17},{9,25},{17,1},{25,9},{2,18},{10... | collective-permute-start | bytes 147464 | tf_op jit(solution)/shard_map/ppermute | solution.py:305
  21.0 1.6 %collective-permute-done.10.refs_3_ = bf16[6,2,2048]{2,1,0:T(2,128)(2,1)S(1)} collective-permute-done((bf16[6,2,2048]{2,1,0:T(2,128)(2,1)S(1)}, bf16[6,2,2048]{2,1,0:T(2,128)(2,1)S(1)}, u32[]{:S(2)}, u32[]{:S(2)}) %collective-permute-start.10) | collective-permute-done | bytes 49184 | tf_op jit(solution)/shard_map/ppermute | solution.py:305
  22.7 1.4 %collective-permute-done.8.refs_1_ = bf16[6,2,2048]{2,1,0:T(2,128)(2,1)S(1)} collective-permute-done((bf16[6,2,2048]{2,1,0:T(2,128)(2,1)S(1)}, bf16[6,2,2048]{2,1,0:T(2,128)(2,1)S(1)}, u32[]{:S(2)}, u32[]{:S(2)}) %collective-permute-start.8) | collective-permute-done | bytes 49184 | tf_op jit(solution)/shard_map/ppermute | solution.py:305
  24.1 0.5 %collective-permute-done.9.refs_2_ = bf16[6,2,2048]{2,1,0:T(2,128)(2,1)S(1)} collective-permute-done((bf16[6,2,2048]{2,1,0:T(2,128)(2,1)S(1)}, bf16[6,2,2048]{2,1,0:T(2,128)(2,1)S(1)}, u32[]{:S(2)}, u32[]{:S(2)}) %collective-permute-start.9) | collective-permute-done | bytes 49184 | tf_op jit(solution)/shard_map/ppermute | solution.py:305
  24.6 0.0 copy-done.3
  24.6 0.0 copy-done.6
  24.6 0.0 copy-done.7
  24.6 0.8 %residual_scores.1 = (bf16[6,2,2048]{2,1,0:T(2,128)(2,1)}, f32[6]{0:T(128)}) custom-call(bf16[6,2,2048]{2,1,0:T(2,128)(2,1)S(1)} %combine_project.1.refs_0_, bf16[6,2,2048]{2,1,0:T(2,128)(2,1)S(1)} %collective-permute-done.8.refs_1_, bf16[6,2,2048]{2,1,0:T(2,128)(2,1)S(1)} %collective-permute-done.9.refs_2_, ...), custom_call_target="tpu_custom_call" | custom-call | flops 1 | bytes 294912 | tf_op jit(solution)/shard_map/residual_scores/pallas_call | solution.py:433
Async XLA Ops:
  0.6 6.9 %copy-start.1 = (bf16[1,24,64,512]{3,2,1,0:T(8,128)(2,1)S(1)}, bf16[1,24,64,512]{3,2,1,0:T(8,128)(2,1)}, u32[]{:S(2)}) copy-start(bf16[1,24,64,512]{3,2,1,0:T(8,128)(2,1)} %param.12) | copy-start | bytes 4718596
  0.6 6.9 %collective-permute-start.4 = (bf16[24,64,512]{2,1,0:T(8,128)(2,1)}, bf16[24,64,512]{2,1,0:T(8,128)(2,1)S(1)}, u32[]{:S(2)}, u32[]{:S(2)}) collective-permute-start(bf16[24,64,512]{2,1,0:T(8,128)(2,1)} %bitcast.5), channel_id=1, source_target_pairs={{0,1},{1,0},{2,3},{3,2},{4,5},{5,4},{6,7},{7,6},{8,9},{9,8},{10,11... | collective-permute-start | bytes 4718600 | tf_op jit(solution)/shard_map/ppermute | solution.py:305
  1.2 7.4 %collective-permute-start = (bf16[6,2,512]{2,1,0:T(2,128)(2,1)}, bf16[6,2,512]{2,1,0:T(2,128)(2,1)S(1)}, u32[]{:S(2)}, u32[]{:S(2)}) collective-permute-start(bf16[6,2,512]{2,1,0:T(2,128)(2,1)} %q_ref.3), channel_id=1, source_target_pairs={{0,5},{1,4},{2,7},{3,6},{4,1},{5,0},{6,3},{7,2},{8,13},{9,12},{10,... | collective-permute-start | bytes 36872 | tf_op jit(solution)/shard_map/ppermute | solution.py:305
  4.9 5.1 %collective-permute-start.1 = (bf16[6,2,512]{2,1,0:T(2,128)(2,1)}, bf16[6,2,512]{2,1,0:T(2,128)(2,1)S(1)}, u32[]{:S(2)}, u32[]{:S(2)}) collective-permute-start(bf16[6,2,512]{2,1,0:T(2,128)(2,1)} %q_ref.3), channel_id=1, source_target_pairs={{0,7},{1,6},{2,5},{3,4},{4,3},{5,2},{6,1},{7,0},{8,15},{9,14},{10,... | collective-permute-start | bytes 36872 | tf_op jit(solution)/shard_map/ppermute | solution.py:305
  5.9 4.1 %collective-permute-start.2 = (bf16[6,2,512]{2,1,0:T(2,128)(2,1)}, bf16[6,2,512]{2,1,0:T(2,128)(2,1)S(1)}, u32[]{:S(2)}, u32[]{:S(2)}) collective-permute-start(bf16[6,2,512]{2,1,0:T(2,128)(2,1)} %q_ref.3), channel_id=1, source_target_pairs={{0,3},{1,2},{2,1},{3,0},{4,7},{5,6},{6,5},{7,4},{8,11},{9,10},{10,... | collective-permute-start | bytes 36872 | tf_op jit(solution)/shard_map/ppermute | solution.py:305
  6.1 1.4 %collective-permute-start.3 = (s32[24]{0:T(128)}, s32[24]{0:T(128)S(1)}, u32[]{:S(2)}, u32[]{:S(2)}) collective-permute-start(s32[24]{0:T(128)} %page_hbm.1), channel_id=1, source_target_pairs={{0,1},{1,0},{2,3},{3,2},{4,5},{5,4},{6,7},{7,6},{8,9},{9,8},{10,11... | collective-permute-start | bytes 296 | tf_op jit(solution)/shard_map/ppermute | solution.py:305
  10.0 4.9 %copy-start.2 = (bf16[1,6,128,512]{3,2,1,0:T(8,128)(2,1)S(1)}, bf16[1,6,128,512]{3,2,1,0:T(8,128)(2,1)}, u32[]{:S(2)}) copy-start(bf16[1,6,128,512]{3,2,1,0:T(8,128)(2,1)} %param.17) | copy-start | bytes 2359300
  10.0 4.9 %copy-start.4 = (bf16[6,2,512]{2,1,0:T(2,128)(2,1)S(1)}, bf16[6,2,512]{2,1,0:T(2,128)(2,1)}, u32[]{:S(2)}) copy-start(bf16[6,2,512]{2,1,0:T(2,128)(2,1)} %q_ref.3) | copy-start | bytes 36868
  10.0 4.9 %copy-start.5 = (bf16[1,6,2,512]{3,2,1,0:T(2,128)(2,1)S(1)}, bf16[1,6,2,512]{3,2,1,0:T(2,128)(2,1)}, u32[]{:S(2)}) copy-start(bf16[1,6,2,512]{3,2,1,0:T(2,128)(2,1)} %param.19) | copy-start | bytes 36868
  10.0 4.9 %copy-start.8 = (s32[6]{0:T(128)S(1)}, s32[6]{0:T(128)}, u32[]{:S(2)}) copy-start(s32[6]{0:T(128)} %len_ref.1) | copy-start | bytes 76
  10.0 6.9 %copy-start = (bf16[512,2048]{1,0:T(8,128)(2,1)S(1)}, bf16[512,2048]{1,0:T(8,128)(2,1)}, u32[]{:S(2)}) copy-start(bf16[512,2048]{1,0:T(8,128)(2,1)} %refs_5_.1) | copy-start | bytes 6291460
  11.0 5.2 %collective-permute-start.5 = (bf16[32,384]{1,0:T(8,128)(2,1)S(1)}, bf16[32,384]{1,0:T(8,128)(2,1)S(1)}, u32[]{:S(2)}, u32[]{:S(2)}) collective-permute-start(bf16[32,384]{1,0:T(8,128)(2,1)S(1)} %get-tuple-element.21), channel_id=1, source_target_pairs={{0,7},{1,6},{2,5},{3,4},{4,3},{5,2},{6,1},{7,0},{8,15},{9,14},{10,... | collective-permute-start | bytes 73736 | tf_op jit(solution)/shard_map/ppermute | solution.py:305
  12.8 3.9 %collective-permute-start.6 = (bf16[32,384]{1,0:T(8,128)(2,1)S(1)}, bf16[32,384]{1,0:T(8,128)(2,1)S(1)}, u32[]{:S(2)}, u32[]{:S(2)}) collective-permute-start(bf16[32,384]{1,0:T(8,128)(2,1)S(1)} %get-tuple-element.22), channel_id=1, source_target_pairs={{0,3},{1,2},{2,1},{3,0},{4,7},{5,6},{6,5},{7,4},{8,11},{9,10},{10,... | collective-permute-start | bytes 73736 | tf_op jit(solution)/shard_map/ppermute | solution.py:305
  12.8 4.2 %collective-permute-start.7 = (bf16[32,384]{1,0:T(8,128)(2,1)S(1)}, bf16[32,384]{1,0:T(8,128)(2,1)S(1)}, u32[]{:S(2)}, u32[]{:S(2)}) collective-permute-start(bf16[32,384]{1,0:T(8,128)(2,1)S(1)} %get-tuple-element.23), channel_id=1, source_target_pairs={{0,5},{1,4},{2,7},{3,6},{4,1},{5,0},{6,3},{7,2},{8,13},{9,12},{10,... | collective-permute-start | bytes 73736 | tf_op jit(solution)/shard_map/ppermute | solution.py:305
  14.9 9.7 %copy-start.3 = (bf16[6,2,2048]{2,1,0:T(2,128)(2,1)S(1)}, bf16[6,2,2048]{2,1,0:T(2,128)(2,1)}, u32[]{:S(2)}) copy-start(bf16[6,2,2048]{2,1,0:T(2,128)(2,1)} %refs_4_.1) | copy-start | bytes 147460
  14.9 9.7 %copy-start.6 = (f32[2048]{0:T(1024)S(1)}, f32[2048]{0:T(1024)}, u32[]{:S(2)}) copy-start(f32[2048]{0:T(1024)} %param.22) | copy-start | bytes 24580
  14.9 9.7 %copy-start.7 = (f32[2048]{0:T(1024)S(1)}, f32[2048]{0:T(1024)}, u32[]{:S(2)}) copy-start(f32[2048]{0:T(1024)} %param.23) | copy-start | bytes 24580
  17.5 5.2 %collective-permute-start.10 = (bf16[6,2,2048]{2,1,0:T(2,128)(2,1)S(1)}, bf16[6,2,2048]{2,1,0:T(2,128)(2,1)S(1)}, u32[]{:S(2)}, u32[]{:S(2)}) collective-permute-start(bf16[6,2,2048]{2,1,0:T(2,128)(2,1)S(1)} %combine_project.1.refs_0_), channel_id=1, source_target_pairs={{0,24},{8,16},{16,8},{24,0},{1,25},{9,17},{17,9},{25,1},{2,26},{10... | collective-permute-start | bytes 147464 | tf_op jit(solution)/shard_map/ppermute | solution.py:305
  20.0 4.1 %collective-permute-start.8 = (bf16[6,2,2048]{2,1,0:T(2,128)(2,1)S(1)}, bf16[6,2,2048]{2,1,0:T(2,128)(2,1)S(1)}, u32[]{:S(2)}, u32[]{:S(2)}) collective-permute-start(bf16[6,2,2048]{2,1,0:T(2,128)(2,1)S(1)} %combine_project.1.refs_0_), channel_id=1, source_target_pairs={{0,8},{8,0},{16,24},{24,16},{1,9},{9,1},{17,25},{25,17},{2,10},{10... | collective-permute-start | bytes 147464 | tf_op jit(solution)/shard_map/ppermute | solution.py:305
  20.5 4.1 %collective-permute-start.9 = (bf16[6,2,2048]{2,1,0:T(2,128)(2,1)S(1)}, bf16[6,2,2048]{2,1,0:T(2,128)(2,1)S(1)}, u32[]{:S(2)}, u32[]{:S(2)}) collective-permute-start(bf16[6,2,2048]{2,1,0:T(2,128)(2,1)S(1)} %combine_project.1.refs_0_), channel_id=1, source_target_pairs={{0,16},{8,24},{16,0},{24,8},{1,17},{9,25},{17,1},{25,9},{2,18},{10... | collective-permute-start | bytes 147464 | tf_op jit(solution)/shard_map/ppermute | solution.py:305

commit v7 on v6

--- a/solution.py
+++ b/solution.py
@@ -126,7 +126,7 @@
         flip_ref[...] = keys.T
 
 
-def prefix_kernel(heads, rows, scale, sources, parts_out, *refs):
+def prefix_kernel(heads, rows, scale, sources, parts_out, first_slot, *refs):
     q_refs, refs = refs[:sources], refs[sources:]
     (low_ref, high_ref), refs = refs[:2], refs[2:]
     both_refs, out_refs, q_rows = refs[:-parts_out - 1], refs[-parts_out - 1:-1], refs[-1]
@@ -138,7 +138,8 @@
     head_size = head_pair // 2
     for j, block in enumerate(blocks):
         spread_rows(q_rows, j * heads * rows, block, heads, head_size, rows)
-    low, high = low_ref[...], high_ref[...]
+    ranges = pl.ds(first_slot * heads * rows, slots * heads * rows)
+    low, high = low_ref[ranges, :], high_ref[ranges, :]
     queries = q_rows[...]
     chunk = CHUNK if pages % CHUNK == 0 else pages
     masked = []
@@ -175,7 +176,8 @@
         out_ref[:, head_size:] = stats[j * per:(j + 1) * per].astype(out_ref.dtype)
 
 
-def own_kernel(heads, rows, scale, len_ref, q_ref, tail_ref, fresh_ref, out_ref, q_rows, f_rows):
+def own_kernel(heads, rows, scale, len_ref, q_ref, tail_ref, fresh_ref, weight_ref, out_ref, q_rows, f_rows):
+    del weight_ref
     reqs, drafts, _ = q_ref.shape
     tail = tail_ref.shape[1]
     head_size = tail_ref.shape[2] // 2
@@ -350,7 +352,7 @@
     own = pl.pallas_call(
         functools.partial(own_kernel, heads, rows, scale),
         out_shape=jax.ShapeDtypeStruct((per, head_size + LANES), jnp.float32),
-        in_specs=[SMEM] + [VMEM] * 3,
+        in_specs=[SMEM] + [VMEM] * 4,
         out_specs=VMEM,
         scratch_shapes=[
             pltpu.VMEM((per, head_size), jnp.bfloat16),
@@ -359,28 +361,29 @@
         compiler_params=vmem(8),
         cost_estimate=cost(4 * per * local * tail_cache.shape[2] * head_size, 2 * tail_cache.size),
         name="own_keys",
-    )(tail_len, queries, tail_cache[0], new_kv[0])
+    )(tail_len, queries, tail_cache[0], new_kv[0], out_weight)
 
     block_shape = jax.ShapeDtypeStruct((per, head_size + LANES), jnp.bfloat16)
     scratch = [pltpu.VMEM((min(slots, 4) * per, head_size), jnp.bfloat16)]
     price = cost(4 * slots * per * keys * len(pools) * head_size, 2 * pool.size * len(pools))
 
-    def prefix_column(blocks):
+    def prefix_column(blocks, first_slot):
+        count = len(blocks)
         return pl.pallas_call(
-            functools.partial(prefix_kernel, heads, rows, scale, slots, slots),
-            out_shape=(block_shape,) * slots,
-            in_specs=[VMEM] * (slots + 2 + 3 * len(pools)),
-            out_specs=(VMEM,) * slots,
-            scratch_shapes=scratch,
+            functools.partial(prefix_kernel, heads, rows, scale, count, count, first_slot),
+            out_shape=(block_shape,) * count,
+            in_specs=[VMEM] * (count + 2 + 3 * len(pools)),
+            out_specs=(VMEM,) * count,
+            scratch_shapes=[pltpu.VMEM((count * per, head_size), jnp.bfloat16)],
             compiler_params=vmem(24),
-            cost_estimate=price,
+            cost_estimate=cost(price.flops // slots * count, price.bytes_accessed),
             name="prefix_keys",
         )(*blocks, low, high, *key_lists, *flips, *pools)
 
     def prefix_many(block):
         step = min(slots, 4)
         return pl.pallas_call(
-            functools.partial(prefix_kernel, heads, rows, scale, 1, 1),
+            functools.partial(prefix_kernel, heads, rows, scale, 1, 1, 0),
             out_shape=jax.ShapeDtypeStruct((slots,) + block_shape.shape, jnp.bfloat16),
             grid=(slots // step,),
             in_specs=[
@@ -401,7 +404,8 @@
     partial_shape = jax.ShapeDtypeStruct((local, drafts, width), jnp.bfloat16)
     if paired:
         column = [near_queries] + [swap(queries, "blk", blk, mask) for mask in masks[1:]]
-        sums = prefix_column(column)
+        sums = [None, *prefix_column(column[1:], 1)] if half > 1 else [None]
+        sums[0] = prefix_column(column[:1], 0)[0]
         blocks = [sums[0]] + [
             swap(sums[partners.index(j)], "blk", blk, 2 * j + 1) for j in ORDER_B if j < half
         ]

time: 25.6 us -> 25.5 us (level)
  waiting for transfers between devices: 6.05 us -> 5.31 us
  Pallas kernels: 5.22 us -> 5.8 us
    ppermute x11, waiting for transfers between devices: 6.05 us -> 5.31 us  [swap(): return lax.ppermute(x, axis, [(i, i ^ mask) for i in range(size)])]
    pallas_call x1 -> x2, Pallas kernels: 0.95 us -> 1.53 us  [prefix_column(): pl.pallas_call(functools.partial(prefix_kernel, heads, rows, scale, count...]
  transfers between devices with their start and end apart: 11 -> 11, of which waited for: 8 -> 6; matrix products, arithmetic and copies ran while one was open for 0% -> 0% of each run, Pallas kernels for 12% -> 15%
where the time goes in v7:
time: 25.5 us; the launch traced here: 25.3 us
  starting transfers between devices  13.4 us (53%)
  Pallas kernels  5.8 us (23%)
  waiting for transfers between devices  5.31 us (21%)
  between operations  0.75 us (3%)
    ppermute x11, starting transfers between devices, swap(): return lax.ppermute(x, axis, [(i, i ^ mask) for i in range(size)])  13.4 us
    ppermute x11, waiting for transfers between devices, swap(): return lax.ppermute(x, axis, [(i, i ^ mask) for i in range(size)])  5.31 us
    pallas_call x2, Pallas kernels, prefix_column(): pl.pallas_call(functools.partial(prefix_kernel, heads, rows, scale, count...  1.53 us
    pallas_call x1, Pallas kernels, body(): pl.pallas_call(functools.partial(own_kernel, heads, rows, scale), out_sha...  1.08 us
    pallas_call x1, Pallas kernels, body(): pl.pallas_call(functools.partial(flip_kernel, page_tokens), out_shape=(ja...  1.03 us
    pallas_call x1, Pallas kernels, body(): pl.pallas_call(functools.partial(layout_kernel, device_of, slots, local,...  0.88 us
    pallas_call x1, Pallas kernels, body(): pl.pallas_call(final_kernel, out_shape=(jax.ShapeDtypeStruct(hidden.shape...  0.77 us
    pallas_call x1, Pallas kernels, body(): pl.pallas_call(functools.partial(combine_kernel, heads, rows, head_size),...  0.52 us
  transfers between devices with their start and end apart: 11, of which 6 were waited for; matrix products, arithmetic and copies ran while one was open for 0% of the time, Pallas kernels for 15%

profile of v7, /device:TPU:0, one launch (start us, length us, event | category | flops | bytes accessed | tf_op | source)
XLA Modules:
  0.0 25.3 jit_solution(1052067194259256725)
XLA Ops:
  0.6 0.0 copy-start.1
  0.6 0.5 %collective-permute-start.1 = (bf16[24,64,512]{2,1,0:T(8,128)(2,1)}, bf16[24,64,512]{2,1,0:T(8,128)(2,1)S(1)}, u32[]{:S(2)}, u32[]{:S(2)}) collective-permute-start(bf16[24,64,512]{2,1,0:T(8,128)(2,1)} %bitcast.5), channel_id=1, source_target_pairs={{0,1},{1,0},{2,3},{3,2},{4,5},{5,4},{6,7},{7,6},{8,9},{9,8},{10,11... | collective-permute-start | bytes 4718600 | tf_op jit(solution)/shard_map/ppermute | solution.py:307
  1.2 3.7 %collective-permute-start.2 = (bf16[6,2,512]{2,1,0:T(2,128)(2,1)}, bf16[6,2,512]{2,1,0:T(2,128)(2,1)S(1)}, u32[]{:S(2)}, u32[]{:S(2)}) collective-permute-start(bf16[6,2,512]{2,1,0:T(2,128)(2,1)} %q_ref.3), channel_id=1, source_target_pairs={{0,5},{1,4},{2,7},{3,6},{4,1},{5,0},{6,3},{7,2},{8,13},{9,12},{10,... | collective-permute-start | bytes 36872 | tf_op jit(solution)/shard_map/ppermute | solution.py:307
  4.9 1.0 %collective-permute-start.3 = (bf16[6,2,512]{2,1,0:T(2,128)(2,1)}, bf16[6,2,512]{2,1,0:T(2,128)(2,1)S(1)}, u32[]{:S(2)}, u32[]{:S(2)}) collective-permute-start(bf16[6,2,512]{2,1,0:T(2,128)(2,1)} %q_ref.3), channel_id=1, source_target_pairs={{0,7},{1,6},{2,5},{3,4},{4,3},{5,2},{6,1},{7,0},{8,15},{9,14},{10,... | collective-permute-start | bytes 36872 | tf_op jit(solution)/shard_map/ppermute | solution.py:307
  5.9 0.2 collective-permute-start.4
  6.1 0.4 %collective-permute-start = (s32[24]{0:T(128)}, s32[24]{0:T(128)S(1)}, u32[]{:S(2)}, u32[]{:S(2)}) collective-permute-start(s32[24]{0:T(128)} %page_hbm.1), channel_id=1, source_target_pairs={{0,1},{1,0},{2,3},{3,2},{4,5},{5,4},{6,7},{7,6},{8,9},{9,8},{10,11... | collective-permute-start | bytes 296 | tf_op jit(solution)/shard_map/ppermute | solution.py:307
  6.6 0.9 %key_ranges.1 = (s32[128,128]{1,0:T(8,128)S(1)}, s32[128,128]{1,0:T(8,128)S(1)}, s32[8,1536]{1,0:T(8,128)S(1)}, bf16[6,2,512]{2,1,0:T(2,128)(2,1)S(1)}) custom-call(s32[48]{0:T(128)} %ids_hbm.1, s32[3]{0:T(128)} %len_hbm.1, s32[24]{0:T(128)} %page_hbm.1, bf16[6,2,512]{2,1,0:T(2,128)(2,1)} %q_ref.3), custom_call_target="tpu_custom_call" | custom-call | flops 4000000000 | bytes 131072 | tf_op jit(solution)/shard_map/key_ranges/pallas_call | solution.py:319
  7.5 0.1 collective-permute-done.refs_0_
  7.5 0.0 collective-permute-done.1.refs_2_.refs_8_.refs_10_
  7.5 0.0 copy-done.1
  7.5 1.0 %flip_keys.1 = (s32[8,1536]{1,0:T(8,128)S(1)}, bf16[256,1536]{1,0:T(8,128)(2,1)S(1)}, bf16[256,1536]{1,0:T(8,128)(2,1)S(1)}) custom-call(s32[24]{0:T(128)S(1)} %collective-permute-done.refs_0_, bf16[24,64,512]{2,1,0:T(8,128)(2,1)S(1)} %bitcast.6, bf16[24,64,512]{2,1,0:T(8,128)(2,1)S(1)} %collective-permute-done.1.refs_2_.refs_8_.refs_10_), custom_call_target="tpu_custom_call" | custom-call | flops 1000000000 | bytes 6291456 | tf_op jit(solution)/shard_map/flip_keys/pallas_call | solution.py:340
  8.6 0.0 collective-permute-done.2.refs_0_
  8.6 1.4 %collective-permute-done.3.refs_1_ = bf16[6,2,512]{2,1,0:T(2,128)(2,1)S(1)} collective-permute-done((bf16[6,2,512]{2,1,0:T(2,128)(2,1)}, bf16[6,2,512]{2,1,0:T(2,128)(2,1)S(1)}, u32[]{:S(2)}, u32[]{:S(2)}) %collective-permute-start.3) | collective-permute-done | bytes 12320 | tf_op jit(solution)/shard_map/ppermute | solution.py:307
  10.0 0.0 collective-permute-done.4.refs_2_
  10.0 0.0 copy-start
  10.0 0.0 copy-start.2
  10.0 0.0 copy-start.4
  10.0 0.0 copy-start.5
  10.0 0.0 copy-start.8
  10.0 0.8 %prefix_keys.3 = (bf16[32,384]{1,0:T(8,128)(2,1)S(1)}, bf16[32,384]{1,0:T(8,128)(2,1)S(1)}, bf16[32,384]{1,0:T(8,128)(2,1)S(1)}) custom-call(bf16[6,2,512]{2,1,0:T(2,128)(2,1)S(1)} %collective-permute-done.2.refs_0_, bf16[6,2,512]{2,1,0:T(2,128)(2,1)S(1)} %collective-permute-done.3.refs_1_, bf16[6,2,512]{2,1,0:T(2,128)(2,1)S(1)} %collective-permute-done.4.refs_2_, ...), custom_call_target="tpu_custom_call" | custom-call | flops 301989888 | bytes 3145728 | tf_op jit(solution)/shard_map/prefix_keys/pallas_call | solution.py:372
  10.9 1.8 %collective-permute-start.5 = (bf16[32,384]{1,0:T(8,128)(2,1)S(1)}, bf16[32,384]{1,0:T(8,128)(2,1)S(1)}, u32[]{:S(2)}, u32[]{:S(2)}) collective-permute-start(bf16[32,384]{1,0:T(8,128)(2,1)S(1)} %get-tuple-element.19), channel_id=1, source_target_pairs={{0,7},{1,6},{2,5},{3,4},{4,3},{5,2},{6,1},{7,0},{8,15},{9,14},{10,... | collective-permute-start | bytes 73736 | tf_op jit(solution)/shard_map/ppermute | solution.py:307
  12.7 0.0 collective-permute-start.6
  12.7 2.1 %collective-permute-start.7 = (bf16[32,384]{1,0:T(8,128)(2,1)S(1)}, bf16[32,384]{1,0:T(8,128)(2,1)S(1)}, u32[]{:S(2)}, u32[]{:S(2)}) collective-permute-start(bf16[32,384]{1,0:T(8,128)(2,1)S(1)} %get-tuple-element.21), channel_id=1, source_target_pairs={{0,5},{1,4},{2,7},{3,6},{4,1},{5,0},{6,3},{7,2},{8,13},{9,12},{10,... | collective-permute-start | bytes 73736 | tf_op jit(solution)/shard_map/ppermute | solution.py:307
  14.8 0.0 copy-done
  14.8 0.0 copy-done.2
  14.8 0.0 copy-done.4
  14.8 0.0 copy-done.5
  14.8 0.0 copy-done.8
  14.8 1.1 %own_keys.1.refs_0_ = f32[32,384]{1,0:T(8,128)S(1)} custom-call(s32[6]{0:T(128)S(1)} %copy-done.8, bf16[6,2,512]{2,1,0:T(2,128)(2,1)S(1)} %copy-done.4, bf16[6,128,512]{2,1,0:T(8,128)(2,1)S(1)} %bitcast.9, bf16[6,2,512]{2,1,0:T(2,128)(2,1)S(1)} %bitcast.10, bf16[512,2048]{1,0:T(8,128)(2,1)S(1)} %copy-done), custom_call_target="tpu_custom_call" | custom-call | flops 25165824 | bytes 786432 | tf_op jit(solution)/shard_map/own_keys/pallas_call | solution.py:352
  15.9 0.7 %prefix_keys.2.refs_1_ = bf16[32,384]{1,0:T(8,128)(2,1)S(1)} custom-call(bf16[6,2,512]{2,1,0:T(2,128)(2,1)S(1)} %get-tuple-element.12.refs_0_, s32[128,128]{1,0:T(8,128)S(1)} %get-tuple-element.13.refs_1_.refs_3_, s32[128,128]{1,0:T(8,128)S(1)} %get-tuple-element.14.refs_2_.refs_4_, s32[8,1536]{1,0:T(8,128)S(1)} %get-tuple-element.15.refs_3_.refs_5_, ...), custom_call_target="tpu_custom_call" | custom-call | flops 100663296 | bytes 3145728 | tf_op jit(solution)/shard_map/prefix_keys/pallas_call | solution.py:372
  16.6 0.0 copy-start.3
  16.6 0.0 copy-start.6
  16.6 0.0 copy-start.7
  16.6 0.0 collective-permute-done.5.refs_2_
  16.6 0.0 collective-permute-done.6.refs_3_
  16.7 0.2 collective-permute-done.7.refs_4_
  16.9 0.5 %combine_project.1.refs_0_ = bf16[6,2,2048]{2,1,0:T(2,128)(2,1)S(1)} custom-call(f32[32,384]{1,0:T(8,128)S(1)} %own_keys.1.refs_0_, bf16[32,384]{1,0:T(8,128)(2,1)S(1)} %prefix_keys.2.refs_1_, bf16[32,384]{1,0:T(8,128)(2,1)S(1)} %collective-permute-done.5.refs_2_, bf16[32,384]{1,0:T(8,128)(2,1)S(1)} %collective-permute-done.6.refs_3_, ...), custom_call_target="tpu_custom_call" | custom-call | flops 33554432 | bytes 2097152 | tf_op jit(solution)/shard_map/combine_project/pallas_call | solution.py:412
  17.4 2.5 %collective-permute-start.10 = (bf16[6,2,2048]{2,1,0:T(2,128)(2,1)S(1)}, bf16[6,2,2048]{2,1,0:T(2,128)(2,1)S(1)}, u32[]{:S(2)}, u32[]{:S(2)}) collective-permute-start(bf16[6,2,2048]{2,1,0:T(2,128)(2,1)S(1)} %combine_project.1.refs_0_), channel_id=1, source_target_pairs={{0,24},{8,16},{16,8},{24,0},{1,25},{9,17},{17,9},{25,1},{2,26},{10... | collective-permute-start | bytes 147464 | tf_op jit(solution)/shard_map/ppermute | solution.py:307
  19.9 0.5 %collective-permute-start.8 = (bf16[6,2,2048]{2,1,0:T(2,128)(2,1)S(1)}, bf16[6,2,2048]{2,1,0:T(2,128)(2,1)S(1)}, u32[]{:S(2)}, u32[]{:S(2)}) collective-permute-start(bf16[6,2,2048]{2,1,0:T(2,128)(2,1)S(1)} %combine_project.1.refs_0_), channel_id=1, source_target_pairs={{0,8},{8,0},{16,24},{24,16},{1,9},{9,1},{17,25},{25,17},{2,10},{10... | collective-permute-start | bytes 147464 | tf_op jit(solution)/shard_map/ppermute | solution.py:307
  20.4 0.5 %collective-permute-start.9 = (bf16[6,2,2048]{2,1,0:T(2,128)(2,1)S(1)}, bf16[6,2,2048]{2,1,0:T(2,128)(2,1)S(1)}, u32[]{:S(2)}, u32[]{:S(2)}) collective-permute-start(bf16[6,2,2048]{2,1,0:T(2,128)(2,1)S(1)} %combine_project.1.refs_0_), channel_id=1, source_target_pairs={{0,16},{8,24},{16,0},{24,8},{1,17},{9,25},{17,1},{25,9},{2,18},{10... | collective-permute-start | bytes 147464 | tf_op jit(solution)/shard_map/ppermute | solution.py:307
  20.9 1.7 %collective-permute-done.10.refs_3_ = bf16[6,2,2048]{2,1,0:T(2,128)(2,1)S(1)} collective-permute-done((bf16[6,2,2048]{2,1,0:T(2,128)(2,1)S(1)}, bf16[6,2,2048]{2,1,0:T(2,128)(2,1)S(1)}, u32[]{:S(2)}, u32[]{:S(2)}) %collective-permute-start.10) | collective-permute-done | bytes 49184 | tf_op jit(solution)/shard_map/ppermute | solution.py:307
  22.6 1.4 %collective-permute-done.8.refs_1_ = bf16[6,2,2048]{2,1,0:T(2,128)(2,1)S(1)} collective-permute-done((bf16[6,2,2048]{2,1,0:T(2,128)(2,1)S(1)}, bf16[6,2,2048]{2,1,0:T(2,128)(2,1)S(1)}, u32[]{:S(2)}, u32[]{:S(2)}) %collective-permute-start.8) | collective-permute-done | bytes 49184 | tf_op jit(solution)/shard_map/ppermute | solution.py:307
  24.0 0.5 %collective-permute-done.9.refs_2_ = bf16[6,2,2048]{2,1,0:T(2,128)(2,1)S(1)} collective-permute-done((bf16[6,2,2048]{2,1,0:T(2,128)(2,1)S(1)}, bf16[6,2,2048]{2,1,0:T(2,128)(2,1)S(1)}, u32[]{:S(2)}, u32[]{:S(2)}) %collective-permute-start.9) | collective-permute-done | bytes 49184 | tf_op jit(solution)/shard_map/ppermute | solution.py:307
  24.5 0.0 copy-done.3
  24.5 0.0 copy-done.6
  24.5 0.0 copy-done.7
  24.5 0.8 %residual_scores.1 = (bf16[6,2,2048]{2,1,0:T(2,128)(2,1)}, f32[6]{0:T(128)}) custom-call(bf16[6,2,2048]{2,1,0:T(2,128)(2,1)S(1)} %combine_project.1.refs_0_, bf16[6,2,2048]{2,1,0:T(2,128)(2,1)S(1)} %collective-permute-done.8.refs_1_, bf16[6,2,2048]{2,1,0:T(2,128)(2,1)S(1)} %collective-permute-done.9.refs_2_, ...), custom_call_target="tpu_custom_call" | custom-call | flops 1 | bytes 294912 | tf_op jit(solution)/shard_map/residual_scores/pallas_call | solution.py:437
Async XLA Ops:
  0.6 6.9 %copy-start.1 = (bf16[1,24,64,512]{3,2,1,0:T(8,128)(2,1)S(1)}, bf16[1,24,64,512]{3,2,1,0:T(8,128)(2,1)}, u32[]{:S(2)}) copy-start(bf16[1,24,64,512]{3,2,1,0:T(8,128)(2,1)} %param.12) | copy-start | bytes 4718596
  0.6 6.9 %collective-permute-start.1 = (bf16[24,64,512]{2,1,0:T(8,128)(2,1)}, bf16[24,64,512]{2,1,0:T(8,128)(2,1)S(1)}, u32[]{:S(2)}, u32[]{:S(2)}) collective-permute-start(bf16[24,64,512]{2,1,0:T(8,128)(2,1)} %bitcast.5), channel_id=1, source_target_pairs={{0,1},{1,0},{2,3},{3,2},{4,5},{5,4},{6,7},{7,6},{8,9},{9,8},{10,11... | collective-permute-start | bytes 4718600 | tf_op jit(solution)/shard_map/ppermute | solution.py:307
  1.2 7.4 %collective-permute-start.2 = (bf16[6,2,512]{2,1,0:T(2,128)(2,1)}, bf16[6,2,512]{2,1,0:T(2,128)(2,1)S(1)}, u32[]{:S(2)}, u32[]{:S(2)}) collective-permute-start(bf16[6,2,512]{2,1,0:T(2,128)(2,1)} %q_ref.3), channel_id=1, source_target_pairs={{0,5},{1,4},{2,7},{3,6},{4,1},{5,0},{6,3},{7,2},{8,13},{9,12},{10,... | collective-permute-start | bytes 36872 | tf_op jit(solution)/shard_map/ppermute | solution.py:307
  4.9 5.1 %collective-permute-start.3 = (bf16[6,2,512]{2,1,0:T(2,128)(2,1)}, bf16[6,2,512]{2,1,0:T(2,128)(2,1)S(1)}, u32[]{:S(2)}, u32[]{:S(2)}) collective-permute-start(bf16[6,2,512]{2,1,0:T(2,128)(2,1)} %q_ref.3), channel_id=1, source_target_pairs={{0,7},{1,6},{2,5},{3,4},{4,3},{5,2},{6,1},{7,0},{8,15},{9,14},{10,... | collective-permute-start | bytes 36872 | tf_op jit(solution)/shard_map/ppermute | solution.py:307
  5.9 4.1 %collective-permute-start.4 = (bf16[6,2,512]{2,1,0:T(2,128)(2,1)}, bf16[6,2,512]{2,1,0:T(2,128)(2,1)S(1)}, u32[]{:S(2)}, u32[]{:S(2)}) collective-permute-start(bf16[6,2,512]{2,1,0:T(2,128)(2,1)} %q_ref.3), channel_id=1, source_target_pairs={{0,3},{1,2},{2,1},{3,0},{4,7},{5,6},{6,5},{7,4},{8,11},{9,10},{10,... | collective-permute-start | bytes 36872 | tf_op jit(solution)/shard_map/ppermute | solution.py:307
  6.1 1.4 %collective-permute-start = (s32[24]{0:T(128)}, s32[24]{0:T(128)S(1)}, u32[]{:S(2)}, u32[]{:S(2)}) collective-permute-start(s32[24]{0:T(128)} %page_hbm.1), channel_id=1, source_target_pairs={{0,1},{1,0},{2,3},{3,2},{4,5},{5,4},{6,7},{7,6},{8,9},{9,8},{10,11... | collective-permute-start | bytes 296 | tf_op jit(solution)/shard_map/ppermute | solution.py:307
  10.0 4.8 %copy-start = (bf16[512,2048]{1,0:T(8,128)(2,1)S(1)}, bf16[512,2048]{1,0:T(8,128)(2,1)}, u32[]{:S(2)}) copy-start(bf16[512,2048]{1,0:T(8,128)(2,1)} %refs_5_.1) | copy-start | bytes 6291460
  10.0 4.8 %copy-start.2 = (bf16[1,6,128,512]{3,2,1,0:T(8,128)(2,1)S(1)}, bf16[1,6,128,512]{3,2,1,0:T(8,128)(2,1)}, u32[]{:S(2)}) copy-start(bf16[1,6,128,512]{3,2,1,0:T(8,128)(2,1)} %param.17) | copy-start | bytes 2359300
  10.0 4.8 %copy-start.4 = (bf16[6,2,512]{2,1,0:T(2,128)(2,1)S(1)}, bf16[6,2,512]{2,1,0:T(2,128)(2,1)}, u32[]{:S(2)}) copy-start(bf16[6,2,512]{2,1,0:T(2,128)(2,1)} %q_ref.3) | copy-start | bytes 36868
  10.0 4.8 %copy-start.5 = (bf16[1,6,2,512]{3,2,1,0:T(2,128)(2,1)S(1)}, bf16[1,6,2,512]{3,2,1,0:T(2,128)(2,1)}, u32[]{:S(2)}) copy-start(bf16[1,6,2,512]{3,2,1,0:T(2,128)(2,1)} %param.19) | copy-start | bytes 36868
  10.0 4.8 %copy-start.8 = (s32[6]{0:T(128)S(1)}, s32[6]{0:T(128)}, u32[]{:S(2)}) copy-start(s32[6]{0:T(128)} %len_ref.1) | copy-start | bytes 76
  10.9 5.7 %collective-permute-start.5 = (bf16[32,384]{1,0:T(8,128)(2,1)S(1)}, bf16[32,384]{1,0:T(8,128)(2,1)S(1)}, u32[]{:S(2)}, u32[]{:S(2)}) collective-permute-start(bf16[32,384]{1,0:T(8,128)(2,1)S(1)} %get-tuple-element.19), channel_id=1, source_target_pairs={{0,7},{1,6},{2,5},{3,4},{4,3},{5,2},{6,1},{7,0},{8,15},{9,14},{10,... | collective-permute-start | bytes 73736 | tf_op jit(solution)/shard_map/ppermute | solution.py:307
  12.7 4.0 %collective-permute-start.6 = (bf16[32,384]{1,0:T(8,128)(2,1)S(1)}, bf16[32,384]{1,0:T(8,128)(2,1)S(1)}, u32[]{:S(2)}, u32[]{:S(2)}) collective-permute-start(bf16[32,384]{1,0:T(8,128)(2,1)S(1)} %get-tuple-element.20), channel_id=1, source_target_pairs={{0,3},{1,2},{2,1},{3,0},{4,7},{5,6},{6,5},{7,4},{8,11},{9,10},{10,... | collective-permute-start | bytes 73736 | tf_op jit(solution)/shard_map/ppermute | solution.py:307
  12.7 4.2 %collective-permute-start.7 = (bf16[32,384]{1,0:T(8,128)(2,1)S(1)}, bf16[32,384]{1,0:T(8,128)(2,1)S(1)}, u32[]{:S(2)}, u32[]{:S(2)}) collective-permute-start(bf16[32,384]{1,0:T(8,128)(2,1)S(1)} %get-tuple-element.21), channel_id=1, source_target_pairs={{0,5},{1,4},{2,7},{3,6},{4,1},{5,0},{6,3},{7,2},{8,13},{9,12},{10,... | collective-permute-start | bytes 73736 | tf_op jit(solution)/shard_map/ppermute | solution.py:307
  16.6 7.9 %copy-start.3 = (bf16[6,2,2048]{2,1,0:T(2,128)(2,1)S(1)}, bf16[6,2,2048]{2,1,0:T(2,128)(2,1)}, u32[]{:S(2)}) copy-start(bf16[6,2,2048]{2,1,0:T(2,128)(2,1)} %refs_4_.1) | copy-start | bytes 147460
  16.6 7.9 %copy-start.6 = (f32[2048]{0:T(1024)S(1)}, f32[2048]{0:T(1024)}, u32[]{:S(2)}) copy-start(f32[2048]{0:T(1024)} %param.22) | copy-start | bytes 24580
  16.6 7.9 %copy-start.7 = (f32[2048]{0:T(1024)S(1)}, f32[2048]{0:T(1024)}, u32[]{:S(2)}) copy-start(f32[2048]{0:T(1024)} %param.23) | copy-start | bytes 24580
  17.4 5.2 %collective-permute-start.10 = (bf16[6,2,2048]{2,1,0:T(2,128)(2,1)S(1)}, bf16[6,2,2048]{2,1,0:T(2,128)(2,1)S(1)}, u32[]{:S(2)}, u32[]{:S(2)}) collective-permute-start(bf16[6,2,2048]{2,1,0:T(2,128)(2,1)S(1)} %combine_project.1.refs_0_), channel_id=1, source_target_pairs={{0,24},{8,16},{16,8},{24,0},{1,25},{9,17},{17,9},{25,1},{2,26},{10... | collective-permute-start | bytes 147464 | tf_op jit(solution)/shard_map/ppermute | solution.py:307
  19.9 4.1 %collective-permute-start.8 = (bf16[6,2,2048]{2,1,0:T(2,128)(2,1)S(1)}, bf16[6,2,2048]{2,1,0:T(2,128)(2,1)S(1)}, u32[]{:S(2)}, u32[]{:S(2)}) collective-permute-start(bf16[6,2,2048]{2,1,0:T(2,128)(2,1)S(1)} %combine_project.1.refs_0_), channel_id=1, source_target_pairs={{0,8},{8,0},{16,24},{24,16},{1,9},{9,1},{17,25},{25,17},{2,10},{10... | collective-permute-start | bytes 147464 | tf_op jit(solution)/shard_map/ppermute | solution.py:307
  20.4 4.1 %collective-permute-start.9 = (bf16[6,2,2048]{2,1,0:T(2,128)(2,1)S(1)}, bf16[6,2,2048]{2,1,0:T(2,128)(2,1)S(1)}, u32[]{:S(2)}, u32[]{:S(2)}) collective-permute-start(bf16[6,2,2048]{2,1,0:T(2,128)(2,1)S(1)} %combine_project.1.refs_0_), channel_id=1, source_target_pairs={{0,16},{8,24},{16,0},{24,8},{1,17},{9,25},{17,1},{25,9},{2,18},{10... | collective-permute-start | bytes 147464 | tf_op jit(solution)/shard_map/ppermute | solution.py:307

commit v8 on v7

--- a/solution.py
+++ b/solution.py
@@ -88,21 +88,20 @@
         return start + lax.div(len_ref[p] + page_tokens - 1, page_tokens) * page_tokens
 
     lax.fori_loop(0, prompts, place, jnp.int32(0), unroll=prompts <= 4)
-    request = iota((rows, LANES), 0) // drafts
+    request = iota((heads * rows, LANES), 0) % rows // drafts
 
     def one(j, _):
         device = device_of(j, me)
-        low = jnp.zeros((rows, LANES), jnp.int32)
+        low = jnp.zeros((heads * rows, LANES), jnp.int32)
         high = low
         for r in range(local):
             prompt = lax.shift_right_logical(ids_ref[device * local + r], shift)
             start = start_ref[prompt]
             low = jnp.where(request == r, start, low)
             high = jnp.where(request == r, start + len_ref[prompt], high)
-        for c in range(heads):
-            place_at = pl.ds((j * heads + c) * rows, rows)
-            low_ref[place_at, :] = low
-            high_ref[place_at, :] = high
+        place_at = pl.ds(j * heads * rows, heads * rows)
+        low_ref[place_at, :] = low
+        high_ref[place_at, :] = high
         return 0
 
     if slots <= 8:
@@ -182,7 +181,8 @@
     tail = tail_ref.shape[1]
     head_size = tail_ref.shape[2] // 2
     spread_rows(q_rows, 0, q_ref, heads, head_size, rows)
-    spread_rows(f_rows, 0, fresh_ref, 2, head_size, rows)
+    fresh_rows = f_rows.shape[0] // 2
+    spread_rows(f_rows, 0, fresh_ref, 2, head_size, fresh_rows)
     queries = q_rows[...]
     contract = (((1,), (1,)), ((), ()))
     logits = lax.dot_general(
@@ -197,10 +197,10 @@
         live = (row // drafts == r) & (lane < len_ref[r])
         parts.append(jnp.where(live, logits[:, r * tail:(r + 1) * tail] * scale, FLOOR))
     fresh = lax.dot_general(
-        queries, f_rows[0:rows, :], contract, preferred_element_type=jnp.float32
-    )
-    row = iota((total, rows), 0) % rows
-    key = iota((total, rows), 1)
+        queries, f_rows[0:fresh_rows, :], contract, preferred_element_type=jnp.float32
+    )
+    row = iota((total, fresh_rows), 0) % rows
+    key = iota((total, fresh_rows), 1)
     live = (row // drafts == key // drafts) & (key % drafts <= row % drafts)
     fresh = jnp.where(live, fresh * scale, FLOOR)
     logits = jnp.concatenate(parts, axis=1)
@@ -216,7 +216,7 @@
         preferred_element_type=jnp.float32,
     )
     num = num + jnp.dot(
-        fresh.astype(jnp.bfloat16), f_rows[rows:2 * rows, :], preferred_element_type=jnp.float32
+        fresh.astype(jnp.bfloat16), f_rows[fresh_rows:2 * fresh_rows, :], preferred_element_type=jnp.float32
     )
     out_ref[:, :head_size] = num
     out_ref[:, head_size:] = pack_stats(peak, den)
@@ -234,11 +234,11 @@
 
 def project(num, den, weight_ref, out_ref, heads, rows):
     reqs, drafts, _ = out_ref.shape
-    attention = (num / den).astype(jnp.bfloat16)
+    attention = num / den
     head_size = attention.shape[1]
     value = sum(
         jnp.dot(
-            attention[c * rows:(c + 1) * rows, :], weight_ref[c * head_size:(c + 1) * head_size, :],
+            attention[c * rows:(c + 1) * rows, :].astype(jnp.bfloat16), weight_ref[c * head_size:(c + 1) * head_size, :],
             preferred_element_type=jnp.float32,
         )
         for c in range(heads)
@@ -293,7 +293,9 @@
     head_size = head_pair // 2
     local, drafts, head_width = queries.shape
     heads = head_width // head_size
-    rows = round_up(local * drafts, 16)
+    rows = local * drafts
+    if heads * rows % 8:
+        rows = round_up(rows, 16)
     per = heads * rows
     keys = page_count * page_tokens
     width = hidden.shape[2]
@@ -356,7 +358,7 @@
         out_specs=VMEM,
         scratch_shapes=[
             pltpu.VMEM((per, head_size), jnp.bfloat16),
-            pltpu.VMEM((2 * rows, head_size), jnp.bfloat16),
+            pltpu.VMEM((2 * round_up(local * drafts, 16), head_size), jnp.bfloat16),
         ],
         compiler_params=vmem(8),
         cost_estimate=cost(4 * per * local * tail_cache.shape[2] * head_size, 2 * tail_cache.size),

time: 25.5 us -> 25.3 us (level)
  no operation moved by 1% of the time
where the time goes in v8:
time: 25.3 us; the launch traced here: 25.1 us
  starting transfers between devices  13.4 us (53%)
  Pallas kernels  5.67 us (22%)
  waiting for transfers between devices  5.27 us (21%)
  between operations  0.75 us (3%)
    ppermute x11, starting transfers between devices, swap(): return lax.ppermute(x, axis, [(i, i ^ mask) for i in range(size)])  13.4 us
    ppermute x11, waiting for transfers between devices, swap(): return lax.ppermute(x, axis, [(i, i ^ mask) for i in range(size)])  5.27 us
    pallas_call x2, Pallas kernels, prefix_column(): pl.pallas_call(functools.partial(prefix_kernel, heads, rows, scale, count...  1.41 us
    pallas_call x1, Pallas kernels, body(): pl.pallas_call(functools.partial(own_kernel, heads, rows, scale), out_sha...  1.07 us
    pallas_call x1, Pallas kernels, body(): pl.pallas_call(functools.partial(flip_kernel, page_tokens), out_shape=(ja...  1.03 us
    pallas_call x1, Pallas kernels, body(): pl.pallas_call(functools.partial(layout_kernel, device_of, slots, local,...  0.86 us
    pallas_call x1, Pallas kernels, body(): pl.pallas_call(final_kernel, out_shape=(jax.ShapeDtypeStruct(hidden.shape...  0.77 us
    pallas_call x1, Pallas kernels, body(): pl.pallas_call(functools.partial(combine_kernel, heads, rows, head_size),...  0.52 us
  transfers between devices with their start and end apart: 11, of which 6 were waited for; matrix products, arithmetic and copies ran while one was open for 0% of the time, Pallas kernels for 15%

profile of v8, /device:TPU:0, one launch (start us, length us, event | category | flops | bytes accessed | tf_op | source)
XLA Modules:
  0.0 25.1 jit_solution(10940842086226423054)
XLA Ops:
  0.6 0.0 copy-start.1
  0.6 0.5 %collective-permute-start.1 = (bf16[24,64,512]{2,1,0:T(8,128)(2,1)}, bf16[24,64,512]{2,1,0:T(8,128)(2,1)S(1)}, u32[]{:S(2)}, u32[]{:S(2)}) collective-permute-start(bf16[24,64,512]{2,1,0:T(8,128)(2,1)} %bitcast.5), channel_id=1, source_target_pairs={{0,1},{1,0},{2,3},{3,2},{4,5},{5,4},{6,7},{7,6},{8,9},{9,8},{10,11... | collective-permute-start | bytes 4718600 | tf_op jit(solution)/shard_map/ppermute | solution.py:309
  1.2 3.7 %collective-permute-start.2 = (bf16[6,2,512]{2,1,0:T(2,128)(2,1)}, bf16[6,2,512]{2,1,0:T(2,128)(2,1)S(1)}, u32[]{:S(2)}, u32[]{:S(2)}) collective-permute-start(bf16[6,2,512]{2,1,0:T(2,128)(2,1)} %q_ref.3), channel_id=1, source_target_pairs={{0,5},{1,4},{2,7},{3,6},{4,1},{5,0},{6,3},{7,2},{8,13},{9,12},{10,... | collective-permute-start | bytes 36872 | tf_op jit(solution)/shard_map/ppermute | solution.py:309
  4.9 1.0 %collective-permute-start.3 = (bf16[6,2,512]{2,1,0:T(2,128)(2,1)}, bf16[6,2,512]{2,1,0:T(2,128)(2,1)S(1)}, u32[]{:S(2)}, u32[]{:S(2)}) collective-permute-start(bf16[6,2,512]{2,1,0:T(2,128)(2,1)} %q_ref.3), channel_id=1, source_target_pairs={{0,7},{1,6},{2,5},{3,4},{4,3},{5,2},{6,1},{7,0},{8,15},{9,14},{10,... | collective-permute-start | bytes 36872 | tf_op jit(solution)/shard_map/ppermute | solution.py:309
  5.9 0.2 collective-permute-start.4
  6.1 0.4 %collective-permute-start = (s32[24]{0:T(128)}, s32[24]{0:T(128)S(1)}, u32[]{:S(2)}, u32[]{:S(2)}) collective-permute-start(s32[24]{0:T(128)} %page_hbm.1), channel_id=1, source_target_pairs={{0,1},{1,0},{2,3},{3,2},{4,5},{5,4},{6,7},{7,6},{8,9},{9,8},{10,11... | collective-permute-start | bytes 296 | tf_op jit(solution)/shard_map/ppermute | solution.py:309
  6.6 0.9 %key_ranges.1 = (s32[96,128]{1,0:T(8,128)S(1)}, s32[96,128]{1,0:T(8,128)S(1)}, s32[8,1536]{1,0:T(8,128)S(1)}, bf16[6,2,512]{2,1,0:T(2,128)(2,1)S(1)}) custom-call(s32[48]{0:T(128)} %ids_hbm.1, s32[3]{0:T(128)} %len_hbm.1, s32[24]{0:T(128)} %page_hbm.1, bf16[6,2,512]{2,1,0:T(2,128)(2,1)} %q_ref.3), custom_call_target="tpu_custom_call" | custom-call | flops 4000000000 | bytes 98304 | tf_op jit(solution)/shard_map/key_ranges/pallas_call | solution.py:321
  7.4 0.1 collective-permute-done.refs_0_
  7.5 0.0 collective-permute-done.1.refs_2_.refs_8_.refs_10_
  7.5 0.0 copy-done.1
  7.5 1.0 %flip_keys.1 = (s32[8,1536]{1,0:T(8,128)S(1)}, bf16[256,1536]{1,0:T(8,128)(2,1)S(1)}, bf16[256,1536]{1,0:T(8,128)(2,1)S(1)}) custom-call(s32[24]{0:T(128)S(1)} %collective-permute-done.refs_0_, bf16[24,64,512]{2,1,0:T(8,128)(2,1)S(1)} %bitcast.6, bf16[24,64,512]{2,1,0:T(8,128)(2,1)S(1)} %collective-permute-done.1.refs_2_.refs_8_.refs_10_), custom_call_target="tpu_custom_call" | custom-call | flops 1000000000 | bytes 6291456 | tf_op jit(solution)/shard_map/flip_keys/pallas_call | solution.py:342
  8.6 0.0 collective-permute-done.2.refs_0_
  8.6 1.4 %collective-permute-done.3.refs_1_ = bf16[6,2,512]{2,1,0:T(2,128)(2,1)S(1)} collective-permute-done((bf16[6,2,512]{2,1,0:T(2,128)(2,1)}, bf16[6,2,512]{2,1,0:T(2,128)(2,1)S(1)}, u32[]{:S(2)}, u32[]{:S(2)}) %collective-permute-start.3) | collective-permute-done | bytes 12320 | tf_op jit(solution)/shard_map/ppermute | solution.py:309
  10.0 0.0 collective-permute-done.4.refs_2_
  10.0 0.0 copy-start
  10.0 0.0 copy-start.2
  10.0 0.0 copy-start.4
  10.0 0.0 copy-start.5
  10.0 0.0 copy-start.8
  10.0 0.7 %prefix_keys.3 = (bf16[24,384]{1,0:T(8,128)(2,1)S(1)}, bf16[24,384]{1,0:T(8,128)(2,1)S(1)}, bf16[24,384]{1,0:T(8,128)(2,1)S(1)}) custom-call(bf16[6,2,512]{2,1,0:T(2,128)(2,1)S(1)} %collective-permute-done.2.refs_0_, bf16[6,2,512]{2,1,0:T(2,128)(2,1)S(1)} %collective-permute-done.3.refs_1_, bf16[6,2,512]{2,1,0:T(2,128)(2,1)S(1)} %collective-permute-done.4.refs_2_, ...), custom_call_target="tpu_custom_call" | custom-call | flops 226492416 | bytes 3145728 | tf_op jit(solution)/shard_map/prefix_keys/pallas_call | solution.py:374
  10.8 1.8 %collective-permute-start.5 = (bf16[24,384]{1,0:T(8,128)(2,1)S(1)}, bf16[24,384]{1,0:T(8,128)(2,1)S(1)}, u32[]{:S(2)}, u32[]{:S(2)}) collective-permute-start(bf16[24,384]{1,0:T(8,128)(2,1)S(1)} %get-tuple-element.19), channel_id=1, source_target_pairs={{0,7},{1,6},{2,5},{3,4},{4,3},{5,2},{6,1},{7,0},{8,15},{9,14},{10,... | collective-permute-start | bytes 55304 | tf_op jit(solution)/shard_map/ppermute | solution.py:309
  12.6 0.0 collective-permute-start.6
  12.6 2.1 %collective-permute-start.7 = (bf16[24,384]{1,0:T(8,128)(2,1)S(1)}, bf16[24,384]{1,0:T(8,128)(2,1)S(1)}, u32[]{:S(2)}, u32[]{:S(2)}) collective-permute-start(bf16[24,384]{1,0:T(8,128)(2,1)S(1)} %get-tuple-element.21), channel_id=1, source_target_pairs={{0,5},{1,4},{2,7},{3,6},{4,1},{5,0},{6,3},{7,2},{8,13},{9,12},{10,... | collective-permute-start | bytes 55304 | tf_op jit(solution)/shard_map/ppermute | solution.py:309
  14.7 0.0 copy-done
  14.7 0.0 copy-done.2
  14.7 0.0 copy-done.4
  14.7 0.0 copy-done.5
  14.7 0.0 copy-done.8
  14.7 1.1 %own_keys.1.refs_0_ = f32[24,384]{1,0:T(8,128)S(1)} custom-call(s32[6]{0:T(128)S(1)} %copy-done.8, bf16[6,2,512]{2,1,0:T(2,128)(2,1)S(1)} %copy-done.4, bf16[6,128,512]{2,1,0:T(8,128)(2,1)S(1)} %bitcast.9, bf16[6,2,512]{2,1,0:T(2,128)(2,1)S(1)} %bitcast.10, bf16[512,2048]{1,0:T(8,128)(2,1)S(1)} %copy-done), custom_call_target="tpu_custom_call" | custom-call | flops 18874368 | bytes 786432 | tf_op jit(solution)/shard_map/own_keys/pallas_call | solution.py:354
  15.8 0.7 %prefix_keys.2.refs_1_ = bf16[24,384]{1,0:T(8,128)(2,1)S(1)} custom-call(bf16[6,2,512]{2,1,0:T(2,128)(2,1)S(1)} %get-tuple-element.12.refs_0_, s32[96,128]{1,0:T(8,128)S(1)} %get-tuple-element.13.refs_1_.refs_3_, s32[96,128]{1,0:T(8,128)S(1)} %get-tuple-element.14.refs_2_.refs_4_, s32[8,1536]{1,0:T(8,128)S(1)} %get-tuple-element.15.refs_3_.refs_5_, ...), custom_call_target="tpu_custom_call" | custom-call | flops 75497472 | bytes 3145728 | tf_op jit(solution)/shard_map/prefix_keys/pallas_call | solution.py:374
  16.5 0.0 copy-start.3
  16.5 0.0 copy-start.6
  16.5 0.0 copy-start.7
  16.5 0.0 collective-permute-done.5.refs_2_
  16.5 0.0 collective-permute-done.6.refs_3_
  16.5 0.2 collective-permute-done.7.refs_4_
  16.7 0.5 %combine_project.1.refs_0_ = bf16[6,2,2048]{2,1,0:T(2,128)(2,1)S(1)} custom-call(f32[24,384]{1,0:T(8,128)S(1)} %own_keys.1.refs_0_, bf16[24,384]{1,0:T(8,128)(2,1)S(1)} %prefix_keys.2.refs_1_, bf16[24,384]{1,0:T(8,128)(2,1)S(1)} %collective-permute-done.5.refs_2_, bf16[24,384]{1,0:T(8,128)(2,1)S(1)} %collective-permute-done.6.refs_3_, ...), custom_call_target="tpu_custom_call" | custom-call | flops 25165824 | bytes 2097152 | tf_op jit(solution)/shard_map/combine_project/pallas_call | solution.py:414
  17.2 2.5 %collective-permute-start.10 = (bf16[6,2,2048]{2,1,0:T(2,128)(2,1)S(1)}, bf16[6,2,2048]{2,1,0:T(2,128)(2,1)S(1)}, u32[]{:S(2)}, u32[]{:S(2)}) collective-permute-start(bf16[6,2,2048]{2,1,0:T(2,128)(2,1)S(1)} %combine_project.1.refs_0_), channel_id=1, source_target_pairs={{0,24},{8,16},{16,8},{24,0},{1,25},{9,17},{17,9},{25,1},{2,26},{10... | collective-permute-start | bytes 147464 | tf_op jit(solution)/shard_map/ppermute | solution.py:309
  19.7 0.5 %collective-permute-start.8 = (bf16[6,2,2048]{2,1,0:T(2,128)(2,1)S(1)}, bf16[6,2,2048]{2,1,0:T(2,128)(2,1)S(1)}, u32[]{:S(2)}, u32[]{:S(2)}) collective-permute-start(bf16[6,2,2048]{2,1,0:T(2,128)(2,1)S(1)} %combine_project.1.refs_0_), channel_id=1, source_target_pairs={{0,8},{8,0},{16,24},{24,16},{1,9},{9,1},{17,25},{25,17},{2,10},{10... | collective-permute-start | bytes 147464 | tf_op jit(solution)/shard_map/ppermute | solution.py:309
  20.2 0.5 %collective-permute-start.9 = (bf16[6,2,2048]{2,1,0:T(2,128)(2,1)S(1)}, bf16[6,2,2048]{2,1,0:T(2,128)(2,1)S(1)}, u32[]{:S(2)}, u32[]{:S(2)}) collective-permute-start(bf16[6,2,2048]{2,1,0:T(2,128)(2,1)S(1)} %combine_project.1.refs_0_), channel_id=1, source_target_pairs={{0,16},{8,24},{16,0},{24,8},{1,17},{9,25},{17,1},{25,9},{2,18},{10... | collective-permute-start | bytes 147464 | tf_op jit(solution)/shard_map/ppermute | solution.py:309
  20.7 1.6 %collective-permute-done.10.refs_3_ = bf16[6,2,2048]{2,1,0:T(2,128)(2,1)S(1)} collective-permute-done((bf16[6,2,2048]{2,1,0:T(2,128)(2,1)S(1)}, bf16[6,2,2048]{2,1,0:T(2,128)(2,1)S(1)}, u32[]{:S(2)}, u32[]{:S(2)}) %collective-permute-start.10) | collective-permute-done | bytes 49184 | tf_op jit(solution)/shard_map/ppermute | solution.py:309
  22.3 1.5 %collective-permute-done.8.refs_1_ = bf16[6,2,2048]{2,1,0:T(2,128)(2,1)S(1)} collective-permute-done((bf16[6,2,2048]{2,1,0:T(2,128)(2,1)S(1)}, bf16[6,2,2048]{2,1,0:T(2,128)(2,1)S(1)}, u32[]{:S(2)}, u32[]{:S(2)}) %collective-permute-start.8) | collective-permute-done | bytes 49184 | tf_op jit(solution)/shard_map/ppermute | solution.py:309
  23.8 0.5 %collective-permute-done.9.refs_2_ = bf16[6,2,2048]{2,1,0:T(2,128)(2,1)S(1)} collective-permute-done((bf16[6,2,2048]{2,1,0:T(2,128)(2,1)S(1)}, bf16[6,2,2048]{2,1,0:T(2,128)(2,1)S(1)}, u32[]{:S(2)}, u32[]{:S(2)}) %collective-permute-start.9) | collective-permute-done | bytes 49184 | tf_op jit(solution)/shard_map/ppermute | solution.py:309
  24.3 0.0 copy-done.3
  24.3 0.0 copy-done.6
  24.3 0.0 copy-done.7
  24.3 0.8 %residual_scores.1 = (bf16[6,2,2048]{2,1,0:T(2,128)(2,1)}, f32[6]{0:T(128)}) custom-call(bf16[6,2,2048]{2,1,0:T(2,128)(2,1)S(1)} %combine_project.1.refs_0_, bf16[6,2,2048]{2,1,0:T(2,128)(2,1)S(1)} %collective-permute-done.8.refs_1_, bf16[6,2,2048]{2,1,0:T(2,128)(2,1)S(1)} %collective-permute-done.9.refs_2_, ...), custom_call_target="tpu_custom_call" | custom-call | flops 1 | bytes 294912 | tf_op jit(solution)/shard_map/residual_scores/pallas_call | solution.py:439
Async XLA Ops:
  0.6 6.9 %copy-start.1 = (bf16[1,24,64,512]{3,2,1,0:T(8,128)(2,1)S(1)}, bf16[1,24,64,512]{3,2,1,0:T(8,128)(2,1)}, u32[]{:S(2)}) copy-start(bf16[1,24,64,512]{3,2,1,0:T(8,128)(2,1)} %param.12) | copy-start | bytes 4718596
  0.6 6.9 %collective-permute-start.1 = (bf16[24,64,512]{2,1,0:T(8,128)(2,1)}, bf16[24,64,512]{2,1,0:T(8,128)(2,1)S(1)}, u32[]{:S(2)}, u32[]{:S(2)}) collective-permute-start(bf16[24,64,512]{2,1,0:T(8,128)(2,1)} %bitcast.5), channel_id=1, source_target_pairs={{0,1},{1,0},{2,3},{3,2},{4,5},{5,4},{6,7},{7,6},{8,9},{9,8},{10,11... | collective-permute-start | bytes 4718600 | tf_op jit(solution)/shard_map/ppermute | solution.py:309
  1.2 7.4 %collective-permute-start.2 = (bf16[6,2,512]{2,1,0:T(2,128)(2,1)}, bf16[6,2,512]{2,1,0:T(2,128)(2,1)S(1)}, u32[]{:S(2)}, u32[]{:S(2)}) collective-permute-start(bf16[6,2,512]{2,1,0:T(2,128)(2,1)} %q_ref.3), channel_id=1, source_target_pairs={{0,5},{1,4},{2,7},{3,6},{4,1},{5,0},{6,3},{7,2},{8,13},{9,12},{10,... | collective-permute-start | bytes 36872 | tf_op jit(solution)/shard_map/ppermute | solution.py:309
  4.9 5.1 %collective-permute-start.3 = (bf16[6,2,512]{2,1,0:T(2,128)(2,1)}, bf16[6,2,512]{2,1,0:T(2,128)(2,1)S(1)}, u32[]{:S(2)}, u32[]{:S(2)}) collective-permute-start(bf16[6,2,512]{2,1,0:T(2,128)(2,1)} %q_ref.3), channel_id=1, source_target_pairs={{0,7},{1,6},{2,5},{3,4},{4,3},{5,2},{6,1},{7,0},{8,15},{9,14},{10,... | collective-permute-start | bytes 36872 | tf_op jit(solution)/shard_map/ppermute | solution.py:309
  5.9 4.1 %collective-permute-start.4 = (bf16[6,2,512]{2,1,0:T(2,128)(2,1)}, bf16[6,2,512]{2,1,0:T(2,128)(2,1)S(1)}, u32[]{:S(2)}, u32[]{:S(2)}) collective-permute-start(bf16[6,2,512]{2,1,0:T(2,128)(2,1)} %q_ref.3), channel_id=1, source_target_pairs={{0,3},{1,2},{2,1},{3,0},{4,7},{5,6},{6,5},{7,4},{8,11},{9,10},{10,... | collective-permute-start | bytes 36872 | tf_op jit(solution)/shard_map/ppermute | solution.py:309
  6.1 1.4 %collective-permute-start = (s32[24]{0:T(128)}, s32[24]{0:T(128)S(1)}, u32[]{:S(2)}, u32[]{:S(2)}) collective-permute-start(s32[24]{0:T(128)} %page_hbm.1), channel_id=1, source_target_pairs={{0,1},{1,0},{2,3},{3,2},{4,5},{5,4},{6,7},{7,6},{8,9},{9,8},{10,11... | collective-permute-start | bytes 296 | tf_op jit(solution)/shard_map/ppermute | solution.py:309
  10.0 4.7 %copy-start = (bf16[512,2048]{1,0:T(8,128)(2,1)S(1)}, bf16[512,2048]{1,0:T(8,128)(2,1)}, u32[]{:S(2)}) copy-start(bf16[512,2048]{1,0:T(8,128)(2,1)} %refs_5_.1) | copy-start | bytes 6291460
  10.0 4.7 %copy-start.2 = (bf16[1,6,128,512]{3,2,1,0:T(8,128)(2,1)S(1)}, bf16[1,6,128,512]{3,2,1,0:T(8,128)(2,1)}, u32[]{:S(2)}) copy-start(bf16[1,6,128,512]{3,2,1,0:T(8,128)(2,1)} %param.17) | copy-start | bytes 2359300
  10.0 4.7 %copy-start.4 = (bf16[6,2,512]{2,1,0:T(2,128)(2,1)S(1)}, bf16[6,2,512]{2,1,0:T(2,128)(2,1)}, u32[]{:S(2)}) copy-start(bf16[6,2,512]{2,1,0:T(2,128)(2,1)} %q_ref.3) | copy-start | bytes 36868
  10.0 4.7 %copy-start.5 = (bf16[1,6,2,512]{3,2,1,0:T(2,128)(2,1)S(1)}, bf16[1,6,2,512]{3,2,1,0:T(2,128)(2,1)}, u32[]{:S(2)}) copy-start(bf16[1,6,2,512]{3,2,1,0:T(2,128)(2,1)} %param.19) | copy-start | bytes 36868
  10.0 4.7 %copy-start.8 = (s32[6]{0:T(128)S(1)}, s32[6]{0:T(128)}, u32[]{:S(2)}) copy-start(s32[6]{0:T(128)} %len_ref.1) | copy-start | bytes 76
  10.8 5.7 %collective-permute-start.5 = (bf16[24,384]{1,0:T(8,128)(2,1)S(1)}, bf16[24,384]{1,0:T(8,128)(2,1)S(1)}, u32[]{:S(2)}, u32[]{:S(2)}) collective-permute-start(bf16[24,384]{1,0:T(8,128)(2,1)S(1)} %get-tuple-element.19), channel_id=1, source_target_pairs={{0,7},{1,6},{2,5},{3,4},{4,3},{5,2},{6,1},{7,0},{8,15},{9,14},{10,... | collective-permute-start | bytes 55304 | tf_op jit(solution)/shard_map/ppermute | solution.py:309
  12.6 3.9 %collective-permute-start.6 = (bf16[24,384]{1,0:T(8,128)(2,1)S(1)}, bf16[24,384]{1,0:T(8,128)(2,1)S(1)}, u32[]{:S(2)}, u32[]{:S(2)}) collective-permute-start(bf16[24,384]{1,0:T(8,128)(2,1)S(1)} %get-tuple-element.20), channel_id=1, source_target_pairs={{0,3},{1,2},{2,1},{3,0},{4,7},{5,6},{6,5},{7,4},{8,11},{9,10},{10,... | collective-permute-start | bytes 55304 | tf_op jit(solution)/shard_map/ppermute | solution.py:309
  12.6 4.1 %collective-permute-start.7 = (bf16[24,384]{1,0:T(8,128)(2,1)S(1)}, bf16[24,384]{1,0:T(8,128)(2,1)S(1)}, u32[]{:S(2)}, u32[]{:S(2)}) collective-permute-start(bf16[24,384]{1,0:T(8,128)(2,1)S(1)} %get-tuple-element.21), channel_id=1, source_target_pairs={{0,5},{1,4},{2,7},{3,6},{4,1},{5,0},{6,3},{7,2},{8,13},{9,12},{10,... | collective-permute-start | bytes 55304 | tf_op jit(solution)/shard_map/ppermute | solution.py:309
  16.5 7.9 %copy-start.3 = (bf16[6,2,2048]{2,1,0:T(2,128)(2,1)S(1)}, bf16[6,2,2048]{2,1,0:T(2,128)(2,1)}, u32[]{:S(2)}) copy-start(bf16[6,2,2048]{2,1,0:T(2,128)(2,1)} %refs_4_.1) | copy-start | bytes 147460
  16.5 7.9 %copy-start.6 = (f32[2048]{0:T(1024)S(1)}, f32[2048]{0:T(1024)}, u32[]{:S(2)}) copy-start(f32[2048]{0:T(1024)} %param.22) | copy-start | bytes 24580
  16.5 7.8 %copy-start.7 = (f32[2048]{0:T(1024)S(1)}, f32[2048]{0:T(1024)}, u32[]{:S(2)}) copy-start(f32[2048]{0:T(1024)} %param.23) | copy-start | bytes 24580
  17.2 5.1 %collective-permute-start.10 = (bf16[6,2,2048]{2,1,0:T(2,128)(2,1)S(1)}, bf16[6,2,2048]{2,1,0:T(2,128)(2,1)S(1)}, u32[]{:S(2)}, u32[]{:S(2)}) collective-permute-start(bf16[6,2,2048]{2,1,0:T(2,128)(2,1)S(1)} %combine_project.1.refs_0_), channel_id=1, source_target_pairs={{0,24},{8,16},{16,8},{24,0},{1,25},{9,17},{17,9},{25,1},{2,26},{10... | collective-permute-start | bytes 147464 | tf_op jit(solution)/shard_map/ppermute | solution.py:309
  19.7 4.1 %collective-permute-start.8 = (bf16[6,2,2048]{2,1,0:T(2,128)(2,1)S(1)}, bf16[6,2,2048]{2,1,0:T(2,128)(2,1)S(1)}, u32[]{:S(2)}, u32[]{:S(2)}) collective-permute-start(bf16[6,2,2048]{2,1,0:T(2,128)(2,1)S(1)} %combine_project.1.refs_0_), channel_id=1, source_target_pairs={{0,8},{8,0},{16,24},{24,16},{1,9},{9,1},{17,25},{25,17},{2,10},{10... | collective-permute-start | bytes 147464 | tf_op jit(solution)/shard_map/ppermute | solution.py:309
  20.2 4.1 %collective-permute-start.9 = (bf16[6,2,2048]{2,1,0:T(2,128)(2,1)S(1)}, bf16[6,2,2048]{2,1,0:T(2,128)(2,1)S(1)}, u32[]{:S(2)}, u32[]{:S(2)}) collective-permute-start(bf16[6,2,2048]{2,1,0:T(2,128)(2,1)S(1)} %combine_project.1.refs_0_), channel_id=1, source_target_pairs={{0,16},{8,24},{16,0},{24,8},{1,17},{9,25},{17,1},{25,9},{2,18},{10... | collective-permute-start | bytes 147464 | tf_op jit(solution)/shard_map/ppermute | solution.py:309

commit v9 on v8

--- a/solution.py
+++ b/solution.py
@@ -432,14 +432,20 @@
             cost_estimate=cost(2 * per * head_size * width, 2 * out_weight.size),
             name="combine_project",
         )(own, blocks, out_weight)
+    out_type = hidden.dtype
     if kv in (2, 4):
-        shares = [share] + [swap(share, "kv", kv, j) for j in ORDER_C if j < kv]
+        arrived = {j: swap(share, "kv", kv, j) for j in ORDER_C if j < kv}
+        last = arrived.pop(2 if kv == 4 else 1)
+        early = hidden.astype(jnp.float32) + share.astype(jnp.float32)
+        for value in arrived.values():
+            early = early + value.astype(jnp.float32)
+        hidden, shares = early, [last]
     else:
         shares = [lax.psum(share, "kv")]
     hidden_out, scores = pl.pallas_call(
         final_kernel,
         out_shape=(
-            jax.ShapeDtypeStruct(hidden.shape, hidden.dtype),
+            jax.ShapeDtypeStruct(hidden.shape, out_type),
             jax.ShapeDtypeStruct((local,), jnp.float32),
         ),
         in_specs=[VMEM] * (len(shares) + 3),

time: 25.3 us -> 25.2 us (level)
  no operation moved by 1% of the time
where the time goes in v9:
time: 25.2 us; the launch traced here: 25.1 us
  starting transfers between devices  13.4 us (53%)
  Pallas kernels  5.65 us (22%)
  waiting for transfers between devices  5.17 us (21%)
  between operations  0.75 us (3%)
    ppermute x11, starting transfers between devices, swap(): return lax.ppermute(x, axis, [(i, i ^ mask) for i in range(size)])  13.4 us
    ppermute x11, waiting for transfers between devices, swap(): return lax.ppermute(x, axis, [(i, i ^ mask) for i in range(size)])  5.17 us
    pallas_call x2, Pallas kernels, prefix_column(): pl.pallas_call(functools.partial(prefix_kernel, heads, rows, scale, count...  1.41 us
    pallas_call x1, Pallas kernels, body(): pl.pallas_call(functools.partial(own_kernel, heads, rows, scale), out_sha...  1.07 us
    pallas_call x1, Pallas kernels, body(): pl.pallas_call(functools.partial(flip_kernel, page_tokens), out_shape=(ja...  1.03 us
    pallas_call x1, Pallas kernels, body(): pl.pallas_call(functools.partial(layout_kernel, device_of, slots, local,...  0.86 us
    pallas_call x1, Pallas kernels, body(): pl.pallas_call(final_kernel, out_shape=(jax.ShapeDtypeStruct(hidden.shape...  0.75 us
    pallas_call x1, Pallas kernels, body(): pl.pallas_call(functools.partial(combine_kernel, heads, rows, head_size),...  0.52 us
  transfers between devices with their start and end apart: 11, of which 6 were waited for; matrix products, arithmetic and copies ran while one was open for 0% of the time, Pallas kernels for 15%

profile of v9, /device:TPU:0, one launch (start us, length us, event | category | flops | bytes accessed | tf_op | source)
XLA Modules:
  0.0 25.1 jit_solution(11168134557225117187)
XLA Ops:
  0.6 0.0 copy-start.1
  0.6 0.5 %collective-permute-start.1 = (bf16[24,64,512]{2,1,0:T(8,128)(2,1)}, bf16[24,64,512]{2,1,0:T(8,128)(2,1)S(1)}, u32[]{:S(2)}, u32[]{:S(2)}) collective-permute-start(bf16[24,64,512]{2,1,0:T(8,128)(2,1)} %bitcast.5), channel_id=1, source_target_pairs={{0,1},{1,0},{2,3},{3,2},{4,5},{5,4},{6,7},{7,6},{8,9},{9,8},{10,11... | collective-permute-start | bytes 4718600 | tf_op jit(solution)/shard_map/ppermute | solution.py:309
  1.2 3.7 %collective-permute-start.2 = (bf16[6,2,512]{2,1,0:T(2,128)(2,1)}, bf16[6,2,512]{2,1,0:T(2,128)(2,1)S(1)}, u32[]{:S(2)}, u32[]{:S(2)}) collective-permute-start(bf16[6,2,512]{2,1,0:T(2,128)(2,1)} %q_ref.3), channel_id=1, source_target_pairs={{0,5},{1,4},{2,7},{3,6},{4,1},{5,0},{6,3},{7,2},{8,13},{9,12},{10,... | collective-permute-start | bytes 36872 | tf_op jit(solution)/shard_map/ppermute | solution.py:309
  4.9 1.0 %collective-permute-start.3 = (bf16[6,2,512]{2,1,0:T(2,128)(2,1)}, bf16[6,2,512]{2,1,0:T(2,128)(2,1)S(1)}, u32[]{:S(2)}, u32[]{:S(2)}) collective-permute-start(bf16[6,2,512]{2,1,0:T(2,128)(2,1)} %q_ref.3), channel_id=1, source_target_pairs={{0,7},{1,6},{2,5},{3,4},{4,3},{5,2},{6,1},{7,0},{8,15},{9,14},{10,... | collective-permute-start | bytes 36872 | tf_op jit(solution)/shard_map/ppermute | solution.py:309
  5.9 0.2 collective-permute-start.4
  6.1 0.4 %collective-permute-start = (s32[24]{0:T(128)}, s32[24]{0:T(128)S(1)}, u32[]{:S(2)}, u32[]{:S(2)}) collective-permute-start(s32[24]{0:T(128)} %page_hbm.1), channel_id=1, source_target_pairs={{0,1},{1,0},{2,3},{3,2},{4,5},{5,4},{6,7},{7,6},{8,9},{9,8},{10,11... | collective-permute-start | bytes 296 | tf_op jit(solution)/shard_map/ppermute | solution.py:309
  6.6 0.9 %key_ranges.1 = (s32[96,128]{1,0:T(8,128)S(1)}, s32[96,128]{1,0:T(8,128)S(1)}, s32[8,1536]{1,0:T(8,128)S(1)}, bf16[6,2,512]{2,1,0:T(2,128)(2,1)S(1)}) custom-call(s32[48]{0:T(128)} %ids_hbm.1, s32[3]{0:T(128)} %len_hbm.1, s32[24]{0:T(128)} %page_hbm.1, bf16[6,2,512]{2,1,0:T(2,128)(2,1)} %q_ref.3), custom_call_target="tpu_custom_call" | custom-call | flops 4000000000 | bytes 98304 | tf_op jit(solution)/shard_map/key_ranges/pallas_call | solution.py:321
  7.4 0.1 collective-permute-done.refs_0_
  7.5 0.0 collective-permute-done.1.refs_2_.refs_8_.refs_10_
  7.5 0.0 copy-done.1
  7.5 1.0 %flip_keys.1 = (s32[8,1536]{1,0:T(8,128)S(1)}, bf16[256,1536]{1,0:T(8,128)(2,1)S(1)}, bf16[256,1536]{1,0:T(8,128)(2,1)S(1)}) custom-call(s32[24]{0:T(128)S(1)} %collective-permute-done.refs_0_, bf16[24,64,512]{2,1,0:T(8,128)(2,1)S(1)} %bitcast.6, bf16[24,64,512]{2,1,0:T(8,128)(2,1)S(1)} %collective-permute-done.1.refs_2_.refs_8_.refs_10_), custom_call_target="tpu_custom_call" | custom-call | flops 1000000000 | bytes 6291456 | tf_op jit(solution)/shard_map/flip_keys/pallas_call | solution.py:342
  8.6 0.0 collective-permute-done.2.refs_0_
  8.6 1.4 %collective-permute-done.3.refs_1_ = bf16[6,2,512]{2,1,0:T(2,128)(2,1)S(1)} collective-permute-done((bf16[6,2,512]{2,1,0:T(2,128)(2,1)}, bf16[6,2,512]{2,1,0:T(2,128)(2,1)S(1)}, u32[]{:S(2)}, u32[]{:S(2)}) %collective-permute-start.3) | collective-permute-done | bytes 12320 | tf_op jit(solution)/shard_map/ppermute | solution.py:309
  10.0 0.0 collective-permute-done.4.refs_2_
  10.0 0.0 copy-start
  10.0 0.0 copy-start.2
  10.0 0.0 copy-start.3
  10.0 0.0 copy-start.4
  10.0 0.0 copy-start.7
  10.0 0.7 %prefix_keys.3 = (bf16[24,384]{1,0:T(8,128)(2,1)S(1)}, bf16[24,384]{1,0:T(8,128)(2,1)S(1)}, bf16[24,384]{1,0:T(8,128)(2,1)S(1)}) custom-call(bf16[6,2,512]{2,1,0:T(2,128)(2,1)S(1)} %collective-permute-done.2.refs_0_, bf16[6,2,512]{2,1,0:T(2,128)(2,1)S(1)} %collective-permute-done.3.refs_1_, bf16[6,2,512]{2,1,0:T(2,128)(2,1)S(1)} %collective-permute-done.4.refs_2_, ...), custom_call_target="tpu_custom_call" | custom-call | flops 226492416 | bytes 3145728 | tf_op jit(solution)/shard_map/prefix_keys/pallas_call | solution.py:374
  10.8 1.8 %collective-permute-start.5 = (bf16[24,384]{1,0:T(8,128)(2,1)S(1)}, bf16[24,384]{1,0:T(8,128)(2,1)S(1)}, u32[]{:S(2)}, u32[]{:S(2)}) collective-permute-start(bf16[24,384]{1,0:T(8,128)(2,1)S(1)} %get-tuple-element.19), channel_id=1, source_target_pairs={{0,7},{1,6},{2,5},{3,4},{4,3},{5,2},{6,1},{7,0},{8,15},{9,14},{10,... | collective-permute-start | bytes 55304 | tf_op jit(solution)/shard_map/ppermute | solution.py:309
  12.6 0.0 collective-permute-start.6
  12.6 2.1 %collective-permute-start.7 = (bf16[24,384]{1,0:T(8,128)(2,1)S(1)}, bf16[24,384]{1,0:T(8,128)(2,1)S(1)}, u32[]{:S(2)}, u32[]{:S(2)}) collective-permute-start(bf16[24,384]{1,0:T(8,128)(2,1)S(1)} %get-tuple-element.21), channel_id=1, source_target_pairs={{0,5},{1,4},{2,7},{3,6},{4,1},{5,0},{6,3},{7,2},{8,13},{9,12},{10,... | collective-permute-start | bytes 55304 | tf_op jit(solution)/shard_map/ppermute | solution.py:309
  14.7 0.0 copy-done
  14.7 0.0 copy-done.2
  14.7 0.0 copy-done.3
  14.7 0.0 copy-done.4
  14.7 0.0 copy-done.7
  14.7 1.1 %own_keys.1.refs_0_ = f32[24,384]{1,0:T(8,128)S(1)} custom-call(s32[6]{0:T(128)S(1)} %copy-done.7, bf16[6,2,512]{2,1,0:T(2,128)(2,1)S(1)} %copy-done.3, bf16[6,128,512]{2,1,0:T(8,128)(2,1)S(1)} %bitcast.9, bf16[6,2,512]{2,1,0:T(2,128)(2,1)S(1)} %bitcast.10, bf16[512,2048]{1,0:T(8,128)(2,1)S(1)} %copy-done), custom_call_target="tpu_custom_call" | custom-call | flops 18874368 | bytes 786432 | tf_op jit(solution)/shard_map/own_keys/pallas_call | solution.py:354
  15.8 0.7 %prefix_keys.2.refs_1_ = bf16[24,384]{1,0:T(8,128)(2,1)S(1)} custom-call(bf16[6,2,512]{2,1,0:T(2,128)(2,1)S(1)} %get-tuple-element.12.refs_0_, s32[96,128]{1,0:T(8,128)S(1)} %get-tuple-element.13.refs_1_.refs_3_, s32[96,128]{1,0:T(8,128)S(1)} %get-tuple-element.14.refs_2_.refs_4_, s32[8,1536]{1,0:T(8,128)S(1)} %get-tuple-element.15.refs_3_.refs_5_, ...), custom_call_target="tpu_custom_call" | custom-call | flops 75497472 | bytes 3145728 | tf_op jit(solution)/shard_map/prefix_keys/pallas_call | solution.py:374
  16.5 0.0 copy-start.8
  16.5 0.0 copy-start.5
  16.5 0.0 copy-start.6
  16.5 0.0 collective-permute-done.5.refs_2_
  16.5 0.0 collective-permute-done.6.refs_3_
  16.5 0.2 collective-permute-done.7.refs_4_
  16.7 0.5 %combine_project.1 = bf16[6,2,2048]{2,1,0:T(2,128)(2,1)S(1)} custom-call(f32[24,384]{1,0:T(8,128)S(1)} %own_keys.1.refs_0_, bf16[24,384]{1,0:T(8,128)(2,1)S(1)} %prefix_keys.2.refs_1_, bf16[24,384]{1,0:T(8,128)(2,1)S(1)} %collective-permute-done.5.refs_2_, bf16[24,384]{1,0:T(8,128)(2,1)S(1)} %collective-permute-done.6.refs_3_, ...), custom_call_target="tpu_custom_call" | custom-call | flops 25165824 | bytes 2097152 | tf_op jit(solution)/shard_map/combine_project/pallas_call | solution.py:414
  17.2 2.5 %collective-permute-start.10 = (bf16[6,2,2048]{2,1,0:T(2,128)(2,1)S(1)}, bf16[6,2,2048]{2,1,0:T(2,128)(2,1)S(1)}, u32[]{:S(2)}, u32[]{:S(2)}) collective-permute-start(bf16[6,2,2048]{2,1,0:T(2,128)(2,1)S(1)} %combine_project.1), channel_id=1, source_target_pairs={{0,24},{8,16},{16,8},{24,0},{1,25},{9,17},{17,9},{25,1},{2,26},{10... | collective-permute-start | bytes 147464 | tf_op jit(solution)/shard_map/ppermute | solution.py:309
  19.7 0.5 %collective-permute-start.9 = (bf16[6,2,2048]{2,1,0:T(2,128)(2,1)S(1)}, bf16[6,2,2048]{2,1,0:T(2,128)(2,1)S(1)}, u32[]{:S(2)}, u32[]{:S(2)}) collective-permute-start(bf16[6,2,2048]{2,1,0:T(2,128)(2,1)S(1)} %combine_project.1), channel_id=1, source_target_pairs={{0,8},{8,0},{16,24},{24,16},{1,9},{9,1},{17,25},{25,17},{2,10},{10... | collective-permute-start | bytes 147464 | tf_op jit(solution)/shard_map/ppermute | solution.py:309
  20.2 0.5 %collective-permute-start.8 = (bf16[6,2,2048]{2,1,0:T(2,128)(2,1)S(1)}, bf16[6,2,2048]{2,1,0:T(2,128)(2,1)S(1)}, u32[]{:S(2)}, u32[]{:S(2)}) collective-permute-start(bf16[6,2,2048]{2,1,0:T(2,128)(2,1)S(1)} %combine_project.1), channel_id=1, source_target_pairs={{0,16},{8,24},{16,0},{24,8},{1,17},{9,25},{17,1},{25,9},{2,18},{10... | collective-permute-start | bytes 147464 | tf_op jit(solution)/shard_map/ppermute | solution.py:309
  20.7 1.6 %collective-permute-done.10 = bf16[6,2,2048]{2,1,0:T(2,128)(2,1)S(1)} collective-permute-done((bf16[6,2,2048]{2,1,0:T(2,128)(2,1)S(1)}, bf16[6,2,2048]{2,1,0:T(2,128)(2,1)S(1)}, u32[]{:S(2)}, u32[]{:S(2)}) %collective-permute-start.10) | collective-permute-done | bytes 49184 | tf_op jit(solution)/shard_map/ppermute | solution.py:309
  22.3 1.5 %collective-permute-done.9 = bf16[6,2,2048]{2,1,0:T(2,128)(2,1)S(1)} collective-permute-done((bf16[6,2,2048]{2,1,0:T(2,128)(2,1)S(1)}, bf16[6,2,2048]{2,1,0:T(2,128)(2,1)S(1)}, u32[]{:S(2)}, u32[]{:S(2)}) %collective-permute-start.9) | collective-permute-done | bytes 49184 | tf_op jit(solution)/shard_map/ppermute | solution.py:309
  23.8 0.0 copy-done.8
  23.8 0.1 convert_add_fusion.refs_1_
  23.9 0.4 %collective-permute-done.8.refs_0_ = bf16[6,2,2048]{2,1,0:T(2,128)(2,1)S(1)} collective-permute-done((bf16[6,2,2048]{2,1,0:T(2,128)(2,1)S(1)}, bf16[6,2,2048]{2,1,0:T(2,128)(2,1)S(1)}, u32[]{:S(2)}, u32[]{:S(2)}) %collective-permute-start.8) | collective-permute-done | bytes 49184 | tf_op jit(solution)/shard_map/ppermute | solution.py:309
  24.3 0.0 copy-done.5
  24.3 0.0 copy-done.6
  24.3 0.7 %residual_scores.1 = (bf16[6,2,2048]{2,1,0:T(2,128)(2,1)}, f32[6]{0:T(128)}) custom-call(bf16[6,2,2048]{2,1,0:T(2,128)(2,1)S(1)} %collective-permute-done.8.refs_0_, f32[6,2,2048]{2,1,0:T(2,128)S(1)} %convert_add_fusion.refs_1_, f32[1,2048]{1,0:T(1,128)S(1)} %bitcast.11, f32[1,2048]{1,0:T(1,128)S(1)} %bitcast.12), custom_call_target="tpu_custom_call" | custom-call | flops 1 | bytes 294912 | tf_op jit(solution)/shard_map/residual_scores/pallas_call | solution.py:445
Async XLA Ops:
  0.6 6.9 %copy-start.1 = (bf16[1,24,64,512]{3,2,1,0:T(8,128)(2,1)S(1)}, bf16[1,24,64,512]{3,2,1,0:T(8,128)(2,1)}, u32[]{:S(2)}) copy-start(bf16[1,24,64,512]{3,2,1,0:T(8,128)(2,1)} %param.12) | copy-start | bytes 4718596
  0.6 6.9 %collective-permute-start.1 = (bf16[24,64,512]{2,1,0:T(8,128)(2,1)}, bf16[24,64,512]{2,1,0:T(8,128)(2,1)S(1)}, u32[]{:S(2)}, u32[]{:S(2)}) collective-permute-start(bf16[24,64,512]{2,1,0:T(8,128)(2,1)} %bitcast.5), channel_id=1, source_target_pairs={{0,1},{1,0},{2,3},{3,2},{4,5},{5,4},{6,7},{7,6},{8,9},{9,8},{10,11... | collective-permute-start | bytes 4718600 | tf_op jit(solution)/shard_map/ppermute | solution.py:309
  1.2 7.4 %collective-permute-start.2 = (bf16[6,2,512]{2,1,0:T(2,128)(2,1)}, bf16[6,2,512]{2,1,0:T(2,128)(2,1)S(1)}, u32[]{:S(2)}, u32[]{:S(2)}) collective-permute-start(bf16[6,2,512]{2,1,0:T(2,128)(2,1)} %q_ref.3), channel_id=1, source_target_pairs={{0,5},{1,4},{2,7},{3,6},{4,1},{5,0},{6,3},{7,2},{8,13},{9,12},{10,... | collective-permute-start | bytes 36872 | tf_op jit(solution)/shard_map/ppermute | solution.py:309
  4.9 5.1 %collective-permute-start.3 = (bf16[6,2,512]{2,1,0:T(2,128)(2,1)}, bf16[6,2,512]{2,1,0:T(2,128)(2,1)S(1)}, u32[]{:S(2)}, u32[]{:S(2)}) collective-permute-start(bf16[6,2,512]{2,1,0:T(2,128)(2,1)} %q_ref.3), channel_id=1, source_target_pairs={{0,7},{1,6},{2,5},{3,4},{4,3},{5,2},{6,1},{7,0},{8,15},{9,14},{10,... | collective-permute-start | bytes 36872 | tf_op jit(solution)/shard_map/ppermute | solution.py:309
  5.9 4.1 %collective-permute-start.4 = (bf16[6,2,512]{2,1,0:T(2,128)(2,1)}, bf16[6,2,512]{2,1,0:T(2,128)(2,1)S(1)}, u32[]{:S(2)}, u32[]{:S(2)}) collective-permute-start(bf16[6,2,512]{2,1,0:T(2,128)(2,1)} %q_ref.3), channel_id=1, source_target_pairs={{0,3},{1,2},{2,1},{3,0},{4,7},{5,6},{6,5},{7,4},{8,11},{9,10},{10,... | collective-permute-start | bytes 36872 | tf_op jit(solution)/shard_map/ppermute | solution.py:309
  6.1 1.4 %collective-permute-start = (s32[24]{0:T(128)}, s32[24]{0:T(128)S(1)}, u32[]{:S(2)}, u32[]{:S(2)}) collective-permute-start(s32[24]{0:T(128)} %page_hbm.1), channel_id=1, source_target_pairs={{0,1},{1,0},{2,3},{3,2},{4,5},{5,4},{6,7},{7,6},{8,9},{9,8},{10,11... | collective-permute-start | bytes 296 | tf_op jit(solution)/shard_map/ppermute | solution.py:309
  10.0 4.7 %copy-start = (bf16[512,2048]{1,0:T(8,128)(2,1)S(1)}, bf16[512,2048]{1,0:T(8,128)(2,1)}, u32[]{:S(2)}) copy-start(bf16[512,2048]{1,0:T(8,128)(2,1)} %refs_5_.1) | copy-start | bytes 6291460
  10.0 4.7 %copy-start.2 = (bf16[1,6,128,512]{3,2,1,0:T(8,128)(2,1)S(1)}, bf16[1,6,128,512]{3,2,1,0:T(8,128)(2,1)}, u32[]{:S(2)}) copy-start(bf16[1,6,128,512]{3,2,1,0:T(8,128)(2,1)} %param.17) | copy-start | bytes 2359300
  10.0 4.7 %copy-start.3 = (bf16[6,2,512]{2,1,0:T(2,128)(2,1)S(1)}, bf16[6,2,512]{2,1,0:T(2,128)(2,1)}, u32[]{:S(2)}) copy-start(bf16[6,2,512]{2,1,0:T(2,128)(2,1)} %q_ref.3) | copy-start | bytes 36868
  10.0 4.7 %copy-start.4 = (bf16[1,6,2,512]{3,2,1,0:T(2,128)(2,1)S(1)}, bf16[1,6,2,512]{3,2,1,0:T(2,128)(2,1)}, u32[]{:S(2)}) copy-start(bf16[1,6,2,512]{3,2,1,0:T(2,128)(2,1)} %param.19) | copy-start | bytes 36868
  10.0 4.7 %copy-start.7 = (s32[6]{0:T(128)S(1)}, s32[6]{0:T(128)}, u32[]{:S(2)}) copy-start(s32[6]{0:T(128)} %len_ref.1) | copy-start | bytes 76
  10.8 5.7 %collective-permute-start.5 = (bf16[24,384]{1,0:T(8,128)(2,1)S(1)}, bf16[24,384]{1,0:T(8,128)(2,1)S(1)}, u32[]{:S(2)}, u32[]{:S(2)}) collective-permute-start(bf16[24,384]{1,0:T(8,128)(2,1)S(1)} %get-tuple-element.19), channel_id=1, source_target_pairs={{0,7},{1,6},{2,5},{3,4},{4,3},{5,2},{6,1},{7,0},{8,15},{9,14},{10,... | collective-permute-start | bytes 55304 | tf_op jit(solution)/shard_map/ppermute | solution.py:309
  12.6 3.9 %collective-permute-start.6 = (bf16[24,384]{1,0:T(8,128)(2,1)S(1)}, bf16[24,384]{1,0:T(8,128)(2,1)S(1)}, u32[]{:S(2)}, u32[]{:S(2)}) collective-permute-start(bf16[24,384]{1,0:T(8,128)(2,1)S(1)} %get-tuple-element.20), channel_id=1, source_target_pairs={{0,3},{1,2},{2,1},{3,0},{4,7},{5,6},{6,5},{7,4},{8,11},{9,10},{10,... | collective-permute-start | bytes 55304 | tf_op jit(solution)/shard_map/ppermute | solution.py:309
  12.6 4.1 %collective-permute-start.7 = (bf16[24,384]{1,0:T(8,128)(2,1)S(1)}, bf16[24,384]{1,0:T(8,128)(2,1)S(1)}, u32[]{:S(2)}, u32[]{:S(2)}) collective-permute-start(bf16[24,384]{1,0:T(8,128)(2,1)S(1)} %get-tuple-element.21), channel_id=1, source_target_pairs={{0,5},{1,4},{2,7},{3,6},{4,1},{5,0},{6,3},{7,2},{8,13},{9,12},{10,... | collective-permute-start | bytes 55304 | tf_op jit(solution)/shard_map/ppermute | solution.py:309
  16.5 7.3 %copy-start.8 = (bf16[6,2,2048]{2,1,0:T(2,128)(2,1)S(1)}, bf16[6,2,2048]{2,1,0:T(2,128)(2,1)}, u32[]{:S(2)}) copy-start(bf16[6,2,2048]{2,1,0:T(2,128)(2,1)} %param.20) | copy-start | bytes 147460
  16.5 7.9 %copy-start.5 = (f32[2048]{0:T(1024)S(1)}, f32[2048]{0:T(1024)}, u32[]{:S(2)}) copy-start(f32[2048]{0:T(1024)} %param.22) | copy-start | bytes 24580
  16.5 7.8 %copy-start.6 = (f32[2048]{0:T(1024)S(1)}, f32[2048]{0:T(1024)}, u32[]{:S(2)}) copy-start(f32[2048]{0:T(1024)} %param.23) | copy-start | bytes 24580
  17.2 5.1 %collective-permute-start.10 = (bf16[6,2,2048]{2,1,0:T(2,128)(2,1)S(1)}, bf16[6,2,2048]{2,1,0:T(2,128)(2,1)S(1)}, u32[]{:S(2)}, u32[]{:S(2)}) collective-permute-start(bf16[6,2,2048]{2,1,0:T(2,128)(2,1)S(1)} %combine_project.1), channel_id=1, source_target_pairs={{0,24},{8,16},{16,8},{24,0},{1,25},{9,17},{17,9},{25,1},{2,26},{10... | collective-permute-start | bytes 147464 | tf_op jit(solution)/shard_map/ppermute | solution.py:309
  19.7 4.1 %collective-permute-start.9 = (bf16[6,2,2048]{2,1,0:T(2,128)(2,1)S(1)}, bf16[6,2,2048]{2,1,0:T(2,128)(2,1)S(1)}, u32[]{:S(2)}, u32[]{:S(2)}) collective-permute-start(bf16[6,2,2048]{2,1,0:T(2,128)(2,1)S(1)} %combine_project.1), channel_id=1, source_target_pairs={{0,8},{8,0},{16,24},{24,16},{1,9},{9,1},{17,25},{25,17},{2,10},{10... | collective-permute-start | bytes 147464 | tf_op jit(solution)/shard_map/ppermute | solution.py:309
  20.2 4.1 %collective-permute-start.8 = (bf16[6,2,2048]{2,1,0:T(2,128)(2,1)S(1)}, bf16[6,2,2048]{2,1,0:T(2,128)(2,1)S(1)}, u32[]{:S(2)}, u32[]{:S(2)}) collective-permute-start(bf16[6,2,2048]{2,1,0:T(2,128)(2,1)S(1)} %combine_project.1), channel_id=1, source_target_pairs={{0,16},{8,24},{16,0},{24,8},{1,17},{9,25},{17,1},{25,9},{2,18},{10... | collective-permute-start | bytes 147464 | tf_op jit(solution)/shard_map/ppermute | solution.py:309

commit v10 on v8

--- a/solution.py
+++ b/solution.py
@@ -139,6 +139,7 @@
         spread_rows(q_rows, j * heads * rows, block, heads, head_size, rows)
     ranges = pl.ds(first_slot * heads * rows, slots * heads * rows)
     low, high = low_ref[ranges, :], high_ref[ranges, :]
+    span = (high - low).astype(jnp.uint32)
     queries = q_rows[...]
     chunk = CHUNK if pages % CHUNK == 0 else pages
     masked = []
@@ -149,7 +150,7 @@
             parts = []
             for k in range(0, chunk * page_tokens, LANES):
                 key = key_ref[0:1, at + k:at + k + LANES]
-                live = (key >= low) & (key < high)
+                live = (key - low).astype(jnp.uint32) < span
                 parts.append(jnp.where(live, logits[:, k:k + LANES] * scale, FLOOR))
             masked.append((pool_ref, first, jnp.concatenate(parts, axis=1)))
     num = den = peak = None

time: 25.3 us -> 25.2 us (level)
  no operation moved by 1% of the time
where the time goes in v10:
time: 25.2 us; the launch traced here: 25.1 us
  starting transfers between devices  13.4 us (53%)
  Pallas kernels  5.65 us (22%)
  waiting for transfers between devices  5.27 us (21%)
  between operations  0.75 us (3%)
    ppermute x11, starting transfers between devices, swap(): return lax.ppermute(x, axis, [(i, i ^ mask) for i in range(size)])  13.4 us
    ppermute x11, waiting for transfers between devices, swap(): return lax.ppermute(x, axis, [(i, i ^ mask) for i in range(size)])  5.27 us
    pallas_call x2, Pallas kernels, prefix_column(): pl.pallas_call(functools.partial(prefix_kernel, heads, rows, scale, count...  1.39 us
    pallas_call x1, Pallas kernels, body(): pl.pallas_call(functools.partial(own_kernel, heads, rows, scale), out_sha...  1.07 us
    pallas_call x1, Pallas kernels, body(): pl.pallas_call(functools.partial(flip_kernel, page_tokens), out_shape=(ja...  1.03 us
    pallas_call x1, Pallas kernels, body(): pl.pallas_call(functools.partial(layout_kernel, device_of, slots, local,...  0.86 us
    pallas_call x1, Pallas kernels, body(): pl.pallas_call(final_kernel, out_shape=(jax.ShapeDtypeStruct(hidden.shape...  0.77 us
    pallas_call x1, Pallas kernels, body(): pl.pallas_call(functools.partial(combine_kernel, heads, rows, head_size),...  0.52 us
  transfers between devices with their start and end apart: 11, of which 6 were waited for; matrix products, arithmetic and copies ran while one was open for 0% of the time, Pallas kernels for 15%

profile of v10, /device:TPU:0, one launch (start us, length us, event | category | flops | bytes accessed | tf_op | source)
XLA Modules:
  0.0 25.1 jit_solution(5570588862402981805)
XLA Ops:
  0.6 0.0 copy-start.1
  0.6 0.5 %collective-permute-start.1 = (bf16[24,64,512]{2,1,0:T(8,128)(2,1)}, bf16[24,64,512]{2,1,0:T(8,128)(2,1)S(1)}, u32[]{:S(2)}, u32[]{:S(2)}) collective-permute-start(bf16[24,64,512]{2,1,0:T(8,128)(2,1)} %bitcast.5), channel_id=1, source_target_pairs={{0,1},{1,0},{2,3},{3,2},{4,5},{5,4},{6,7},{7,6},{8,9},{9,8},{10,11... | collective-permute-start | bytes 4718600 | tf_op jit(solution)/shard_map/ppermute | solution.py:310
  1.2 3.7 %collective-permute-start.2 = (bf16[6,2,512]{2,1,0:T(2,128)(2,1)}, bf16[6,2,512]{2,1,0:T(2,128)(2,1)S(1)}, u32[]{:S(2)}, u32[]{:S(2)}) collective-permute-start(bf16[6,2,512]{2,1,0:T(2,128)(2,1)} %q_ref.3), channel_id=1, source_target_pairs={{0,5},{1,4},{2,7},{3,6},{4,1},{5,0},{6,3},{7,2},{8,13},{9,12},{10,... | collective-permute-start | bytes 36872 | tf_op jit(solution)/shard_map/ppermute | solution.py:310
  4.9 1.0 %collective-permute-start.3 = (bf16[6,2,512]{2,1,0:T(2,128)(2,1)}, bf16[6,2,512]{2,1,0:T(2,128)(2,1)S(1)}, u32[]{:S(2)}, u32[]{:S(2)}) collective-permute-start(bf16[6,2,512]{2,1,0:T(2,128)(2,1)} %q_ref.3), channel_id=1, source_target_pairs={{0,7},{1,6},{2,5},{3,4},{4,3},{5,2},{6,1},{7,0},{8,15},{9,14},{10,... | collective-permute-start | bytes 36872 | tf_op jit(solution)/shard_map/ppermute | solution.py:310
  5.9 0.2 collective-permute-start.4
  6.1 0.4 %collective-permute-start = (s32[24]{0:T(128)}, s32[24]{0:T(128)S(1)}, u32[]{:S(2)}, u32[]{:S(2)}) collective-permute-start(s32[24]{0:T(128)} %page_hbm.1), channel_id=1, source_target_pairs={{0,1},{1,0},{2,3},{3,2},{4,5},{5,4},{6,7},{7,6},{8,9},{9,8},{10,11... | collective-permute-start | bytes 296 | tf_op jit(solution)/shard_map/ppermute | solution.py:310
  6.6 0.9 %key_ranges.1 = (s32[96,128]{1,0:T(8,128)S(1)}, s32[96,128]{1,0:T(8,128)S(1)}, s32[8,1536]{1,0:T(8,128)S(1)}, bf16[6,2,512]{2,1,0:T(2,128)(2,1)S(1)}) custom-call(s32[48]{0:T(128)} %ids_hbm.1, s32[3]{0:T(128)} %len_hbm.1, s32[24]{0:T(128)} %page_hbm.1, bf16[6,2,512]{2,1,0:T(2,128)(2,1)} %q_ref.3), custom_call_target="tpu_custom_call" | custom-call | flops 4000000000 | bytes 98304 | tf_op jit(solution)/shard_map/key_ranges/pallas_call | solution.py:322
  7.4 0.1 collective-permute-done.refs_0_
  7.5 0.0 collective-permute-done.1.refs_2_.refs_8_.refs_10_
  7.5 0.0 copy-done.1
  7.5 1.0 %flip_keys.1 = (s32[8,1536]{1,0:T(8,128)S(1)}, bf16[256,1536]{1,0:T(8,128)(2,1)S(1)}, bf16[256,1536]{1,0:T(8,128)(2,1)S(1)}) custom-call(s32[24]{0:T(128)S(1)} %collective-permute-done.refs_0_, bf16[24,64,512]{2,1,0:T(8,128)(2,1)S(1)} %bitcast.6, bf16[24,64,512]{2,1,0:T(8,128)(2,1)S(1)} %collective-permute-done.1.refs_2_.refs_8_.refs_10_), custom_call_target="tpu_custom_call" | custom-call | flops 1000000000 | bytes 6291456 | tf_op jit(solution)/shard_map/flip_keys/pallas_call | solution.py:343
  8.6 0.0 collective-permute-done.2.refs_0_
  8.6 1.4 %collective-permute-done.3.refs_1_ = bf16[6,2,512]{2,1,0:T(2,128)(2,1)S(1)} collective-permute-done((bf16[6,2,512]{2,1,0:T(2,128)(2,1)}, bf16[6,2,512]{2,1,0:T(2,128)(2,1)S(1)}, u32[]{:S(2)}, u32[]{:S(2)}) %collective-permute-start.3) | collective-permute-done | bytes 12320 | tf_op jit(solution)/shard_map/ppermute | solution.py:310
  10.0 0.0 collective-permute-done.4.refs_2_
  10.0 0.0 copy-start
  10.0 0.0 copy-start.2
  10.0 0.0 copy-start.4
  10.0 0.0 copy-start.5
  10.0 0.0 copy-start.8
  10.0 0.7 %prefix_keys.3 = (bf16[24,384]{1,0:T(8,128)(2,1)S(1)}, bf16[24,384]{1,0:T(8,128)(2,1)S(1)}, bf16[24,384]{1,0:T(8,128)(2,1)S(1)}) custom-call(bf16[6,2,512]{2,1,0:T(2,128)(2,1)S(1)} %collective-permute-done.2.refs_0_, bf16[6,2,512]{2,1,0:T(2,128)(2,1)S(1)} %collective-permute-done.3.refs_1_, bf16[6,2,512]{2,1,0:T(2,128)(2,1)S(1)} %collective-permute-done.4.refs_2_, ...), custom_call_target="tpu_custom_call" | custom-call | flops 226492416 | bytes 3145728 | tf_op jit(solution)/shard_map/prefix_keys/pallas_call | solution.py:375
  10.8 1.8 %collective-permute-start.5 = (bf16[24,384]{1,0:T(8,128)(2,1)S(1)}, bf16[24,384]{1,0:T(8,128)(2,1)S(1)}, u32[]{:S(2)}, u32[]{:S(2)}) collective-permute-start(bf16[24,384]{1,0:T(8,128)(2,1)S(1)} %get-tuple-element.19), channel_id=1, source_target_pairs={{0,7},{1,6},{2,5},{3,4},{4,3},{5,2},{6,1},{7,0},{8,15},{9,14},{10,... | collective-permute-start | bytes 55304 | tf_op jit(solution)/shard_map/ppermute | solution.py:310
  12.6 0.0 collective-permute-start.6
  12.6 2.1 %collective-permute-start.7 = (bf16[24,384]{1,0:T(8,128)(2,1)S(1)}, bf16[24,384]{1,0:T(8,128)(2,1)S(1)}, u32[]{:S(2)}, u32[]{:S(2)}) collective-permute-start(bf16[24,384]{1,0:T(8,128)(2,1)S(1)} %get-tuple-element.21), channel_id=1, source_target_pairs={{0,5},{1,4},{2,7},{3,6},{4,1},{5,0},{6,3},{7,2},{8,13},{9,12},{10,... | collective-permute-start | bytes 55304 | tf_op jit(solution)/shard_map/ppermute | solution.py:310
  14.7 0.0 copy-done
  14.7 0.0 copy-done.2
  14.7 0.0 copy-done.4
  14.7 0.0 copy-done.5
  14.7 0.0 copy-done.8
  14.7 1.1 %own_keys.1.refs_0_ = f32[24,384]{1,0:T(8,128)S(1)} custom-call(s32[6]{0:T(128)S(1)} %copy-done.8, bf16[6,2,512]{2,1,0:T(2,128)(2,1)S(1)} %copy-done.4, bf16[6,128,512]{2,1,0:T(8,128)(2,1)S(1)} %bitcast.9, bf16[6,2,512]{2,1,0:T(2,128)(2,1)S(1)} %bitcast.10, bf16[512,2048]{1,0:T(8,128)(2,1)S(1)} %copy-done), custom_call_target="tpu_custom_call" | custom-call | flops 18874368 | bytes 786432 | tf_op jit(solution)/shard_map/own_keys/pallas_call | solution.py:355
  15.8 0.7 %prefix_keys.2.refs_1_ = bf16[24,384]{1,0:T(8,128)(2,1)S(1)} custom-call(bf16[6,2,512]{2,1,0:T(2,128)(2,1)S(1)} %get-tuple-element.12.refs_0_, s32[96,128]{1,0:T(8,128)S(1)} %get-tuple-element.13.refs_1_.refs_3_, s32[96,128]{1,0:T(8,128)S(1)} %get-tuple-element.14.refs_2_.refs_4_, s32[8,1536]{1,0:T(8,128)S(1)} %get-tuple-element.15.refs_3_.refs_5_, ...), custom_call_target="tpu_custom_call" | custom-call | flops 75497472 | bytes 3145728 | tf_op jit(solution)/shard_map/prefix_keys/pallas_call | solution.py:375
  16.4 0.0 copy-start.3
  16.4 0.0 copy-start.6
  16.4 0.0 copy-start.7
  16.5 0.0 collective-permute-done.5.refs_2_
  16.5 0.0 collective-permute-done.6.refs_3_
  16.5 0.2 collective-permute-done.7.refs_4_
  16.6 0.5 %combine_project.1.refs_0_ = bf16[6,2,2048]{2,1,0:T(2,128)(2,1)S(1)} custom-call(f32[24,384]{1,0:T(8,128)S(1)} %own_keys.1.refs_0_, bf16[24,384]{1,0:T(8,128)(2,1)S(1)} %prefix_keys.2.refs_1_, bf16[24,384]{1,0:T(8,128)(2,1)S(1)} %collective-permute-done.5.refs_2_, bf16[24,384]{1,0:T(8,128)(2,1)S(1)} %collective-permute-done.6.refs_3_, ...), custom_call_target="tpu_custom_call" | custom-call | flops 25165824 | bytes 2097152 | tf_op jit(solution)/shard_map/combine_project/pallas_call | solution.py:415
  17.2 2.5 %collective-permute-start.10 = (bf16[6,2,2048]{2,1,0:T(2,128)(2,1)S(1)}, bf16[6,2,2048]{2,1,0:T(2,128)(2,1)S(1)}, u32[]{:S(2)}, u32[]{:S(2)}) collective-permute-start(bf16[6,2,2048]{2,1,0:T(2,128)(2,1)S(1)} %combine_project.1.refs_0_), channel_id=1, source_target_pairs={{0,24},{8,16},{16,8},{24,0},{1,25},{9,17},{17,9},{25,1},{2,26},{10... | collective-permute-start | bytes 147464 | tf_op jit(solution)/shard_map/ppermute | solution.py:310
  19.7 0.5 %collective-permute-start.8 = (bf16[6,2,2048]{2,1,0:T(2,128)(2,1)S(1)}, bf16[6,2,2048]{2,1,0:T(2,128)(2,1)S(1)}, u32[]{:S(2)}, u32[]{:S(2)}) collective-permute-start(bf16[6,2,2048]{2,1,0:T(2,128)(2,1)S(1)} %combine_project.1.refs_0_), channel_id=1, source_target_pairs={{0,8},{8,0},{16,24},{24,16},{1,9},{9,1},{17,25},{25,17},{2,10},{10... | collective-permute-start | bytes 147464 | tf_op jit(solution)/shard_map/ppermute | solution.py:310
  20.2 0.5 %collective-permute-start.9 = (bf16[6,2,2048]{2,1,0:T(2,128)(2,1)S(1)}, bf16[6,2,2048]{2,1,0:T(2,128)(2,1)S(1)}, u32[]{:S(2)}, u32[]{:S(2)}) collective-permute-start(bf16[6,2,2048]{2,1,0:T(2,128)(2,1)S(1)} %combine_project.1.refs_0_), channel_id=1, source_target_pairs={{0,16},{8,24},{16,0},{24,8},{1,17},{9,25},{17,1},{25,9},{2,18},{10... | collective-permute-start | bytes 147464 | tf_op jit(solution)/shard_map/ppermute | solution.py:310
  20.7 1.6 %collective-permute-done.10.refs_3_ = bf16[6,2,2048]{2,1,0:T(2,128)(2,1)S(1)} collective-permute-done((bf16[6,2,2048]{2,1,0:T(2,128)(2,1)S(1)}, bf16[6,2,2048]{2,1,0:T(2,128)(2,1)S(1)}, u32[]{:S(2)}, u32[]{:S(2)}) %collective-permute-start.10) | collective-permute-done | bytes 49184 | tf_op jit(solution)/shard_map/ppermute | solution.py:310
  22.3 1.5 %collective-permute-done.8.refs_1_ = bf16[6,2,2048]{2,1,0:T(2,128)(2,1)S(1)} collective-permute-done((bf16[6,2,2048]{2,1,0:T(2,128)(2,1)S(1)}, bf16[6,2,2048]{2,1,0:T(2,128)(2,1)S(1)}, u32[]{:S(2)}, u32[]{:S(2)}) %collective-permute-start.8) | collective-permute-done | bytes 49184 | tf_op jit(solution)/shard_map/ppermute | solution.py:310
  23.8 0.5 %collective-permute-done.9.refs_2_ = bf16[6,2,2048]{2,1,0:T(2,128)(2,1)S(1)} collective-permute-done((bf16[6,2,2048]{2,1,0:T(2,128)(2,1)S(1)}, bf16[6,2,2048]{2,1,0:T(2,128)(2,1)S(1)}, u32[]{:S(2)}, u32[]{:S(2)}) %collective-permute-start.9) | collective-permute-done | bytes 49184 | tf_op jit(solution)/shard_map/ppermute | solution.py:310
  24.3 0.0 copy-done.3
  24.3 0.0 copy-done.6
  24.3 0.0 copy-done.7
  24.3 0.8 %residual_scores.1 = (bf16[6,2,2048]{2,1,0:T(2,128)(2,1)}, f32[6]{0:T(128)}) custom-call(bf16[6,2,2048]{2,1,0:T(2,128)(2,1)S(1)} %combine_project.1.refs_0_, bf16[6,2,2048]{2,1,0:T(2,128)(2,1)S(1)} %collective-permute-done.8.refs_1_, bf16[6,2,2048]{2,1,0:T(2,128)(2,1)S(1)} %collective-permute-done.9.refs_2_, ...), custom_call_target="tpu_custom_call" | custom-call | flops 1 | bytes 294912 | tf_op jit(solution)/shard_map/residual_scores/pallas_call | solution.py:440
Async XLA Ops:
  0.6 6.9 %copy-start.1 = (bf16[1,24,64,512]{3,2,1,0:T(8,128)(2,1)S(1)}, bf16[1,24,64,512]{3,2,1,0:T(8,128)(2,1)}, u32[]{:S(2)}) copy-start(bf16[1,24,64,512]{3,2,1,0:T(8,128)(2,1)} %param.12) | copy-start | bytes 4718596
  0.6 6.9 %collective-permute-start.1 = (bf16[24,64,512]{2,1,0:T(8,128)(2,1)}, bf16[24,64,512]{2,1,0:T(8,128)(2,1)S(1)}, u32[]{:S(2)}, u32[]{:S(2)}) collective-permute-start(bf16[24,64,512]{2,1,0:T(8,128)(2,1)} %bitcast.5), channel_id=1, source_target_pairs={{0,1},{1,0},{2,3},{3,2},{4,5},{5,4},{6,7},{7,6},{8,9},{9,8},{10,11... | collective-permute-start | bytes 4718600 | tf_op jit(solution)/shard_map/ppermute | solution.py:310
  1.2 7.4 %collective-permute-start.2 = (bf16[6,2,512]{2,1,0:T(2,128)(2,1)}, bf16[6,2,512]{2,1,0:T(2,128)(2,1)S(1)}, u32[]{:S(2)}, u32[]{:S(2)}) collective-permute-start(bf16[6,2,512]{2,1,0:T(2,128)(2,1)} %q_ref.3), channel_id=1, source_target_pairs={{0,5},{1,4},{2,7},{3,6},{4,1},{5,0},{6,3},{7,2},{8,13},{9,12},{10,... | collective-permute-start | bytes 36872 | tf_op jit(solution)/shard_map/ppermute | solution.py:310
  4.9 5.1 %collective-permute-start.3 = (bf16[6,2,512]{2,1,0:T(2,128)(2,1)}, bf16[6,2,512]{2,1,0:T(2,128)(2,1)S(1)}, u32[]{:S(2)}, u32[]{:S(2)}) collective-permute-start(bf16[6,2,512]{2,1,0:T(2,128)(2,1)} %q_ref.3), channel_id=1, source_target_pairs={{0,7},{1,6},{2,5},{3,4},{4,3},{5,2},{6,1},{7,0},{8,15},{9,14},{10,... | collective-permute-start | bytes 36872 | tf_op jit(solution)/shard_map/ppermute | solution.py:310
  5.9 4.1 %collective-permute-start.4 = (bf16[6,2,512]{2,1,0:T(2,128)(2,1)}, bf16[6,2,512]{2,1,0:T(2,128)(2,1)S(1)}, u32[]{:S(2)}, u32[]{:S(2)}) collective-permute-start(bf16[6,2,512]{2,1,0:T(2,128)(2,1)} %q_ref.3), channel_id=1, source_target_pairs={{0,3},{1,2},{2,1},{3,0},{4,7},{5,6},{6,5},{7,4},{8,11},{9,10},{10,... | collective-permute-start | bytes 36872 | tf_op jit(solution)/shard_map/ppermute | solution.py:310
  6.1 1.4 %collective-permute-start = (s32[24]{0:T(128)}, s32[24]{0:T(128)S(1)}, u32[]{:S(2)}, u32[]{:S(2)}) collective-permute-start(s32[24]{0:T(128)} %page_hbm.1), channel_id=1, source_target_pairs={{0,1},{1,0},{2,3},{3,2},{4,5},{5,4},{6,7},{7,6},{8,9},{9,8},{10,11... | collective-permute-start | bytes 296 | tf_op jit(solution)/shard_map/ppermute | solution.py:310
  10.0 4.7 %copy-start = (bf16[512,2048]{1,0:T(8,128)(2,1)S(1)}, bf16[512,2048]{1,0:T(8,128)(2,1)}, u32[]{:S(2)}) copy-start(bf16[512,2048]{1,0:T(8,128)(2,1)} %refs_5_.1) | copy-start | bytes 6291460
  10.0 4.7 %copy-start.2 = (bf16[1,6,128,512]{3,2,1,0:T(8,128)(2,1)S(1)}, bf16[1,6,128,512]{3,2,1,0:T(8,128)(2,1)}, u32[]{:S(2)}) copy-start(bf16[1,6,128,512]{3,2,1,0:T(8,128)(2,1)} %param.17) | copy-start | bytes 2359300
  10.0 4.7 %copy-start.4 = (bf16[6,2,512]{2,1,0:T(2,128)(2,1)S(1)}, bf16[6,2,512]{2,1,0:T(2,128)(2,1)}, u32[]{:S(2)}) copy-start(bf16[6,2,512]{2,1,0:T(2,128)(2,1)} %q_ref.3) | copy-start | bytes 36868
  10.0 4.6 %copy-start.5 = (bf16[1,6,2,512]{3,2,1,0:T(2,128)(2,1)S(1)}, bf16[1,6,2,512]{3,2,1,0:T(2,128)(2,1)}, u32[]{:S(2)}) copy-start(bf16[1,6,2,512]{3,2,1,0:T(2,128)(2,1)} %param.19) | copy-start | bytes 36868
  10.0 4.6 %copy-start.8 = (s32[6]{0:T(128)S(1)}, s32[6]{0:T(128)}, u32[]{:S(2)}) copy-start(s32[6]{0:T(128)} %len_ref.1) | copy-start | bytes 76
  10.8 5.7 %collective-permute-start.5 = (bf16[24,384]{1,0:T(8,128)(2,1)S(1)}, bf16[24,384]{1,0:T(8,128)(2,1)S(1)}, u32[]{:S(2)}, u32[]{:S(2)}) collective-permute-start(bf16[24,384]{1,0:T(8,128)(2,1)S(1)} %get-tuple-element.19), channel_id=1, source_target_pairs={{0,7},{1,6},{2,5},{3,4},{4,3},{5,2},{6,1},{7,0},{8,15},{9,14},{10,... | collective-permute-start | bytes 55304 | tf_op jit(solution)/shard_map/ppermute | solution.py:310
  12.6 3.9 %collective-permute-start.6 = (bf16[24,384]{1,0:T(8,128)(2,1)S(1)}, bf16[24,384]{1,0:T(8,128)(2,1)S(1)}, u32[]{:S(2)}, u32[]{:S(2)}) collective-permute-start(bf16[24,384]{1,0:T(8,128)(2,1)S(1)} %get-tuple-element.20), channel_id=1, source_target_pairs={{0,3},{1,2},{2,1},{3,0},{4,7},{5,6},{6,5},{7,4},{8,11},{9,10},{10,... | collective-permute-start | bytes 55304 | tf_op jit(solution)/shard_map/ppermute | solution.py:310
  12.6 4.1 %collective-permute-start.7 = (bf16[24,384]{1,0:T(8,128)(2,1)S(1)}, bf16[24,384]{1,0:T(8,128)(2,1)S(1)}, u32[]{:S(2)}, u32[]{:S(2)}) collective-permute-start(bf16[24,384]{1,0:T(8,128)(2,1)S(1)} %get-tuple-element.21), channel_id=1, source_target_pairs={{0,5},{1,4},{2,7},{3,6},{4,1},{5,0},{6,3},{7,2},{8,13},{9,12},{10,... | collective-permute-start | bytes 55304 | tf_op jit(solution)/shard_map/ppermute | solution.py:310
  16.4 7.9 %copy-start.3 = (bf16[6,2,2048]{2,1,0:T(2,128)(2,1)S(1)}, bf16[6,2,2048]{2,1,0:T(2,128)(2,1)}, u32[]{:S(2)}) copy-start(bf16[6,2,2048]{2,1,0:T(2,128)(2,1)} %refs_4_.1) | copy-start | bytes 147460
  16.4 7.9 %copy-start.6 = (f32[2048]{0:T(1024)S(1)}, f32[2048]{0:T(1024)}, u32[]{:S(2)}) copy-start(f32[2048]{0:T(1024)} %param.22) | copy-start | bytes 24580
  16.4 7.8 %copy-start.7 = (f32[2048]{0:T(1024)S(1)}, f32[2048]{0:T(1024)}, u32[]{:S(2)}) copy-start(f32[2048]{0:T(1024)} %param.23) | copy-start | bytes 24580
  17.2 5.1 %collective-permute-start.10 = (bf16[6,2,2048]{2,1,0:T(2,128)(2,1)S(1)}, bf16[6,2,2048]{2,1,0:T(2,128)(2,1)S(1)}, u32[]{:S(2)}, u32[]{:S(2)}) collective-permute-start(bf16[6,2,2048]{2,1,0:T(2,128)(2,1)S(1)} %combine_project.1.refs_0_), channel_id=1, source_target_pairs={{0,24},{8,16},{16,8},{24,0},{1,25},{9,17},{17,9},{25,1},{2,26},{10... | collective-permute-start | bytes 147464 | tf_op jit(solution)/shard_map/ppermute | solution.py:310
  19.7 4.1 %collective-permute-start.8 = (bf16[6,2,2048]{2,1,0:T(2,128)(2,1)S(1)}, bf16[6,2,2048]{2,1,0:T(2,128)(2,1)S(1)}, u32[]{:S(2)}, u32[]{:S(2)}) collective-permute-start(bf16[6,2,2048]{2,1,0:T(2,128)(2,1)S(1)} %combine_project.1.refs_0_), channel_id=1, source_target_pairs={{0,8},{8,0},{16,24},{24,16},{1,9},{9,1},{17,25},{25,17},{2,10},{10... | collective-permute-start | bytes 147464 | tf_op jit(solution)/shard_map/ppermute | solution.py:310
  20.2 4.1 %collective-permute-start.9 = (bf16[6,2,2048]{2,1,0:T(2,128)(2,1)S(1)}, bf16[6,2,2048]{2,1,0:T(2,128)(2,1)S(1)}, u32[]{:S(2)}, u32[]{:S(2)}) collective-permute-start(bf16[6,2,2048]{2,1,0:T(2,128)(2,1)S(1)} %combine_project.1.refs_0_), channel_id=1, source_target_pairs={{0,16},{8,24},{16,0},{24,8},{1,17},{9,25},{17,1},{25,9},{2,18},{10... | collective-permute-start | bytes 147464 | tf_op jit(solution)/shard_map/ppermute | solution.py:310

commit v11 on v9

--- a/solution.py
+++ b/solution.py
@@ -139,6 +139,7 @@
         spread_rows(q_rows, j * heads * rows, block, heads, head_size, rows)
     ranges = pl.ds(first_slot * heads * rows, slots * heads * rows)
     low, high = low_ref[ranges, :], high_ref[ranges, :]
+    span = (high - low).astype(jnp.uint32)
     queries = q_rows[...]
     chunk = CHUNK if pages % CHUNK == 0 else pages
     masked = []
@@ -149,7 +150,7 @@
             parts = []
             for k in range(0, chunk * page_tokens, LANES):
                 key = key_ref[0:1, at + k:at + k + LANES]
-                live = (key >= low) & (key < high)
+                live = (key - low).astype(jnp.uint32) < span
                 parts.append(jnp.where(live, logits[:, k:k + LANES] * scale, FLOOR))
             masked.append((pool_ref, first, jnp.concatenate(parts, axis=1)))
     num = den = peak = None

time: 25.2 us -> 25.2 us (level)
  no operation moved by 1% of the time
where the time goes in v11:
time: 25.2 us; the launch traced here: 25 us
  starting transfers between devices  13.4 us (53%)
  Pallas kernels  5.62 us (22%)
  waiting for transfers between devices  5.17 us (21%)
  between operations  0.75 us (3%)
    ppermute x11, starting transfers between devices, swap(): return lax.ppermute(x, axis, [(i, i ^ mask) for i in range(size)])  13.4 us
    ppermute x11, waiting for transfers between devices, swap(): return lax.ppermute(x, axis, [(i, i ^ mask) for i in range(size)])  5.17 us
    pallas_call x2, Pallas kernels, prefix_column(): pl.pallas_call(functools.partial(prefix_kernel, heads, rows, scale, count...  1.39 us
    pallas_call x1, Pallas kernels, body(): pl.pallas_call(functools.partial(own_kernel, heads, rows, scale), out_sha...  1.07 us
    pallas_call x1, Pallas kernels, body(): pl.pallas_call(functools.partial(flip_kernel, page_tokens), out_shape=(ja...  1.03 us
    pallas_call x1, Pallas kernels, body(): pl.pallas_call(functools.partial(layout_kernel, device_of, slots, local,...  0.86 us
    pallas_call x1, Pallas kernels, body(): pl.pallas_call(final_kernel, out_shape=(jax.ShapeDtypeStruct(hidden.shape...  0.75 us
    pallas_call x1, Pallas kernels, body(): pl.pallas_call(functools.partial(combine_kernel, heads, rows, head_size),...  0.52 us
  transfers between devices with their start and end apart: 11, of which 6 were waited for; matrix products, arithmetic and copies ran while one was open for 0% of the time, Pallas kernels for 15%

profile of v11, /device:TPU:0, one launch (start us, length us, event | category | flops | bytes accessed | tf_op | source)
XLA Modules:
  0.0 25.0 jit_solution(12650503302462101779)
XLA Ops:
  0.6 0.0 copy-start.1
  0.6 0.5 %collective-permute-start.1 = (bf16[24,64,512]{2,1,0:T(8,128)(2,1)}, bf16[24,64,512]{2,1,0:T(8,128)(2,1)S(1)}, u32[]{:S(2)}, u32[]{:S(2)}) collective-permute-start(bf16[24,64,512]{2,1,0:T(8,128)(2,1)} %bitcast.5), channel_id=1, source_target_pairs={{0,1},{1,0},{2,3},{3,2},{4,5},{5,4},{6,7},{7,6},{8,9},{9,8},{10,11... | collective-permute-start | bytes 4718600 | tf_op jit(solution)/shard_map/ppermute | solution.py:310
  1.2 3.7 %collective-permute-start.2 = (bf16[6,2,512]{2,1,0:T(2,128)(2,1)}, bf16[6,2,512]{2,1,0:T(2,128)(2,1)S(1)}, u32[]{:S(2)}, u32[]{:S(2)}) collective-permute-start(bf16[6,2,512]{2,1,0:T(2,128)(2,1)} %q_ref.3), channel_id=1, source_target_pairs={{0,5},{1,4},{2,7},{3,6},{4,1},{5,0},{6,3},{7,2},{8,13},{9,12},{10,... | collective-permute-start | bytes 36872 | tf_op jit(solution)/shard_map/ppermute | solution.py:310
  4.9 1.0 %collective-permute-start.3 = (bf16[6,2,512]{2,1,0:T(2,128)(2,1)}, bf16[6,2,512]{2,1,0:T(2,128)(2,1)S(1)}, u32[]{:S(2)}, u32[]{:S(2)}) collective-permute-start(bf16[6,2,512]{2,1,0:T(2,128)(2,1)} %q_ref.3), channel_id=1, source_target_pairs={{0,7},{1,6},{2,5},{3,4},{4,3},{5,2},{6,1},{7,0},{8,15},{9,14},{10,... | collective-permute-start | bytes 36872 | tf_op jit(solution)/shard_map/ppermute | solution.py:310
  5.9 0.2 collective-permute-start.4
  6.1 0.4 %collective-permute-start = (s32[24]{0:T(128)}, s32[24]{0:T(128)S(1)}, u32[]{:S(2)}, u32[]{:S(2)}) collective-permute-start(s32[24]{0:T(128)} %page_hbm.1), channel_id=1, source_target_pairs={{0,1},{1,0},{2,3},{3,2},{4,5},{5,4},{6,7},{7,6},{8,9},{9,8},{10,11... | collective-permute-start | bytes 296 | tf_op jit(solution)/shard_map/ppermute | solution.py:310
  6.6 0.9 %key_ranges.1 = (s32[96,128]{1,0:T(8,128)S(1)}, s32[96,128]{1,0:T(8,128)S(1)}, s32[8,1536]{1,0:T(8,128)S(1)}, bf16[6,2,512]{2,1,0:T(2,128)(2,1)S(1)}) custom-call(s32[48]{0:T(128)} %ids_hbm.1, s32[3]{0:T(128)} %len_hbm.1, s32[24]{0:T(128)} %page_hbm.1, bf16[6,2,512]{2,1,0:T(2,128)(2,1)} %q_ref.3), custom_call_target="tpu_custom_call" | custom-call | flops 4000000000 | bytes 98304 | tf_op jit(solution)/shard_map/key_ranges/pallas_call | solution.py:322
  7.4 0.1 collective-permute-done.refs_0_
  7.5 0.0 collective-permute-done.1.refs_2_.refs_8_.refs_10_
  7.5 0.0 copy-done.1
  7.5 1.0 %flip_keys.1 = (s32[8,1536]{1,0:T(8,128)S(1)}, bf16[256,1536]{1,0:T(8,128)(2,1)S(1)}, bf16[256,1536]{1,0:T(8,128)(2,1)S(1)}) custom-call(s32[24]{0:T(128)S(1)} %collective-permute-done.refs_0_, bf16[24,64,512]{2,1,0:T(8,128)(2,1)S(1)} %bitcast.6, bf16[24,64,512]{2,1,0:T(8,128)(2,1)S(1)} %collective-permute-done.1.refs_2_.refs_8_.refs_10_), custom_call_target="tpu_custom_call" | custom-call | flops 1000000000 | bytes 6291456 | tf_op jit(solution)/shard_map/flip_keys/pallas_call | solution.py:343
  8.6 0.0 collective-permute-done.2.refs_0_
  8.6 1.4 %collective-permute-done.3.refs_1_ = bf16[6,2,512]{2,1,0:T(2,128)(2,1)S(1)} collective-permute-done((bf16[6,2,512]{2,1,0:T(2,128)(2,1)}, bf16[6,2,512]{2,1,0:T(2,128)(2,1)S(1)}, u32[]{:S(2)}, u32[]{:S(2)}) %collective-permute-start.3) | collective-permute-done | bytes 12320 | tf_op jit(solution)/shard_map/ppermute | solution.py:310
  10.0 0.0 collective-permute-done.4.refs_2_
  10.0 0.0 copy-start
  10.0 0.0 copy-start.2
  10.0 0.0 copy-start.3
  10.0 0.0 copy-start.4
  10.0 0.0 copy-start.7
  10.0 0.7 %prefix_keys.3 = (bf16[24,384]{1,0:T(8,128)(2,1)S(1)}, bf16[24,384]{1,0:T(8,128)(2,1)S(1)}, bf16[24,384]{1,0:T(8,128)(2,1)S(1)}) custom-call(bf16[6,2,512]{2,1,0:T(2,128)(2,1)S(1)} %collective-permute-done.2.refs_0_, bf16[6,2,512]{2,1,0:T(2,128)(2,1)S(1)} %collective-permute-done.3.refs_1_, bf16[6,2,512]{2,1,0:T(2,128)(2,1)S(1)} %collective-permute-done.4.refs_2_, ...), custom_call_target="tpu_custom_call" | custom-call | flops 226492416 | bytes 3145728 | tf_op jit(solution)/shard_map/prefix_keys/pallas_call | solution.py:375
  10.8 1.8 %collective-permute-start.5 = (bf16[24,384]{1,0:T(8,128)(2,1)S(1)}, bf16[24,384]{1,0:T(8,128)(2,1)S(1)}, u32[]{:S(2)}, u32[]{:S(2)}) collective-permute-start(bf16[24,384]{1,0:T(8,128)(2,1)S(1)} %get-tuple-element.19), channel_id=1, source_target_pairs={{0,7},{1,6},{2,5},{3,4},{4,3},{5,2},{6,1},{7,0},{8,15},{9,14},{10,... | collective-permute-start | bytes 55304 | tf_op jit(solution)/shard_map/ppermute | solution.py:310
  12.6 0.0 collective-permute-start.6
  12.6 2.1 %collective-permute-start.7 = (bf16[24,384]{1,0:T(8,128)(2,1)S(1)}, bf16[24,384]{1,0:T(8,128)(2,1)S(1)}, u32[]{:S(2)}, u32[]{:S(2)}) collective-permute-start(bf16[24,384]{1,0:T(8,128)(2,1)S(1)} %get-tuple-element.21), channel_id=1, source_target_pairs={{0,5},{1,4},{2,7},{3,6},{4,1},{5,0},{6,3},{7,2},{8,13},{9,12},{10,... | collective-permute-start | bytes 55304 | tf_op jit(solution)/shard_map/ppermute | solution.py:310
  14.7 0.0 copy-done
  14.7 0.0 copy-done.2
  14.7 0.0 copy-done.3
  14.7 0.0 copy-done.4
  14.7 0.0 copy-done.7
  14.7 1.1 %own_keys.1.refs_0_ = f32[24,384]{1,0:T(8,128)S(1)} custom-call(s32[6]{0:T(128)S(1)} %copy-done.7, bf16[6,2,512]{2,1,0:T(2,128)(2,1)S(1)} %copy-done.3, bf16[6,128,512]{2,1,0:T(8,128)(2,1)S(1)} %bitcast.9, bf16[6,2,512]{2,1,0:T(2,128)(2,1)S(1)} %bitcast.10, bf16[512,2048]{1,0:T(8,128)(2,1)S(1)} %copy-done), custom_call_target="tpu_custom_call" | custom-call | flops 18874368 | bytes 786432 | tf_op jit(solution)/shard_map/own_keys/pallas_call | solution.py:355
  15.8 0.7 %prefix_keys.2.refs_1_ = bf16[24,384]{1,0:T(8,128)(2,1)S(1)} custom-call(bf16[6,2,512]{2,1,0:T(2,128)(2,1)S(1)} %get-tuple-element.12.refs_0_, s32[96,128]{1,0:T(8,128)S(1)} %get-tuple-element.13.refs_1_.refs_3_, s32[96,128]{1,0:T(8,128)S(1)} %get-tuple-element.14.refs_2_.refs_4_, s32[8,1536]{1,0:T(8,128)S(1)} %get-tuple-element.15.refs_3_.refs_5_, ...), custom_call_target="tpu_custom_call" | custom-call | flops 75497472 | bytes 3145728 | tf_op jit(solution)/shard_map/prefix_keys/pallas_call | solution.py:375
  16.4 0.0 copy-start.8
  16.4 0.0 copy-start.5
  16.4 0.0 copy-start.6
  16.5 0.0 collective-permute-done.5.refs_2_
  16.5 0.0 collective-permute-done.6.refs_3_
  16.5 0.2 collective-permute-done.7.refs_4_
  16.6 0.5 %combine_project.1 = bf16[6,2,2048]{2,1,0:T(2,128)(2,1)S(1)} custom-call(f32[24,384]{1,0:T(8,128)S(1)} %own_keys.1.refs_0_, bf16[24,384]{1,0:T(8,128)(2,1)S(1)} %prefix_keys.2.refs_1_, bf16[24,384]{1,0:T(8,128)(2,1)S(1)} %collective-permute-done.5.refs_2_, bf16[24,384]{1,0:T(8,128)(2,1)S(1)} %collective-permute-done.6.refs_3_, ...), custom_call_target="tpu_custom_call" | custom-call | flops 25165824 | bytes 2097152 | tf_op jit(solution)/shard_map/combine_project/pallas_call | solution.py:415
  17.2 2.5 %collective-permute-start.10 = (bf16[6,2,2048]{2,1,0:T(2,128)(2,1)S(1)}, bf16[6,2,2048]{2,1,0:T(2,128)(2,1)S(1)}, u32[]{:S(2)}, u32[]{:S(2)}) collective-permute-start(bf16[6,2,2048]{2,1,0:T(2,128)(2,1)S(1)} %combine_project.1), channel_id=1, source_target_pairs={{0,24},{8,16},{16,8},{24,0},{1,25},{9,17},{17,9},{25,1},{2,26},{10... | collective-permute-start | bytes 147464 | tf_op jit(solution)/shard_map/ppermute | solution.py:310
  19.7 0.5 %collective-permute-start.9 = (bf16[6,2,2048]{2,1,0:T(2,128)(2,1)S(1)}, bf16[6,2,2048]{2,1,0:T(2,128)(2,1)S(1)}, u32[]{:S(2)}, u32[]{:S(2)}) collective-permute-start(bf16[6,2,2048]{2,1,0:T(2,128)(2,1)S(1)} %combine_project.1), channel_id=1, source_target_pairs={{0,8},{8,0},{16,24},{24,16},{1,9},{9,1},{17,25},{25,17},{2,10},{10... | collective-permute-start | bytes 147464 | tf_op jit(solution)/shard_map/ppermute | solution.py:310
  20.2 0.5 %collective-permute-start.8 = (bf16[6,2,2048]{2,1,0:T(2,128)(2,1)S(1)}, bf16[6,2,2048]{2,1,0:T(2,128)(2,1)S(1)}, u32[]{:S(2)}, u32[]{:S(2)}) collective-permute-start(bf16[6,2,2048]{2,1,0:T(2,128)(2,1)S(1)} %combine_project.1), channel_id=1, source_target_pairs={{0,16},{8,24},{16,0},{24,8},{1,17},{9,25},{17,1},{25,9},{2,18},{10... | collective-permute-start | bytes 147464 | tf_op jit(solution)/shard_map/ppermute | solution.py:310
  20.7 1.6 %collective-permute-done.10 = bf16[6,2,2048]{2,1,0:T(2,128)(2,1)S(1)} collective-permute-done((bf16[6,2,2048]{2,1,0:T(2,128)(2,1)S(1)}, bf16[6,2,2048]{2,1,0:T(2,128)(2,1)S(1)}, u32[]{:S(2)}, u32[]{:S(2)}) %collective-permute-start.10) | collective-permute-done | bytes 49184 | tf_op jit(solution)/shard_map/ppermute | solution.py:310
  22.3 1.5 %collective-permute-done.9 = bf16[6,2,2048]{2,1,0:T(2,128)(2,1)S(1)} collective-permute-done((bf16[6,2,2048]{2,1,0:T(2,128)(2,1)S(1)}, bf16[6,2,2048]{2,1,0:T(2,128)(2,1)S(1)}, u32[]{:S(2)}, u32[]{:S(2)}) %collective-permute-start.9) | collective-permute-done | bytes 49184 | tf_op jit(solution)/shard_map/ppermute | solution.py:310
  23.8 0.0 copy-done.8
  23.8 0.1 convert_add_fusion.refs_1_
  23.9 0.4 %collective-permute-done.8.refs_0_ = bf16[6,2,2048]{2,1,0:T(2,128)(2,1)S(1)} collective-permute-done((bf16[6,2,2048]{2,1,0:T(2,128)(2,1)S(1)}, bf16[6,2,2048]{2,1,0:T(2,128)(2,1)S(1)}, u32[]{:S(2)}, u32[]{:S(2)}) %collective-permute-start.8) | collective-permute-done | bytes 49184 | tf_op jit(solution)/shard_map/ppermute | solution.py:310
  24.3 0.0 copy-done.5
  24.3 0.0 copy-done.6
  24.3 0.7 %residual_scores.1 = (bf16[6,2,2048]{2,1,0:T(2,128)(2,1)}, f32[6]{0:T(128)}) custom-call(bf16[6,2,2048]{2,1,0:T(2,128)(2,1)S(1)} %collective-permute-done.8.refs_0_, f32[6,2,2048]{2,1,0:T(2,128)S(1)} %convert_add_fusion.refs_1_, f32[1,2048]{1,0:T(1,128)S(1)} %bitcast.11, f32[1,2048]{1,0:T(1,128)S(1)} %bitcast.12), custom_call_target="tpu_custom_call" | custom-call | flops 1 | bytes 294912 | tf_op jit(solution)/shard_map/residual_scores/pallas_call | solution.py:446
Async XLA Ops:
  0.6 6.9 %copy-start.1 = (bf16[1,24,64,512]{3,2,1,0:T(8,128)(2,1)S(1)}, bf16[1,24,64,512]{3,2,1,0:T(8,128)(2,1)}, u32[]{:S(2)}) copy-start(bf16[1,24,64,512]{3,2,1,0:T(8,128)(2,1)} %param.12) | copy-start | bytes 4718596
  0.6 6.9 %collective-permute-start.1 = (bf16[24,64,512]{2,1,0:T(8,128)(2,1)}, bf16[24,64,512]{2,1,0:T(8,128)(2,1)S(1)}, u32[]{:S(2)}, u32[]{:S(2)}) collective-permute-start(bf16[24,64,512]{2,1,0:T(8,128)(2,1)} %bitcast.5), channel_id=1, source_target_pairs={{0,1},{1,0},{2,3},{3,2},{4,5},{5,4},{6,7},{7,6},{8,9},{9,8},{10,11... | collective-permute-start | bytes 4718600 | tf_op jit(solution)/shard_map/ppermute | solution.py:310
  1.2 7.4 %collective-permute-start.2 = (bf16[6,2,512]{2,1,0:T(2,128)(2,1)}, bf16[6,2,512]{2,1,0:T(2,128)(2,1)S(1)}, u32[]{:S(2)}, u32[]{:S(2)}) collective-permute-start(bf16[6,2,512]{2,1,0:T(2,128)(2,1)} %q_ref.3), channel_id=1, source_target_pairs={{0,5},{1,4},{2,7},{3,6},{4,1},{5,0},{6,3},{7,2},{8,13},{9,12},{10,... | collective-permute-start | bytes 36872 | tf_op jit(solution)/shard_map/ppermute | solution.py:310
  4.9 5.1 %collective-permute-start.3 = (bf16[6,2,512]{2,1,0:T(2,128)(2,1)}, bf16[6,2,512]{2,1,0:T(2,128)(2,1)S(1)}, u32[]{:S(2)}, u32[]{:S(2)}) collective-permute-start(bf16[6,2,512]{2,1,0:T(2,128)(2,1)} %q_ref.3), channel_id=1, source_target_pairs={{0,7},{1,6},{2,5},{3,4},{4,3},{5,2},{6,1},{7,0},{8,15},{9,14},{10,... | collective-permute-start | bytes 36872 | tf_op jit(solution)/shard_map/ppermute | solution.py:310
  5.9 4.1 %collective-permute-start.4 = (bf16[6,2,512]{2,1,0:T(2,128)(2,1)}, bf16[6,2,512]{2,1,0:T(2,128)(2,1)S(1)}, u32[]{:S(2)}, u32[]{:S(2)}) collective-permute-start(bf16[6,2,512]{2,1,0:T(2,128)(2,1)} %q_ref.3), channel_id=1, source_target_pairs={{0,3},{1,2},{2,1},{3,0},{4,7},{5,6},{6,5},{7,4},{8,11},{9,10},{10,... | collective-permute-start | bytes 36872 | tf_op jit(solution)/shard_map/ppermute | solution.py:310
  6.1 1.4 %collective-permute-start = (s32[24]{0:T(128)}, s32[24]{0:T(128)S(1)}, u32[]{:S(2)}, u32[]{:S(2)}) collective-permute-start(s32[24]{0:T(128)} %page_hbm.1), channel_id=1, source_target_pairs={{0,1},{1,0},{2,3},{3,2},{4,5},{5,4},{6,7},{7,6},{8,9},{9,8},{10,11... | collective-permute-start | bytes 296 | tf_op jit(solution)/shard_map/ppermute | solution.py:310
  10.0 4.7 %copy-start = (bf16[512,2048]{1,0:T(8,128)(2,1)S(1)}, bf16[512,2048]{1,0:T(8,128)(2,1)}, u32[]{:S(2)}) copy-start(bf16[512,2048]{1,0:T(8,128)(2,1)} %refs_5_.1) | copy-start | bytes 6291460
  10.0 4.7 %copy-start.2 = (bf16[1,6,128,512]{3,2,1,0:T(8,128)(2,1)S(1)}, bf16[1,6,128,512]{3,2,1,0:T(8,128)(2,1)}, u32[]{:S(2)}) copy-start(bf16[1,6,128,512]{3,2,1,0:T(8,128)(2,1)} %param.17) | copy-start | bytes 2359300
  10.0 4.7 %copy-start.3 = (bf16[6,2,512]{2,1,0:T(2,128)(2,1)S(1)}, bf16[6,2,512]{2,1,0:T(2,128)(2,1)}, u32[]{:S(2)}) copy-start(bf16[6,2,512]{2,1,0:T(2,128)(2,1)} %q_ref.3) | copy-start | bytes 36868
  10.0 4.6 %copy-start.4 = (bf16[1,6,2,512]{3,2,1,0:T(2,128)(2,1)S(1)}, bf16[1,6,2,512]{3,2,1,0:T(2,128)(2,1)}, u32[]{:S(2)}) copy-start(bf16[1,6,2,512]{3,2,1,0:T(2,128)(2,1)} %param.19) | copy-start | bytes 36868
  10.0 4.6 %copy-start.7 = (s32[6]{0:T(128)S(1)}, s32[6]{0:T(128)}, u32[]{:S(2)}) copy-start(s32[6]{0:T(128)} %len_ref.1) | copy-start | bytes 76
  10.8 5.7 %collective-permute-start.5 = (bf16[24,384]{1,0:T(8,128)(2,1)S(1)}, bf16[24,384]{1,0:T(8,128)(2,1)S(1)}, u32[]{:S(2)}, u32[]{:S(2)}) collective-permute-start(bf16[24,384]{1,0:T(8,128)(2,1)S(1)} %get-tuple-element.19), channel_id=1, source_target_pairs={{0,7},{1,6},{2,5},{3,4},{4,3},{5,2},{6,1},{7,0},{8,15},{9,14},{10,... | collective-permute-start | bytes 55304 | tf_op jit(solution)/shard_map/ppermute | solution.py:310
  12.6 3.9 %collective-permute-start.6 = (bf16[24,384]{1,0:T(8,128)(2,1)S(1)}, bf16[24,384]{1,0:T(8,128)(2,1)S(1)}, u32[]{:S(2)}, u32[]{:S(2)}) collective-permute-start(bf16[24,384]{1,0:T(8,128)(2,1)S(1)} %get-tuple-element.20), channel_id=1, source_target_pairs={{0,3},{1,2},{2,1},{3,0},{4,7},{5,6},{6,5},{7,4},{8,11},{9,10},{10,... | collective-permute-start | bytes 55304 | tf_op jit(solution)/shard_map/ppermute | solution.py:310
  12.6 4.1 %collective-permute-start.7 = (bf16[24,384]{1,0:T(8,128)(2,1)S(1)}, bf16[24,384]{1,0:T(8,128)(2,1)S(1)}, u32[]{:S(2)}, u32[]{:S(2)}) collective-permute-start(bf16[24,384]{1,0:T(8,128)(2,1)S(1)} %get-tuple-element.21), channel_id=1, source_target_pairs={{0,5},{1,4},{2,7},{3,6},{4,1},{5,0},{6,3},{7,2},{8,13},{9,12},{10,... | collective-permute-start | bytes 55304 | tf_op jit(solution)/shard_map/ppermute | solution.py:310
  16.4 7.3 %copy-start.8 = (bf16[6,2,2048]{2,1,0:T(2,128)(2,1)S(1)}, bf16[6,2,2048]{2,1,0:T(2,128)(2,1)}, u32[]{:S(2)}) copy-start(bf16[6,2,2048]{2,1,0:T(2,128)(2,1)} %param.20) | copy-start | bytes 147460
  16.4 7.9 %copy-start.5 = (f32[2048]{0:T(1024)S(1)}, f32[2048]{0:T(1024)}, u32[]{:S(2)}) copy-start(f32[2048]{0:T(1024)} %param.22) | copy-start | bytes 24580
  16.4 7.8 %copy-start.6 = (f32[2048]{0:T(1024)S(1)}, f32[2048]{0:T(1024)}, u32[]{:S(2)}) copy-start(f32[2048]{0:T(1024)} %param.23) | copy-start | bytes 24580
  17.2 5.1 %collective-permute-start.10 = (bf16[6,2,2048]{2,1,0:T(2,128)(2,1)S(1)}, bf16[6,2,2048]{2,1,0:T(2,128)(2,1)S(1)}, u32[]{:S(2)}, u32[]{:S(2)}) collective-permute-start(bf16[6,2,2048]{2,1,0:T(2,128)(2,1)S(1)} %combine_project.1), channel_id=1, source_target_pairs={{0,24},{8,16},{16,8},{24,0},{1,25},{9,17},{17,9},{25,1},{2,26},{10... | collective-permute-start | bytes 147464 | tf_op jit(solution)/shard_map/ppermute | solution.py:310
  19.7 4.1 %collective-permute-start.9 = (bf16[6,2,2048]{2,1,0:T(2,128)(2,1)S(1)}, bf16[6,2,2048]{2,1,0:T(2,128)(2,1)S(1)}, u32[]{:S(2)}, u32[]{:S(2)}) collective-permute-start(bf16[6,2,2048]{2,1,0:T(2,128)(2,1)S(1)} %combine_project.1), channel_id=1, source_target_pairs={{0,8},{8,0},{16,24},{24,16},{1,9},{9,1},{17,25},{25,17},{2,10},{10... | collective-permute-start | bytes 147464 | tf_op jit(solution)/shard_map/ppermute | solution.py:310
  20.2 4.1 %collective-permute-start.8 = (bf16[6,2,2048]{2,1,0:T(2,128)(2,1)S(1)}, bf16[6,2,2048]{2,1,0:T(2,128)(2,1)S(1)}, u32[]{:S(2)}, u32[]{:S(2)}) collective-permute-start(bf16[6,2,2048]{2,1,0:T(2,128)(2,1)S(1)} %combine_project.1), channel_id=1, source_target_pairs={{0,16},{8,24},{16,0},{24,8},{1,17},{9,25},{17,1},{25,9},{2,18},{10... | collective-permute-start | bytes 147464 | tf_op jit(solution)/shard_map/ppermute | solution.py:310
